TPU v7x, 32 devices: a whole 2x2x4 slice. The times are simulated.
32 devices in a mesh: groups: 2 (over y), rows: 16 (over z, x, core).
Axes of the slice: x: 2, y: 2, z: 4, core: 2. Of those that a mesh axis runs over, the one named last changes fastest.
Arguments:
- tile_values: bfloat16 [3072, 256, 256], P(('groups', 'rows')), parts along dimension 0, may hold values from -0.078125 to 0.078125
- tile_rows: int32 [3072], P(('groups', 'rows')), parts along dimension 0, may hold values from 0 to 7
- tile_slots: int32 [3072], P(('groups', 'rows')), parts along dimension 0, may hold values from 0 to 255, as said below
- send_list: int32 [32, 16, 16], P(('groups', 'rows')), parts along dimension 0, may hold values from 0 to 7, as said below
- self_links: float32 [65536], P(('groups', 'rows')), parts along dimension 0, may hold values from 0.25 to 2
- start_panel: float32 [32, 65536], P(None, ('groups', 'rows')), parts along dimension 1, may hold values from -25 to 25
Outputs:
- next_basis: float32 [32, 65536], P(None, ('groups', 'rows')), parts along dimension 1
- couplings: float32 [4, 32, 32], P('groups'), parts along dimension 0
- factors: float32 [4, 32, 32], P('groups'), parts along dimension 0
There are 2 independent parts, one for each index of `groups`. A program takes and returns all parts, laid end to end along the dimension named above; each array names one. Nothing has to cross between parts.
Inputs may be any that keep to these rules, and one draw needn't show every extreme that they name: send_list[p, q, s] is the local block of sender p that goes to receiver q in slot s. Each receiver gets 16 blocks from 4 senders, 8 blocks (slots below 8) from another 16/4, and none from the rest; slots at or past that number hold 0. tile_slots[t] = p * 16 + s names a live slot (p, s) of the tile's device; every live slot of a device is named by exactly one of its 96 tiles.
All inputs are finite; a program needn't handle non-finite values.
Results may differ from a plain program's by a relative error of at most 0.0042.
Values may be sent and summed in bfloat16 or wider, within the bound.
No kernel may reach another device: no remote copies, remote signals or barrier semaphores. Data moves between devices by JAX's collectives and lax.ppermute only.
A program may use at most 128 MiB of HBM per device.

v0:
```python
import math

import jax
import jax.numpy as jnp
from jax import lax
from jax.sharding import PartitionSpec as P

ITERS = 2


precise = lax.Precision.HIGHEST


def product(left, right):
    return jnp.dot(left, right, precision=precise, preferred_element_type=jnp.float32)


def on_device(tile_values, tile_rows, tile_slots, send_list, self_links, start_panel):
    peer_count = lax.axis_size("rows")
    panel_width = start_panel.shape[0]
    tile_size = tile_values.shape[1]
    own_rows = start_panel.shape[1]
    blocks_here = own_rows // tile_size
    capacity = send_list.shape[2]
    flat_send = send_list.reshape(-1)
    block_ids = jnp.arange(blocks_here, dtype=jnp.int32)
    row_onehot = (tile_rows[None, :] == block_ids[:, None]).astype(jnp.float32)
    send_onehot = (flat_send[None, :] == block_ids[:, None]).astype(jnp.float32)
    gram_now = lax.psum(product(start_panel, start_panel.T), "rows")
    factor = jnp.linalg.cholesky(gram_now)
    basis_now = jax.scipy.linalg.solve_triangular(factor, start_panel, lower=True)
    basis_prev = None
    factor_prev = None
    couplings = []
    factors = []
    for iteration in range(ITERS):
        rounded = basis_now.astype(jnp.bfloat16)
        panel_blocks = rounded.reshape(panel_width, blocks_here, tile_size).transpose(1, 0, 2)
        outgoing = panel_blocks[flat_send].reshape(peer_count, capacity, panel_width, tile_size)
        arrived = lax.all_to_all(outgoing, "rows", split_axis=0, concat_axis=0, tiled=True)
        arrived = arrived.reshape(peer_count * capacity, panel_width, tile_size)
        forward = lax.dot_general(
            arrived[tile_slots],
            tile_values,
            (((2,), (2,)), ((0,), (0,))),
            preferred_element_type=jnp.float32,
        )
        own_blocks = panel_blocks[tile_rows]
        backward = lax.dot_general(
            own_blocks,
            tile_values,
            (((2,), (1,)), ((0,), (0,))),
            preferred_element_type=jnp.float32,
        )
        coupled = jnp.einsum("rt,tkj->rkj", row_onehot, forward, precision=precise)
        slot_terms = (
            jnp.zeros((peer_count * capacity, panel_width, tile_size), jnp.float32)
            .at[tile_slots]
            .add(backward)
        )
        returned = lax.all_to_all(
            slot_terms.reshape(peer_count, capacity, panel_width, tile_size),
            "rows",
            split_axis=0,
            concat_axis=0,
            tiled=True,
        )
        returned = returned.reshape(peer_count * capacity, panel_width, tile_size)
        coupled = coupled + jnp.einsum("rs,skj->rkj", send_onehot, returned, precision=precise)
        applied = self_links[None, :] * basis_now + coupled.transpose(1, 0, 2).reshape(
            panel_width, own_rows
        )
        coupling = lax.psum(product(basis_now, applied.T), "rows")
        residual = applied - product(coupling.T, basis_now)
        if basis_prev is not None:
            residual = residual - product(factor_prev.T, basis_prev)
        gram_now = lax.psum(product(residual, residual.T), "rows")
        factor = jnp.linalg.cholesky(gram_now)
        following = jax.scipy.linalg.solve_triangular(factor, residual, lower=True)
        couplings.append(coupling)
        factors.append(factor)
        basis_prev, basis_now, factor_prev = (basis_now, following, factor)
    scale_all = math.sqrt(own_rows * peer_count)
    return (basis_now * scale_all, jnp.stack(couplings), jnp.stack(factors))


def solution(mesh):
    placed = (
        P(("groups", "rows"), None, None),
        P(("groups", "rows")),
        P(("groups", "rows")),
        P(("groups", "rows"), None, None),
        P(("groups", "rows")),
        P(None, ("groups", "rows")),
    )
    return jax.shard_map(
        on_device,
        mesh=mesh,
        in_specs=placed,
        out_specs=(P(None, ("groups", "rows")), P("groups", None, None), P("groups", None, None)),
        check_vma=False,
    )
```

profile of v0, /device:TPU:0, one launch (start us, length us, event | category | flops | bytes accessed | tf_op | source)
XLA Modules:
  0.0 928.4 jit_solution(6561124471687218664)
XLA Ops:
  1.9 62.9 %psum.35 = f32[32,32]{0,1:T(8,128)S(1)} all-reduce(f32[32,32]{0,1:T(8,128)S(1)} %fusion.53), channel_id=1, replica_groups=mesh['groups'=2,'rows'=16] {'rows'}, use_global_device_ids=true, to_apply=%region_0.0 | all-reduce | flops 1024 | bytes 8192 | tf_op jit(solution)/shard_map/psum | solution.py:29
  65.0 2.9 cholesky.59
  76.4 4.7 all-to-all-start
  83.0 7.3 fusion.55
  90.4 4.3 broadcast.74.clone
  94.6 13.3 %scatter_fusion = f32[256,32,256]{2,1,0:T(8,128)} fusion(f32[256,32,256]{2,1,0:T(8,128)} %broadcast.74.clone, s32[96]{0:T(128)S(1)} %compare_select_fusion.2, f32[96,32,256]{2,1,0:T(8,128)S(1)} %fusion.55), kind=kCustom, calls=%fused_computation.6 | custom fusion | flops 786432 | bytes 9437568 | tf_op jit(solution)/shard_map/scatter-add | solution.py:59
  108.0 13.3 %copy.29 = f32[16,16,32,256]{3,1,2,0:T(8,128)} copy(f32[16,16,32,256]{3,2,1,0:T(8,128)} %bitcast.105) | data formatting | bytes 16777216 | tf_op jit(solution)/shard_map/reshape | solution.py:62
  121.2 37.4 %all-to-all-done = bf16[16,16,32,256]{3,2,1,0:T(8,128)(2,1)} async-done(((bf16[16,16,32,256]{3,2,1,0:T(8,128)(2,1)}), bf16[16,16,32,256]{3,2,1,0:T(8,128)(2,1)}, u32[]{:S(2)}, u32[]{:S(2)}) %all-to-all-start) | async-done | bytes 4194336 | tf_op jit(solution)/shard_map/all_to_all | solution.py:40
  158.7 19.9 %all-to-all-start.1 = ((f32[16,16,32,256]{3,1,2,0:T(8,128)}), f32[16,16,32,256]{3,1,2,0:T(8,128)}, u32[]{:S(2)}, u32[]{:S(2)}) async-start(f32[16,16,32,256]{3,1,2,0:T(8,128)} %copy.29), calls=%async_computation.1 | async-start | bytes 16777216 | tf_op jit(solution)/shard_map/all_to_all | solution.py:61
  178.7 4.1 gather_fusion.1
  182.8 8.8 fusion.54
  191.6 137.7 %all-to-all-done.1 = f32[16,16,32,256]{3,1,2,0:T(8,128)} async-done(((f32[16,16,32,256]{3,1,2,0:T(8,128)}), f32[16,16,32,256]{3,1,2,0:T(8,128)}, u32[]{:S(2)}, u32[]{:S(2)}) %all-to-all-start.1) | async-done | bytes 8388640 | tf_op jit(solution)/shard_map/all_to_all | solution.py:61
  329.2 4.4 copy.30
  336.4 2.9 fusion.4
  339.7 92.6 %psum.36 = f32[32,32]{1,0:T(8,128)S(1)} all-reduce(f32[32,32]{1,0:T(8,128)S(1)} %fusion.11), channel_id=1, replica_groups=mesh['groups'=2,'rows'=16] {'rows'}, use_global_device_ids=true, to_apply=%region_4.0 | all-reduce | flops 1024 | bytes 8192 | tf_op jit(solution)/shard_map/psum | solution.py:73
  433.1 57.6 %psum.37 = f32[32,32]{0,1:T(8,128)S(1)} all-reduce(f32[32,32]{0,1:T(8,128)S(1)} %fusion.56), channel_id=1, replica_groups=mesh['groups'=2,'rows'=16] {'rows'}, use_global_device_ids=true, to_apply=%region_5.0 | all-reduce | flops 1024 | bytes 8192 | tf_op jit(solution)/shard_map/psum | solution.py:77
  490.8 2.9 cholesky.70
  501.4 4.9 all-to-all-start.2
  508.3 7.3 fusion.58
  515.6 4.3 broadcast.74
  519.9 13.3 %scatter_fusion.1 = f32[256,32,256]{2,1,0:T(8,128)} fusion(f32[256,32,256]{2,1,0:T(8,128)} %broadcast.74, s32[96]{0:T(128)S(1)} %compare_select_fusion.2, f32[96,32,256]{2,1,0:T(8,128)S(1)} %fusion.58), kind=kCustom, calls=%fused_computation.7 | custom fusion | flops 786432 | bytes 9437568 | tf_op jit(solution)/shard_map/scatter-add | solution.py:59
  533.2 13.3 %copy.35 = f32[16,16,32,256]{3,1,2,0:T(8,128)} copy(f32[16,16,32,256]{3,2,1,0:T(8,128)} %bitcast.104) | data formatting | bytes 16777216 | tf_op jit(solution)/shard_map/reshape | solution.py:62
  546.5 37.5 %all-to-all-done.2 = bf16[16,16,32,256]{3,2,1,0:T(8,128)(2,1)} async-done(((bf16[16,16,32,256]{3,2,1,0:T(8,128)(2,1)}), bf16[16,16,32,256]{3,2,1,0:T(8,128)(2,1)}, u32[]{:S(2)}, u32[]{:S(2)}) %all-to-all-start.2) | async-done | bytes 4194336 | tf_op jit(solution)/shard_map/all_to_all | solution.py:40
  584.0 19.8 %all-to-all-start.3 = ((f32[16,16,32,256]{3,1,2,0:T(8,128)}), f32[16,16,32,256]{3,1,2,0:T(8,128)}, u32[]{:S(2)}, u32[]{:S(2)}) async-start(f32[16,16,32,256]{3,1,2,0:T(8,128)} %copy.35), calls=%async_computation.3 | async-start | bytes 16777216 | tf_op jit(solution)/shard_map/all_to_all | solution.py:61
  603.8 4.1 gather_fusion.4
  607.9 8.8 fusion.57
  616.7 137.8 %all-to-all-done.3 = f32[16,16,32,256]{3,1,2,0:T(8,128)} async-done(((f32[16,16,32,256]{3,1,2,0:T(8,128)}), f32[16,16,32,256]{3,1,2,0:T(8,128)}, u32[]{:S(2)}, u32[]{:S(2)}) %all-to-all-start.3) | async-done | bytes 8388640 | tf_op jit(solution)/shard_map/all_to_all | solution.py:61
  754.5 4.4 copy.36
  761.7 2.9 fusion.7
  765.0 92.6 %psum.38 = f32[32,32]{1,0:T(8,128)S(1)} all-reduce(f32[32,32]{1,0:T(8,128)S(1)} %fusion.10), channel_id=1, replica_groups=mesh['groups'=2,'rows'=16] {'rows'}, use_global_device_ids=true, to_apply=%region_7.10 | all-reduce | flops 1024 | bytes 8192 | tf_op jit(solution)/shard_map/psum | solution.py:73
  861.4 57.6 %psum.39 = f32[32,32]{0,1:T(8,128)S(1)} all-reduce(f32[32,32]{0,1:T(8,128)S(1)} %fusion.59), channel_id=1, replica_groups=mesh['groups'=2,'rows'=16] {'rows'}, use_global_device_ids=true, to_apply=%region_8.11 | all-reduce | flops 1024 | bytes 8192 | tf_op jit(solution)/shard_map/psum | solution.py:77
  919.1 2.9 cholesky.81
  (65 shorter events, 38.8 us)
Async XLA Ops:
  0.6 1.0 copy-start
  76.4 4.7 copy-start.6
  76.4 82.3 %all-to-all-start = ((bf16[16,16,32,256]{3,2,1,0:T(8,128)(2,1)}), bf16[16,16,32,256]{3,2,1,0:T(8,128)(2,1)}, u32[]{:S(2)}, u32[]{:S(2)}) async-start(bf16[16,16,32,256]{3,2,1,0:T(8,128)(2,1)} %bitcast.108), calls=%async_computation | async-start | bytes 8388608 | tf_op jit(solution)/shard_map/all_to_all | solution.py:40
  81.1 2.0 copy-start.7
  121.2 57.4 %copy-start.5 = (s32[1,16,16]{2,1,0:T(8,128)S(1)}, s32[1,16,16]{2,1,0:T(8,128)}, u32[]{:S(2)}) copy-start(s32[1,16,16]{2,1,0:T(8,128)} %param.12) | copy-start | bytes 3076
  158.7 170.6 %all-to-all-start.1 = ((f32[16,16,32,256]{3,1,2,0:T(8,128)}), f32[16,16,32,256]{3,1,2,0:T(8,128)}, u32[]{:S(2)}, u32[]{:S(2)}) async-start(f32[16,16,32,256]{3,1,2,0:T(8,128)} %copy.29), calls=%async_computation.1 | async-start | bytes 16777216 | tf_op jit(solution)/shard_map/all_to_all | solution.py:61
  336.4 3.0 copy-start.2
  336.4 3.0 copy-start.4
  501.4 82.5 %all-to-all-start.2 = ((bf16[16,16,32,256]{3,2,1,0:T(8,128)(2,1)}), bf16[16,16,32,256]{3,2,1,0:T(8,128)(2,1)}, u32[]{:S(2)}, u32[]{:S(2)}) async-start(bf16[16,16,32,256]{3,2,1,0:T(8,128)(2,1)} %bitcast.109), calls=%async_computation.2 | async-start | bytes 8388608 | tf_op jit(solution)/shard_map/all_to_all | solution.py:40
  584.0 170.5 %all-to-all-start.3 = ((f32[16,16,32,256]{3,1,2,0:T(8,128)}), f32[16,16,32,256]{3,1,2,0:T(8,128)}, u32[]{:S(2)}, u32[]{:S(2)}) async-start(f32[16,16,32,256]{3,1,2,0:T(8,128)} %copy.35), calls=%async_computation.3 | async-start | bytes 16777216 | tf_op jit(solution)/shard_map/all_to_all | solution.py:61
  758.9 169.3 %copy-start.1 = (f32[32,2048]{1,0:T(8,128)S(1)}, f32[32,2048]{1,0:T(8,128)}, u32[]{:S(2)}) copy-start(f32[32,2048]{1,0:T(8,128)} %param.14) | copy-start | bytes 786436
  761.7 3.0 copy-start.3
where the time goes:
time: 943 us; the launch traced here: 928 us
  blocking collectives  363 us (38%)
  waiting for transfers between devices  350 us (37%)
  local copies, waits for them, and re-layouts  63.7 us (7%)
  matrix products  52.6 us (6%)
  starting transfers between devices  49.3 us (5%)
  other arithmetic  48 us (5%)
    all_to_all x2, waiting for transfers between devices, on_device(): lax.all_to_all(slot_terms.reshape(peer_count, capacity, panel_width, tile...  275 us
    psum x2, blocking collectives, on_device(): coupling = lax.psum(product(basis_now, applied.T), 'rows')  185 us
    psum x2, blocking collectives, on_device(): gram_now = lax.psum(product(residual, residual.T), 'rows')  115 us
    all_to_all x2, waiting for transfers between devices, on_device(): lax.all_to_all(outgoing, 'rows', split_axis=0, concat_axis=0, tiled=True)  75 us
    psum x1, blocking collectives, on_device(): gram_now = lax.psum(product(start_panel, start_panel.T), 'rows')  62.9 us
    all_to_all x2, starting transfers between devices, on_device(): lax.all_to_all(slot_terms.reshape(peer_count, capacity, panel_width, tile...  39.7 us
    scatter-add x2, other arithmetic, on_device(): slot_terms = jnp.zeros((peer_count * capacity, panel_width, tile_size), j...  26.6 us
    reshape x2, local copies, waits for them, and re-layouts, on_device(): slot_terms.reshape(peer_count, capacity, panel_width, tile_size)  26.5 us
  transfers between devices with their start and end apart: 4, of which 4 were waited for; matrix products, arithmetic and copies ran while one was open for 11% of the time, Pallas kernels for 0%

commit v1 on v0

v1 whole, which is shorter than its diff:
```python
import functools
import math

import jax
import jax.numpy as jnp
import numpy as np
from jax import lax
from jax.experimental import pallas as pl
from jax.experimental.pallas import tpu as pltpu
from jax.sharding import PartitionSpec as P

precise = lax.Precision.HIGHEST
SMEM = pl.BlockSpec(memory_space=pltpu.SMEM)
VMEM = pl.BlockSpec(memory_space=pltpu.VMEM)
UNROLL = 16


def product(left, right):
    return lax.dot_general(left, right, (((1,), (0,)), ((), ())), precision=precise, preferred_element_type=jnp.float32)


def product_t(left, right):
    return lax.dot_general(left, right, (((1,), (1,)), ((), ())), precision=precise, preferred_element_type=jnp.float32)


def t_product(left, right):
    return lax.dot_general(left, right, (((0,), (0,)), ((), ())), precision=precise, preferred_element_type=jnp.float32)


def swap(array, offset):
    count = lax.axis_size("rows")
    return lax.ppermute(array, "rows", [(place, place ^ offset) for place in range(count)])


def stages(count):
    bits = count.bit_length() - 1
    top = min(2, bits)
    return list(range(bits - top)), bits - top, 1 << top


def positions(count):
    low, shift, wide = stages(count)
    bits = count.bit_length() - 1
    place = []
    for offset in range(count):
        spot = offset >> shift
        for bit in low:
            spot += ((offset >> bit) & 1) << (bits - 1 - bit)
        place.append(spot)
    return np.array(place, np.int32)


def gather_panel(panel):
    low, shift, wide = stages(lax.axis_size("rows"))
    arrays = [jnp.stack([panel] + [swap(panel, far << shift) for far in range(1, wide)])]
    for bit in reversed(low):
        arrays = arrays + [swap(array, 1 << bit) for array in arrays]
    return arrays


def reduce_panels(kept, sent):
    low, shift, wide = stages(lax.axis_size("rows"))
    for bit in low:
        arrived = swap(sent, 1 << bit)
        half = kept.shape[0] // 2
        if bit != low[-1]:
            sent = (kept[half:] + arrived[half:]).astype(jnp.bfloat16)
            kept = kept[:half] + arrived[:half]
    terms = []
    for far in range(wide - 1, 0, -1):
        terms.append(swap((kept[far] + arrived[far]).astype(jnp.bfloat16), far << shift))
    return [kept[0], arrived[0]] + terms


def reduce_small(array):
    low, shift, wide = stages(lax.axis_size("rows"))
    for bit in low:
        array = array + swap(array, 1 << bit)
    others = [swap(array, far << shift) for far in range(1, wide)]
    total = array + others[0]
    if wide == 4:
        total = total + (others[1] + others[2])
    return total


def tile_place(tile, me_ref, rows_ref, slots_ref, list_ref, place_ref, capacity, tile_size):
    slot = slots_ref[tile]
    block = list_ref[slot]
    piece = place_ref[(slot // capacity) ^ me_ref[0]]
    own = pl.ds(pl.multiple_of(rows_ref[tile] * tile_size, tile_size), tile_size)
    other = pl.ds(pl.multiple_of(block * tile_size, tile_size), tile_size)
    return own, piece, other


def backward_kernel(me_ref, rows_ref, slots_ref, list_ref, place_ref, high_ref, low_ref, tiles_ref, kept_ref, sent_ref, total, *, capacity):
    tiles, tile_size, _ = tiles_ref.shape
    width = high_ref.shape[0]
    half = kept_ref.shape[0]
    total[...] = jnp.zeros_like(total)

    def some(step, carry):
        for u in range(UNROLL):
            tile = step * UNROLL + u
            own, piece, other = tile_place(tile, me_ref, rows_ref, slots_ref, list_ref, place_ref, capacity, tile_size)
            left = jnp.concatenate([high_ref[:, own], low_ref[:, own]], axis=0)
            both = jnp.dot(left, tiles_ref[tile], preferred_element_type=jnp.float32)
            total[piece, :, other] += (both[:width] + both[width:]).astype(total.dtype)
        return carry

    lax.fori_loop(0, tiles // UNROLL, some, 0)
    kept_ref[...] = total[:half].astype(kept_ref.dtype)
    sent_ref[...] = total[half:].astype(sent_ref.dtype)


def forward_kernel(me_ref, rows_ref, slots_ref, list_ref, place_ref, tiles_ref, *refs, capacity, groups):
    group_refs, (out_ref, pieces) = refs[:groups], refs[groups:]
    tiles, tile_size, _ = tiles_ref.shape
    wide = group_refs[0].shape[0]
    for group, ref in enumerate(group_refs):
        pieces[group * wide : (group + 1) * wide] = ref[...]
    out_ref[...] = jnp.zeros_like(out_ref)

    def some(step, carry):
        for u in range(UNROLL):
            tile = step * UNROLL + u
            own, piece, other = tile_place(tile, me_ref, rows_ref, slots_ref, list_ref, place_ref, capacity, tile_size)
            out_ref[:, own] += lax.dot_general(
                pieces[piece, :, other], tiles_ref[tile], (((1,), (1,)), ((), ())), preferred_element_type=jnp.float32
            )
        return carry

    lax.fori_loop(0, tiles // UNROLL, some, 0)


def split_kernel(whole_ref, high_ref, low_ref):
    high = whole_ref[...].astype(jnp.bfloat16)
    high_ref[...] = high
    low_ref[...] = (whole_ref[...] - high.astype(jnp.float32)).astype(jnp.bfloat16)


def combine_kernel(links_ref, panel_ref, forward_ref, *refs):
    term_refs, (out_ref, high_ref, low_ref) = refs[:-3], refs[-3:]
    out = links_ref[...] * panel_ref[...] + forward_ref[...]
    for ref in term_refs:
        out = out + ref[...].astype(jnp.float32)
    out_ref[...] = out
    high = out.astype(jnp.bfloat16)
    high_ref[...] = high
    low_ref[...] = (out - high.astype(jnp.float32)).astype(jnp.bfloat16)


def gram_kernel(left_ref, right_ref, out_ref):
    both = jnp.concatenate([left_ref[...], right_ref[...]], axis=0)
    out_ref[...] = product_t(both, both)


def factor_of(gram):
    width = gram.shape[0]
    rows = lax.broadcasted_iota(jnp.int32, (width, width), 0)
    columns = lax.broadcasted_iota(jnp.int32, (width, width), 1)
    unit = (rows == columns).astype(jnp.float32)
    work = jnp.concatenate([gram, unit], axis=1)
    found = []
    for j in range(width):
        scale = lax.rsqrt(work[j : j + 1, j : j + 1])
        row = work[j : j + 1, :] * scale
        found.append(row)
        work = work - (work[:, j : j + 1] * scale) * row
    found = jnp.concatenate(found, axis=0)
    factor = jnp.where(rows >= columns, found[:, :width].T, 0.0)
    return factor, found[:, width:]


def first_coefficients_kernel(gram_ref, coupling_ref, factor_ref, mix_ref):
    width = gram_ref.shape[0] // 2
    gram = gram_ref[...]
    _, inverse0 = factor_of(gram[:width, :width])
    coupling = product_t(product(inverse0, gram[:width, width:]), inverse0)
    image = product_t(product(inverse0, gram[width:, width:]), inverse0)
    factor, inverse1 = factor_of(image - t_product(coupling, coupling))
    coupling_ref[...] = coupling
    factor_ref[...] = factor
    after = product(inverse1, inverse0)
    before = -product(inverse1, t_product(coupling, inverse0))
    none = jnp.zeros_like(after)
    mix_ref[...] = jnp.concatenate(
        [
            jnp.concatenate([inverse0, none, none], axis=1),
            jnp.concatenate([before, after, none], axis=1),
            jnp.concatenate([none, before, after], axis=1),
        ],
        axis=0,
    )


def basis_kernel(mix_ref, start_ref, first_ref, links_ref, forward_ref, *refs):
    term_refs, (basis_ref, gram_ref) = refs[:-2], refs[-2:]
    width = start_ref.shape[0]
    second = links_ref[...] * first_ref[...] + forward_ref[...]
    for ref in term_refs:
        second = second + ref[...].astype(jnp.float32)
    basis = product(mix_ref[...], jnp.concatenate([start_ref[...], first_ref[...], second], axis=0))
    basis_ref[...] = basis
    gram_ref[...] = product_t(basis, basis[2 * width :])


def last_kernel(gram_ref, factor_ref, basis_ref, out_ref, coupling_ref, last_ref, *, scale):
    width = gram_ref.shape[1]
    before = factor_ref[...]
    crossed, coupling, image = gram_ref[:width], gram_ref[width : 2 * width], gram_ref[2 * width :]
    mixed = t_product(crossed, before)
    gram = image - t_product(coupling, coupling) - mixed - mixed.T + t_product(before, before)
    factor, inverse = factor_of(gram)
    coupling_ref[...] = coupling
    last_ref[...] = factor
    terms = jnp.concatenate([-product(inverse, before.T), -product(inverse, coupling.T), inverse], axis=1)
    out_ref[...] = product(terms, basis_ref[...]) * scale


def call(kernel, out, *args, name, scratch=(), specs=None, cost=None):
    return pl.pallas_call(
        kernel,
        out_shape=out,
        in_specs=specs or [VMEM] * len(args),
        out_specs=jax.tree.map(lambda _: VMEM, out),
        scratch_shapes=list(scratch),
        compiler_params=pltpu.CompilerParams(vmem_limit_bytes=40 << 20),
        cost_estimate=cost,
        name=name,
    )(*args)


def on_device(tile_values, tile_rows, tile_slots, send_list, self_links, start_panel):
    count = lax.axis_size("rows")
    width, here = start_panel.shape
    tiles, tile_size, _ = tile_values.shape
    capacity = send_list.shape[2]
    f32, bf16 = jnp.float32, jnp.bfloat16
    shape = jax.ShapeDtypeStruct
    links = self_links[None, :]
    place = jnp.asarray(positions(count))
    me = lax.axis_index("rows").astype(jnp.int32).reshape(1)
    listed = lax.all_to_all(send_list[0], "rows", split_axis=0, concat_axis=0, tiled=True).reshape(-1)
    indices = (me, tile_rows, tile_slots, listed, place)
    spec = [SMEM] * len(indices)
    work = 2 * tiles * width * tile_size * tile_size
    cost = pl.CostEstimate(flops=4 * work, bytes_accessed=2 * tile_values.size, transcendentals=0)
    total_type = f32 if count <= 16 else bf16

    def backward(high, low):
        return call(
            functools.partial(backward_kernel, capacity=capacity),
            (shape((count // 2, width, here), f32 if count <= 16 else bf16), shape((count // 2, width, here), bf16)),
            *indices, high, low, tile_values,
            name="backward", specs=spec + [VMEM] * 3, scratch=[pltpu.VMEM((count, width, here), total_type)], cost=cost,
        )

    def forward(groups):
        return call(
            functools.partial(forward_kernel, capacity=capacity, groups=len(groups)),
            shape((width, here), f32),
            *indices, tile_values, *groups,
            name="forward", specs=spec + [VMEM] * (1 + len(groups)),
            scratch=[pltpu.VMEM((count, width, here), bf16)], cost=cost,
        )

    def applied(high, low):
        groups = gather_panel(high)
        kept, sent = backward(high, low)
        terms = reduce_panels(kept, sent)
        return [forward(groups)] + terms

    panel = shape((width, here), f32)
    half = shape((width, here), bf16)
    small = shape((width, width), f32)
    high, low = call(split_kernel, (half, half), start_panel, name="split")
    terms = applied(high, low)
    first, high, low = call(combine_kernel, (panel, half, half), links, start_panel, *terms, name="combine")
    gram = call(gram_kernel, shape((2 * width, 2 * width), f32), start_panel, first, name="gram")
    gram = reduce_small(gram)
    coupling1, factor1, mix = call(
        first_coefficients_kernel, (small, small, shape((3 * width, 3 * width), f32)), gram, name="coefficients"
    )
    terms = applied(high, low)
    basis, gram = call(
        basis_kernel, (shape((3 * width, here), f32), shape((3 * width, width), f32)), mix, start_panel, first, links, *terms, name="basis"
    )
    gram = reduce_small(gram)
    out, coupling2, factor2 = call(
        functools.partial(last_kernel, scale=math.sqrt(here * count)), (panel, small, small), gram, factor1, basis, name="last"
    )
    return out, jnp.stack([coupling1, coupling2]), jnp.stack([factor1, factor2])


def solution(mesh):
    placed = (
        P(("groups", "rows"), None, None),
        P(("groups", "rows")),
        P(("groups", "rows")),
        P(("groups", "rows"), None, None),
        P(("groups", "rows")),
        P(None, ("groups", "rows")),
    )
    return jax.shard_map(
        on_device,
        mesh=mesh,
        in_specs=placed,
        out_specs=(P(None, ("groups", "rows")), P("groups", None, None), P("groups", None, None)),
        check_vma=False,
    )
```

time: 943 us -> 192 us (0.20); the launches traced: 928 us -> 192 us
  blocking collectives: 363 us -> 0 us
  waiting for transfers between devices: 350 us -> 97 us
  local copies, waits for them, and re-layouts: 63.7 us -> 3.55 us
  matrix products: 52.6 us -> 0 us
  Pallas kernels: 0 us -> 47.5 us
  other arithmetic: 48 us -> 2.23 us
    psum x5 -> x0, blocking collectives: 363 us -> none  [the longest x2 185 us: on_device(): coupling = lax.psum(product(basis_now, applied.T), 'rows')]
    all_to_all x4 -> x1, waiting for transfers between devices: 350 us -> 5.32 us  [on_device(): lax.all_to_all(send_list[0], 'rows', split_axis=0, concat_axis=0, tiled=T...]
    ppermute x0 -> x32, waiting for transfers between devices: none -> 91.7 us  [swap(): lax.ppermute(array, 'rows', [(place, place ^ offset) for place in range(c...]
    dot_general x16 -> x0, matrix products: 49.2 us -> none  [the longest x2 17.6 us: on_device(): lax.dot_general(arrived[tile_slots], tile_values, (((2,), (2,)), ((0,), (...]
    pallas_call x0 -> x10, Pallas kernels: none -> 47.5 us  [call(): pl.pallas_call(kernel, out_shape=out, in_specs=specs or [VMEM] * len(args...]
    all_to_all x4 -> x1, starting transfers between devices: 49.3 us -> 7.37 us  [on_device(): lax.all_to_all(send_list[0], 'rows', split_axis=0, concat_axis=0, tiled=T...]
    ppermute x0 -> x32, starting transfers between devices: none -> 32.9 us  [swap(): lax.ppermute(array, 'rows', [(place, place ^ offset) for place in range(c...]
    reshape x5 -> x1, local copies, waits for them, and re-layouts: 27.3 us -> 0.08 us  [on_device(): lax.all_to_all(send_list[0], 'rows', split_axis=0, concat_axis=0, tiled=T...]
  transfers between devices with their start and end apart: 4 -> 33, of which waited for: 4 -> 23; matrix products, arithmetic and copies ran while one was open for 11% -> 0% of each run, Pallas kernels for 0% -> 13%
where the time goes in v1:
time: 192 us
  waiting for transfers between devices  97 us (51%)
  Pallas kernels  47.5 us (25%)
  starting transfers between devices  40.3 us (21%)
  local copies, waits for them, and re-layouts  3.55 us (2%)
  other arithmetic  2.23 us (1%)
    ppermute x32, waiting for transfers between devices, swap(): lax.ppermute(array, 'rows', [(place, place ^ offset) for place in range(c...  91.7 us
    pallas_call x10, Pallas kernels, call(): pl.pallas_call(kernel, out_shape=out, in_specs=specs or [VMEM] * len(args...  47.5 us
    ppermute x32, starting transfers between devices, swap(): lax.ppermute(array, 'rows', [(place, place ^ offset) for place in range(c...  32.9 us
    all_to_all x1, starting transfers between devices, on_device(): lax.all_to_all(send_list[0], 'rows', split_axis=0, concat_axis=0, tiled=T...  7.37 us
    all_to_all x1, waiting for transfers between devices, on_device(): lax.all_to_all(send_list[0], 'rows', split_axis=0, concat_axis=0, tiled=T...  5.32 us
  transfers between devices with their start and end apart: 33, of which 23 were waited for; matrix products, arithmetic and copies ran while one was open for 0% of the time, Pallas kernels for 13%

profile of v1, /device:TPU:0, one launch (start us, length us, event | category | flops | bytes accessed | tf_op | source)
XLA Modules:
  0.0 191.5 jit_solution(14132071625591439688)
XLA Ops:
  0.6 7.4 %all-to-all-start = ((s32[16,1,16]{2,1,0:T(1,128)}), s32[16,1,16]{2,1,0:T(1,128)S(1)}, u32[]{:S(2)}, u32[]{:S(2)}) async-start(s32[16,1,16]{2,1,0:T(1,128)} %bitcast.49), calls=%async_computation | async-start | bytes 16384 | tf_op jit(solution)/shard_map/all_to_all | solution.py:243
  9.0 5.3 %all-to-all-done = s32[16,1,16]{2,1,0:T(1,128)S(1)} async-done(((s32[16,1,16]{2,1,0:T(1,128)}), s32[16,1,16]{2,1,0:T(1,128)S(1)}, u32[]{:S(2)}, u32[]{:S(2)}) %all-to-all-start) | async-done | bytes 1056 | tf_op jit(solution)/shard_map/all_to_all | solution.py:243
  17.6 8.1 %backward.2 = (f32[8,32,2048]{2,1,0:T(8,128)S(1)}, bf16[8,32,2048]{2,1,0:T(8,128)(2,1)S(1)}) custom-call(s32[1]{0:T(128)} %bitcast.1.me_ref, s32[96]{0:T(128)S(1)} %copy-done.3, s32[96]{0:T(128)S(1)} %copy-done.5, s32[256]{0:T(256)S(1)} %reshape.35.list_ref, s32[16]{0:T(128)S(1)} %copy-done.7, bf16[32,2048]{1,0:T(8,128)(2,1)S(1)} %get-tuple-element.20.high_ref, ...), custom_call_target="tpu_custom_call" | custom-call | flops 1610612736 | bytes 12582912 | tf_op jit(solution)/shard_map/backward/pallas_call | solution.py:221
  27.0 3.2 %collective-permute-start.2 = (bf16[32,2048]{1,0:T(8,128)(2,1)S(1)}, bf16[32,2048]{1,0:T(8,128)(2,1)S(1)}, u32[]{:S(2)}, u32[]{:S(2)}) collective-permute-start(bf16[32,2048]{1,0:T(8,128)(2,1)S(1)} %get-tuple-element.20.high_ref), channel_id=1, source_target_pairs={{0,12},{1,13},{2,14},{3,15},{4,8},{5,9},{6,10},{7,11},{8,4},{9,5},... | collective-permute-start | bytes 393224 | tf_op jit(solution)/shard_map/ppermute | solution.py:32
  30.2 3.2 %collective-permute-done = bf16[32,2048]{1,0:T(8,128)(2,1)S(1)} collective-permute-done((bf16[32,2048]{1,0:T(8,128)(2,1)S(1)}, bf16[32,2048]{1,0:T(8,128)(2,1)S(1)}, u32[]{:S(2)}, u32[]{:S(2)}) %collective-permute-start) | collective-permute-done | bytes 131104 | tf_op jit(solution)/shard_map/ppermute | solution.py:32
  33.4 5.9 %collective-permute-done.1 = bf16[32,2048]{1,0:T(8,128)(2,1)S(1)} collective-permute-done((bf16[32,2048]{1,0:T(8,128)(2,1)S(1)}, bf16[32,2048]{1,0:T(8,128)(2,1)S(1)}, u32[]{:S(2)}, u32[]{:S(2)}) %collective-permute-start.1) | collective-permute-done | bytes 131104 | tf_op jit(solution)/shard_map/ppermute | solution.py:32
  40.0 11.8 %collective-permute-done.3.refs_1_ = bf16[4,32,2048]{2,1,0:T(8,128)(2,1)S(1)} collective-permute-done((bf16[4,32,2048]{2,1,0:T(8,128)(2,1)S(1)}, bf16[4,32,2048]{2,1,0:T(8,128)(2,1)S(1)}, u32[]{:S(2)}, u32[]{:S(2)}) %collective-permute-start.3) | collective-permute-done | bytes 524320 | tf_op jit(solution)/shard_map/ppermute | solution.py:32
  53.7 9.2 %forward.2.forward_ref = f32[32,2048]{1,0:T(8,128)S(1)} custom-call(s32[1]{0:T(128)} %bitcast.1.me_ref, s32[96]{0:T(128)S(1)} %copy-done.3, s32[96]{0:T(128)S(1)} %copy-done.5, s32[256]{0:T(256)S(1)} %reshape.35.list_ref, s32[16]{0:T(128)S(1)} %copy-done.7, bf16[96,256,256]{2,1,0:T(8,128)(2,1)} %tiles_ref.7, ...), custom_call_target="tpu_custom_call" | custom-call | flops 1610612736 | bytes 12582912 | tf_op jit(solution)/shard_map/forward/pallas_call | solution.py:221
  62.9 3.5 %collective-permute-done.7 = bf16[4,32,2048]{2,1,0:T(8,128)(2,1)S(1)} collective-permute-done((bf16[4,32,2048]{2,1,0:T(8,128)(2,1)S(1)}, bf16[4,32,2048]{2,1,0:T(8,128)(2,1)S(1)}, u32[]{:S(2)}, u32[]{:S(2)}) %collective-permute-start.7) | collective-permute-done | bytes 524320 | tf_op jit(solution)/shard_map/ppermute | solution.py:32
  66.6 3.4 %collective-permute-start.10 = (bf16[32,2048]{1,0:T(8,128)(2,1)S(1)}, bf16[32,2048]{1,0:T(8,128)(2,1)S(1)}, u32[]{:S(2)}, u32[]{:S(2)}) collective-permute-start(bf16[32,2048]{1,0:T(8,128)(2,1)S(1)} %get-tuple-element.44), channel_id=1, source_target_pairs={{0,4},{1,5},{2,6},{3,7},{4,0},{5,1},{6,2},{7,3},{8,12},{9,13},{10,... | collective-permute-start | bytes 393224 | tf_op jit(solution)/shard_map/ppermute | solution.py:32
  71.6 2.4 %collective-permute-done.10.refs_4_ = bf16[32,2048]{1,0:T(8,128)(2,1)S(1)} collective-permute-done((bf16[32,2048]{1,0:T(8,128)(2,1)S(1)}, bf16[32,2048]{1,0:T(8,128)(2,1)S(1)}, u32[]{:S(2)}, u32[]{:S(2)}) %collective-permute-start.10) | collective-permute-done | bytes 131104 | tf_op jit(solution)/shard_map/ppermute | solution.py:32
  73.9 4.3 %collective-permute-done.8.refs_2_ = bf16[32,2048]{1,0:T(8,128)(2,1)S(1)} collective-permute-done((bf16[32,2048]{1,0:T(8,128)(2,1)S(1)}, bf16[32,2048]{1,0:T(8,128)(2,1)S(1)}, u32[]{:S(2)}, u32[]{:S(2)}) %collective-permute-start.8) | collective-permute-done | bytes 131104 | tf_op jit(solution)/shard_map/ppermute | solution.py:32
  78.2 4.8 %collective-permute-done.9.refs_3_ = bf16[32,2048]{1,0:T(8,128)(2,1)S(1)} collective-permute-done((bf16[32,2048]{1,0:T(8,128)(2,1)S(1)}, bf16[32,2048]{1,0:T(8,128)(2,1)S(1)}, u32[]{:S(2)}, u32[]{:S(2)}) %collective-permute-start.9) | collective-permute-done | bytes 131104 | tf_op jit(solution)/shard_map/ppermute | solution.py:32
  83.3 8.1 %backward.3 = (f32[8,32,2048]{2,1,0:T(8,128)S(1)}, bf16[8,32,2048]{2,1,0:T(8,128)(2,1)S(1)}) custom-call(s32[1]{0:T(128)} %bitcast.1.me_ref, s32[96]{0:T(128)S(1)} %copy-done.4, s32[96]{0:T(128)S(1)} %copy-done.6, s32[256]{0:T(256)S(1)} %reshape.35.list_ref, s32[16]{0:T(128)S(1)} %copy-done.8, bf16[32,2048]{1,0:T(8,128)(2,1)S(1)} %get-tuple-element.26.high_ref, ...), custom_call_target="tpu_custom_call" | custom-call | flops 1610612736 | bytes 12582912 | tf_op jit(solution)/shard_map/backward/pallas_call | solution.py:221
  91.5 2.0 %collective-permute-start.17 = (bf16[32,2048]{1,0:T(8,128)(2,1)S(1)}, bf16[32,2048]{1,0:T(8,128)(2,1)S(1)}, u32[]{:S(2)}, u32[]{:S(2)}) collective-permute-start(bf16[32,2048]{1,0:T(8,128)(2,1)S(1)} %get-tuple-element.26.high_ref), channel_id=1, source_target_pairs={{0,8},{1,9},{2,10},{3,11},{4,12},{5,13},{6,14},{7,15},{8,0},{9,1},... | collective-permute-start | bytes 393224 | tf_op jit(solution)/shard_map/ppermute | solution.py:32
  93.6 2.3 %collective-permute-start.18 = (bf16[32,2048]{1,0:T(8,128)(2,1)S(1)}, bf16[32,2048]{1,0:T(8,128)(2,1)S(1)}, u32[]{:S(2)}, u32[]{:S(2)}) collective-permute-start(bf16[32,2048]{1,0:T(8,128)(2,1)S(1)} %get-tuple-element.26.high_ref), channel_id=1, source_target_pairs={{0,12},{1,13},{2,14},{3,15},{4,8},{5,9},{6,10},{7,11},{8,4},{9,5},... | collective-permute-start | bytes 393224 | tf_op jit(solution)/shard_map/ppermute | solution.py:32
  95.9 3.2 %collective-permute-done.16 = bf16[32,2048]{1,0:T(8,128)(2,1)S(1)} collective-permute-done((bf16[32,2048]{1,0:T(8,128)(2,1)S(1)}, bf16[32,2048]{1,0:T(8,128)(2,1)S(1)}, u32[]{:S(2)}, u32[]{:S(2)}) %collective-permute-start.16) | collective-permute-done | bytes 131104 | tf_op jit(solution)/shard_map/ppermute | solution.py:32
  99.1 5.4 %collective-permute-done.17 = bf16[32,2048]{1,0:T(8,128)(2,1)S(1)} collective-permute-done((bf16[32,2048]{1,0:T(8,128)(2,1)S(1)}, bf16[32,2048]{1,0:T(8,128)(2,1)S(1)}, u32[]{:S(2)}, u32[]{:S(2)}) %collective-permute-start.17) | collective-permute-done | bytes 131104 | tf_op jit(solution)/shard_map/ppermute | solution.py:32
  105.2 12.2 %collective-permute-done.19.refs_1_ = bf16[4,32,2048]{2,1,0:T(8,128)(2,1)S(1)} collective-permute-done((bf16[4,32,2048]{2,1,0:T(8,128)(2,1)S(1)}, bf16[4,32,2048]{2,1,0:T(8,128)(2,1)S(1)}, u32[]{:S(2)}, u32[]{:S(2)}) %collective-permute-start.19) | collective-permute-done | bytes 524320 | tf_op jit(solution)/shard_map/ppermute | solution.py:32
  121.7 11.2 %collective-permute-done.12 = f32[64,64]{1,0:T(8,128)S(1)} collective-permute-done((f32[64,64]{1,0:T(8,128)S(1)}, f32[64,64]{1,0:T(8,128)S(1)}, u32[]{:S(2)}, u32[]{:S(2)}) %collective-permute-start.12) | collective-permute-done | bytes 16416 | tf_op jit(solution)/shard_map/ppermute | solution.py:32
  132.8 3.4 %collective-permute-start.13 = (f32[64,64]{1,0:T(8,128)S(1)}, f32[64,64]{1,0:T(8,128)S(1)}, u32[]{:S(2)}, u32[]{:S(2)}) collective-permute-start(f32[64,64]{1,0:T(8,128)S(1)} %add.72), channel_id=1, source_target_pairs={{0,4},{1,5},{2,6},{3,7},{4,0},{5,1},{6,2},{7,3},{8,12},{9,13},{10,... | collective-permute-start | bytes 49160 | tf_op jit(solution)/shard_map/ppermute | solution.py:32
  141.3 2.5 %collective-permute-done.15 = f32[64,64]{1,0:T(8,128)S(1)} collective-permute-done((f32[64,64]{1,0:T(8,128)S(1)}, f32[64,64]{1,0:T(8,128)S(1)}, u32[]{:S(2)}, u32[]{:S(2)}) %collective-permute-start.15) | collective-permute-done | bytes 16416 | tf_op jit(solution)/shard_map/ppermute | solution.py:32
  143.8 6.2 %coefficients.1 = (f32[32,32]{1,0:T(8,128)S(1)}, f32[32,32]{1,0:T(8,128)S(1)}, f32[96,96]{1,0:T(8,128)S(1)}) custom-call(f32[64,64]{1,0:T(8,128)S(1)} %add_add_fusion.1.gram_ref), custom_call_target="tpu_custom_call" | custom-call | tf_op jit(solution)/shard_map/coefficients/pallas_call | solution.py:221
  150.0 9.2 %forward.3.forward_ref = f32[32,2048]{1,0:T(8,128)S(1)} custom-call(s32[1]{0:T(128)} %bitcast.1.me_ref, s32[96]{0:T(128)S(1)} %copy-done.4, s32[96]{0:T(128)S(1)} %copy-done.6, s32[256]{0:T(256)S(1)} %reshape.35.list_ref, s32[16]{0:T(128)S(1)} %copy-done.8, bf16[96,256,256]{2,1,0:T(8,128)(2,1)} %tiles_ref.7, ...), custom_call_target="tpu_custom_call" | custom-call | flops 1610612736 | bytes 12582912 | tf_op jit(solution)/shard_map/forward/pallas_call | solution.py:221
  161.1 2.7 %collective-permute-start.26 = (bf16[32,2048]{1,0:T(8,128)(2,1)S(1)}, bf16[32,2048]{1,0:T(8,128)(2,1)S(1)}, u32[]{:S(2)}, u32[]{:S(2)}) collective-permute-start(bf16[32,2048]{1,0:T(8,128)(2,1)S(1)} %get-tuple-element.41), channel_id=1, source_target_pairs={{0,4},{1,5},{2,6},{3,7},{4,0},{5,1},{6,2},{7,3},{8,12},{9,13},{10,... | collective-permute-start | bytes 393224 | tf_op jit(solution)/shard_map/ppermute | solution.py:32
  163.8 3.4 %collective-permute-done.24.refs_2_ = bf16[32,2048]{1,0:T(8,128)(2,1)S(1)} collective-permute-done((bf16[32,2048]{1,0:T(8,128)(2,1)S(1)}, bf16[32,2048]{1,0:T(8,128)(2,1)S(1)}, u32[]{:S(2)}, u32[]{:S(2)}) %collective-permute-start.24) | collective-permute-done | bytes 131104 | tf_op jit(solution)/shard_map/ppermute | solution.py:32
  167.2 4.1 %collective-permute-done.25.refs_3_ = bf16[32,2048]{1,0:T(8,128)(2,1)S(1)} collective-permute-done((bf16[32,2048]{1,0:T(8,128)(2,1)S(1)}, bf16[32,2048]{1,0:T(8,128)(2,1)S(1)}, u32[]{:S(2)}, u32[]{:S(2)}) %collective-permute-start.25) | collective-permute-done | bytes 131104 | tf_op jit(solution)/shard_map/ppermute | solution.py:32
  175.0 3.5 %collective-permute-done.28 = f32[96,32]{1,0:T(8,128)S(1)} collective-permute-done((f32[96,32]{1,0:T(8,128)S(1)}, f32[96,32]{1,0:T(8,128)S(1)}, u32[]{:S(2)}, u32[]{:S(2)}) %collective-permute-start.28) | collective-permute-done | bytes 12320 | tf_op jit(solution)/shard_map/ppermute | solution.py:32
  178.5 2.1 %collective-permute-start.30 = (f32[96,32]{1,0:T(8,128)S(1)}, f32[96,32]{1,0:T(8,128)S(1)}, u32[]{:S(2)}, u32[]{:S(2)}) collective-permute-start(f32[96,32]{1,0:T(8,128)S(1)} %add.82), channel_id=1, source_target_pairs={{0,8},{1,9},{2,10},{3,11},{4,12},{5,13},{6,14},{7,15},{8,0},{9,1},... | collective-permute-start | bytes 36872 | tf_op jit(solution)/shard_map/ppermute | solution.py:32
  180.7 2.2 %collective-permute-start.31 = (f32[96,32]{1,0:T(8,128)S(1)}, f32[96,32]{1,0:T(8,128)S(1)}, u32[]{:S(2)}, u32[]{:S(2)}) collective-permute-start(f32[96,32]{1,0:T(8,128)S(1)} %add.82), channel_id=1, source_target_pairs={{0,12},{1,13},{2,14},{3,15},{4,8},{5,9},{6,10},{7,11},{8,4},{9,5},... | collective-permute-start | bytes 36872 | tf_op jit(solution)/shard_map/ppermute | solution.py:32
  184.1 2.4 %collective-permute-done.31 = f32[96,32]{1,0:T(8,128)S(1)} collective-permute-done((f32[96,32]{1,0:T(8,128)S(1)}, f32[96,32]{1,0:T(8,128)S(1)}, u32[]{:S(2)}, u32[]{:S(2)}) %collective-permute-start.31) | collective-permute-done | bytes 12320 | tf_op jit(solution)/shard_map/ppermute | solution.py:32
  186.6 4.3 %last.1 = (f32[32,2048]{1,0:T(8,128)}, f32[32,32]{1,0:T(8,128)S(1)}, f32[32,32]{1,0:T(8,128)S(1)}) custom-call(f32[96,32]{1,0:T(8,128)S(1)} %add_add_fusion.gram_ref, f32[32,32]{1,0:T(8,128)S(1)} %get-tuple-element.31.factor_ref, f32[96,2048]{1,0:T(8,128)S(1)} %get-tuple-element.32.basis_ref), custom_call_target="tpu_custom_call" | custom-call | tf_op jit(solution)/shard_map/last/pallas_call | solution.py:221
  (80 shorter events, 27.5 us)
Async XLA Ops:
  0.6 13.7 %all-to-all-start = ((s32[16,1,16]{2,1,0:T(1,128)}), s32[16,1,16]{2,1,0:T(1,128)S(1)}, u32[]{:S(2)}, u32[]{:S(2)}) async-start(s32[16,1,16]{2,1,0:T(1,128)} %bitcast.49), calls=%async_computation | async-start | bytes 16384 | tf_op jit(solution)/shard_map/all_to_all | solution.py:243
  25.7 26.1 %collective-permute-start.6 = (bf16[8,32,2048]{2,1,0:T(8,128)(2,1)S(1)}, bf16[8,32,2048]{2,1,0:T(8,128)(2,1)S(1)}, u32[]{:S(2)}, u32[]{:S(2)}) collective-permute-start(bf16[8,32,2048]{2,1,0:T(8,128)(2,1)S(1)} %get-tuple-element.23), channel_id=1, source_target_pairs={{0,1},{1,0},{2,3},{3,2},{4,5},{5,4},{6,7},{7,6},{8,9},{9,8},{10,11... | collective-permute-start | bytes 3145736 | tf_op jit(solution)/shard_map/ppermute | solution.py:32
  25.7 7.6 %collective-permute-start = (bf16[32,2048]{1,0:T(8,128)(2,1)S(1)}, bf16[32,2048]{1,0:T(8,128)(2,1)S(1)}, u32[]{:S(2)}, u32[]{:S(2)}) collective-permute-start(bf16[32,2048]{1,0:T(8,128)(2,1)S(1)} %get-tuple-element.20.high_ref), channel_id=1, source_target_pairs={{0,4},{1,5},{2,6},{3,7},{4,0},{5,1},{6,2},{7,3},{8,12},{9,13},{10,... | collective-permute-start | bytes 393224 | tf_op jit(solution)/shard_map/ppermute | solution.py:32
  26.3 12.9 %collective-permute-start.1 = (bf16[32,2048]{1,0:T(8,128)(2,1)S(1)}, bf16[32,2048]{1,0:T(8,128)(2,1)S(1)}, u32[]{:S(2)}, u32[]{:S(2)}) collective-permute-start(bf16[32,2048]{1,0:T(8,128)(2,1)S(1)} %get-tuple-element.20.high_ref), channel_id=1, source_target_pairs={{0,8},{1,9},{2,10},{3,11},{4,12},{5,13},{6,14},{7,15},{8,0},{9,1},... | collective-permute-start | bytes 393224 | tf_op jit(solution)/shard_map/ppermute | solution.py:32
  27.0 12.3 %collective-permute-start.2 = (bf16[32,2048]{1,0:T(8,128)(2,1)S(1)}, bf16[32,2048]{1,0:T(8,128)(2,1)S(1)}, u32[]{:S(2)}, u32[]{:S(2)}) collective-permute-start(bf16[32,2048]{1,0:T(8,128)(2,1)S(1)} %get-tuple-element.20.high_ref), channel_id=1, source_target_pairs={{0,12},{1,13},{2,14},{3,15},{4,8},{5,9},{6,10},{7,11},{8,4},{9,5},... | collective-permute-start | bytes 393224 | tf_op jit(solution)/shard_map/ppermute | solution.py:32
  39.3 12.5 %collective-permute-start.3 = (bf16[4,32,2048]{2,1,0:T(8,128)(2,1)S(1)}, bf16[4,32,2048]{2,1,0:T(8,128)(2,1)S(1)}, u32[]{:S(2)}, u32[]{:S(2)}) collective-permute-start(bf16[4,32,2048]{2,1,0:T(8,128)(2,1)S(1)} %pad_maximum_fusion.refs_0_), channel_id=1, source_target_pairs={{0,2},{1,3},{2,0},{3,1},{4,6},{5,7},{6,4},{7,5},{8,10},{9,11},{10,... | collective-permute-start | bytes 1572872 | tf_op jit(solution)/shard_map/ppermute | solution.py:32
  39.9 12.7 %collective-permute-start.4 = (bf16[4,32,2048]{2,1,0:T(8,128)(2,1)S(1)}, bf16[4,32,2048]{2,1,0:T(8,128)(2,1)S(1)}, u32[]{:S(2)}, u32[]{:S(2)}) collective-permute-start(bf16[4,32,2048]{2,1,0:T(8,128)(2,1)S(1)} %pad_maximum_fusion.refs_0_), channel_id=1, source_target_pairs={{0,1},{1,0},{2,3},{3,2},{4,5},{5,4},{6,7},{7,6},{8,9},{9,8},{10,11... | collective-permute-start | bytes 1572872 | tf_op jit(solution)/shard_map/ppermute | solution.py:32
  51.8 1.9 collective-permute-start.5
  52.1 14.4 %collective-permute-start.7 = (bf16[4,32,2048]{2,1,0:T(8,128)(2,1)S(1)}, bf16[4,32,2048]{2,1,0:T(8,128)(2,1)S(1)}, u32[]{:S(2)}, u32[]{:S(2)}) collective-permute-start(bf16[4,32,2048]{2,1,0:T(8,128)(2,1)S(1)} %get-tuple-element.39), channel_id=1, source_target_pairs={{0,2},{1,3},{2,0},{3,1},{4,6},{5,7},{6,4},{7,5},{8,10},{9,11},{10,... | collective-permute-start | bytes 1572872 | tf_op jit(solution)/shard_map/ppermute | solution.py:32
  66.6 7.4 %collective-permute-start.10 = (bf16[32,2048]{1,0:T(8,128)(2,1)S(1)}, bf16[32,2048]{1,0:T(8,128)(2,1)S(1)}, u32[]{:S(2)}, u32[]{:S(2)}) collective-permute-start(bf16[32,2048]{1,0:T(8,128)(2,1)S(1)} %get-tuple-element.44), channel_id=1, source_target_pairs={{0,4},{1,5},{2,6},{3,7},{4,0},{5,1},{6,2},{7,3},{8,12},{9,13},{10,... | collective-permute-start | bytes 393224 | tf_op jit(solution)/shard_map/ppermute | solution.py:32
  70.0 8.2 %collective-permute-start.8 = (bf16[32,2048]{1,0:T(8,128)(2,1)S(1)}, bf16[32,2048]{1,0:T(8,128)(2,1)S(1)}, u32[]{:S(2)}, u32[]{:S(2)}) collective-permute-start(bf16[32,2048]{1,0:T(8,128)(2,1)S(1)} %get-tuple-element.46), channel_id=1, source_target_pairs={{0,12},{1,13},{2,14},{3,15},{4,8},{5,9},{6,10},{7,11},{8,4},{9,5},... | collective-permute-start | bytes 393224 | tf_op jit(solution)/shard_map/ppermute | solution.py:32
  71.5 11.6 %collective-permute-start.9 = (bf16[32,2048]{1,0:T(8,128)(2,1)S(1)}, bf16[32,2048]{1,0:T(8,128)(2,1)S(1)}, u32[]{:S(2)}, u32[]{:S(2)}) collective-permute-start(bf16[32,2048]{1,0:T(8,128)(2,1)S(1)} %get-tuple-element.45), channel_id=1, source_target_pairs={{0,8},{1,9},{2,10},{3,11},{4,12},{5,13},{6,14},{7,15},{8,0},{9,1},... | collective-permute-start | bytes 393224 | tf_op jit(solution)/shard_map/ppermute | solution.py:32
  91.4 26.1 %collective-permute-start.22 = (bf16[8,32,2048]{2,1,0:T(8,128)(2,1)S(1)}, bf16[8,32,2048]{2,1,0:T(8,128)(2,1)S(1)}, u32[]{:S(2)}, u32[]{:S(2)}) collective-permute-start(bf16[8,32,2048]{2,1,0:T(8,128)(2,1)S(1)} %get-tuple-element.29), channel_id=1, source_target_pairs={{0,1},{1,0},{2,3},{3,2},{4,5},{5,4},{6,7},{7,6},{8,9},{9,8},{10,11... | collective-permute-start | bytes 3145736 | tf_op jit(solution)/shard_map/ppermute | solution.py:32
  91.4 7.6 %collective-permute-start.16 = (bf16[32,2048]{1,0:T(8,128)(2,1)S(1)}, bf16[32,2048]{1,0:T(8,128)(2,1)S(1)}, u32[]{:S(2)}, u32[]{:S(2)}) collective-permute-start(bf16[32,2048]{1,0:T(8,128)(2,1)S(1)} %get-tuple-element.26.high_ref), channel_id=1, source_target_pairs={{0,4},{1,5},{2,6},{3,7},{4,0},{5,1},{6,2},{7,3},{8,12},{9,13},{10,... | collective-permute-start | bytes 393224 | tf_op jit(solution)/shard_map/ppermute | solution.py:32
  91.5 12.9 %collective-permute-start.17 = (bf16[32,2048]{1,0:T(8,128)(2,1)S(1)}, bf16[32,2048]{1,0:T(8,128)(2,1)S(1)}, u32[]{:S(2)}, u32[]{:S(2)}) collective-permute-start(bf16[32,2048]{1,0:T(8,128)(2,1)S(1)} %get-tuple-element.26.high_ref), channel_id=1, source_target_pairs={{0,8},{1,9},{2,10},{3,11},{4,12},{5,13},{6,14},{7,15},{8,0},{9,1},... | collective-permute-start | bytes 393224 | tf_op jit(solution)/shard_map/ppermute | solution.py:32
  93.6 10.9 %collective-permute-start.18 = (bf16[32,2048]{1,0:T(8,128)(2,1)S(1)}, bf16[32,2048]{1,0:T(8,128)(2,1)S(1)}, u32[]{:S(2)}, u32[]{:S(2)}) collective-permute-start(bf16[32,2048]{1,0:T(8,128)(2,1)S(1)} %get-tuple-element.26.high_ref), channel_id=1, source_target_pairs={{0,12},{1,13},{2,14},{3,15},{4,8},{5,9},{6,10},{7,11},{8,4},{9,5},... | collective-permute-start | bytes 393224 | tf_op jit(solution)/shard_map/ppermute | solution.py:32
  104.5 12.9 %collective-permute-start.19 = (bf16[4,32,2048]{2,1,0:T(8,128)(2,1)S(1)}, bf16[4,32,2048]{2,1,0:T(8,128)(2,1)S(1)}, u32[]{:S(2)}, u32[]{:S(2)}) collective-permute-start(bf16[4,32,2048]{2,1,0:T(8,128)(2,1)S(1)} %pad_maximum_fusion.1.refs_0_), channel_id=1, source_target_pairs={{0,2},{1,3},{2,0},{3,1},{4,6},{5,7},{6,4},{7,5},{8,10},{9,11},{10,... | collective-permute-start | bytes 1572872 | tf_op jit(solution)/shard_map/ppermute | solution.py:32
  105.2 44.8 %collective-permute-start.20 = (bf16[4,32,2048]{2,1,0:T(8,128)(2,1)S(1)}, bf16[4,32,2048]{2,1,0:T(8,128)(2,1)S(1)}, u32[]{:S(2)}, u32[]{:S(2)}) collective-permute-start(bf16[4,32,2048]{2,1,0:T(8,128)(2,1)S(1)} %pad_maximum_fusion.1.refs_0_), channel_id=1, source_target_pairs={{0,1},{1,0},{2,3},{3,2},{4,5},{5,4},{6,7},{7,6},{8,9},{9,8},{10,11... | collective-permute-start | bytes 1572872 | tf_op jit(solution)/shard_map/ppermute | solution.py:32
  117.4 32.6 %collective-permute-start.21 = (bf16[4,32,2048]{2,1,0:T(8,128)(2,1)S(1)}, bf16[4,32,2048]{2,1,0:T(8,128)(2,1)S(1)}, u32[]{:S(2)}, u32[]{:S(2)}) collective-permute-start(bf16[4,32,2048]{2,1,0:T(8,128)(2,1)S(1)} %collective-permute-done.19.refs_1_), channel_id=1, source_target_pairs={{0,1},{1,0},{2,3},{3,2},{4,5},{5,4},{6,7},{7,6},{8,9},{9,8},{10,11... | collective-permute-start | bytes 1572872 | tf_op jit(solution)/shard_map/ppermute | solution.py:32
  117.7 41.5 %collective-permute-start.23 = (bf16[4,32,2048]{2,1,0:T(8,128)(2,1)S(1)}, bf16[4,32,2048]{2,1,0:T(8,128)(2,1)S(1)}, u32[]{:S(2)}, u32[]{:S(2)}) collective-permute-start(bf16[4,32,2048]{2,1,0:T(8,128)(2,1)S(1)} %get-tuple-element.37), channel_id=1, source_target_pairs={{0,2},{1,3},{2,0},{3,1},{4,6},{5,7},{6,4},{7,5},{8,10},{9,11},{10,... | collective-permute-start | bytes 1572872 | tf_op jit(solution)/shard_map/ppermute | solution.py:32
  120.2 12.6 %collective-permute-start.12 = (f32[64,64]{1,0:T(8,128)S(1)}, f32[64,64]{1,0:T(8,128)S(1)}, u32[]{:S(2)}, u32[]{:S(2)}) collective-permute-start(f32[64,64]{1,0:T(8,128)S(1)} %add.71), channel_id=1, source_target_pairs={{0,2},{1,3},{2,0},{3,1},{4,6},{5,7},{6,4},{7,5},{8,10},{9,11},{10,... | collective-permute-start | bytes 49160 | tf_op jit(solution)/shard_map/ppermute | solution.py:32
  132.8 5.3 %collective-permute-start.13 = (f32[64,64]{1,0:T(8,128)S(1)}, f32[64,64]{1,0:T(8,128)S(1)}, u32[]{:S(2)}, u32[]{:S(2)}) collective-permute-start(f32[64,64]{1,0:T(8,128)S(1)} %add.72), channel_id=1, source_target_pairs={{0,4},{1,5},{2,6},{3,7},{4,0},{5,1},{6,2},{7,3},{8,12},{9,13},{10,... | collective-permute-start | bytes 49160 | tf_op jit(solution)/shard_map/ppermute | solution.py:32
  136.2 5.1 %collective-permute-start.14 = (f32[64,64]{1,0:T(8,128)S(1)}, f32[64,64]{1,0:T(8,128)S(1)}, u32[]{:S(2)}, u32[]{:S(2)}) collective-permute-start(f32[64,64]{1,0:T(8,128)S(1)} %add.72), channel_id=1, source_target_pairs={{0,8},{1,9},{2,10},{3,11},{4,12},{5,13},{6,14},{7,15},{8,0},{9,1},... | collective-permute-start | bytes 49160 | tf_op jit(solution)/shard_map/ppermute | solution.py:32
  138.1 5.7 %collective-permute-start.15 = (f32[64,64]{1,0:T(8,128)S(1)}, f32[64,64]{1,0:T(8,128)S(1)}, u32[]{:S(2)}, u32[]{:S(2)}) collective-permute-start(f32[64,64]{1,0:T(8,128)S(1)} %add.72), channel_id=1, source_target_pairs={{0,12},{1,13},{2,14},{3,15},{4,8},{5,9},{6,10},{7,11},{8,4},{9,5},... | collective-permute-start | bytes 49160 | tf_op jit(solution)/shard_map/ppermute | solution.py:32
  159.4 7.9 %collective-permute-start.24 = (bf16[32,2048]{1,0:T(8,128)(2,1)S(1)}, bf16[32,2048]{1,0:T(8,128)(2,1)S(1)}, u32[]{:S(2)}, u32[]{:S(2)}) collective-permute-start(bf16[32,2048]{1,0:T(8,128)(2,1)S(1)} %get-tuple-element.43), channel_id=1, source_target_pairs={{0,12},{1,13},{2,14},{3,15},{4,8},{5,9},{6,10},{7,11},{8,4},{9,5},... | collective-permute-start | bytes 393224 | tf_op jit(solution)/shard_map/ppermute | solution.py:32
  161.0 10.4 %collective-permute-start.25 = (bf16[32,2048]{1,0:T(8,128)(2,1)S(1)}, bf16[32,2048]{1,0:T(8,128)(2,1)S(1)}, u32[]{:S(2)}, u32[]{:S(2)}) collective-permute-start(bf16[32,2048]{1,0:T(8,128)(2,1)S(1)} %get-tuple-element.42), channel_id=1, source_target_pairs={{0,8},{1,9},{2,10},{3,11},{4,12},{5,13},{6,14},{7,15},{8,0},{9,1},... | collective-permute-start | bytes 393224 | tf_op jit(solution)/shard_map/ppermute | solution.py:32
  161.1 10.2 %collective-permute-start.26 = (bf16[32,2048]{1,0:T(8,128)(2,1)S(1)}, bf16[32,2048]{1,0:T(8,128)(2,1)S(1)}, u32[]{:S(2)}, u32[]{:S(2)}) collective-permute-start(bf16[32,2048]{1,0:T(8,128)(2,1)S(1)} %get-tuple-element.41), channel_id=1, source_target_pairs={{0,4},{1,5},{2,6},{3,7},{4,0},{5,1},{6,2},{7,3},{8,12},{9,13},{10,... | collective-permute-start | bytes 393224 | tf_op jit(solution)/shard_map/ppermute | solution.py:32
  173.0 1.3 collective-permute-start.27
  174.3 4.2 %collective-permute-start.28 = (f32[96,32]{1,0:T(8,128)S(1)}, f32[96,32]{1,0:T(8,128)S(1)}, u32[]{:S(2)}, u32[]{:S(2)}) collective-permute-start(f32[96,32]{1,0:T(8,128)S(1)} %add.81), channel_id=1, source_target_pairs={{0,2},{1,3},{2,0},{3,1},{4,6},{5,7},{6,4},{7,5},{8,10},{9,11},{10,... | collective-permute-start | bytes 36872 | tf_op jit(solution)/shard_map/ppermute | solution.py:32
  178.5 4.5 %collective-permute-start.29 = (f32[96,32]{1,0:T(8,128)S(1)}, f32[96,32]{1,0:T(8,128)S(1)}, u32[]{:S(2)}, u32[]{:S(2)}) collective-permute-start(f32[96,32]{1,0:T(8,128)S(1)} %add.82), channel_id=1, source_target_pairs={{0,4},{1,5},{2,6},{3,7},{4,0},{5,1},{6,2},{7,3},{8,12},{9,13},{10,... | collective-permute-start | bytes 36872 | tf_op jit(solution)/shard_map/ppermute | solution.py:32
  178.5 5.6 %collective-permute-start.30 = (f32[96,32]{1,0:T(8,128)S(1)}, f32[96,32]{1,0:T(8,128)S(1)}, u32[]{:S(2)}, u32[]{:S(2)}) collective-permute-start(f32[96,32]{1,0:T(8,128)S(1)} %add.82), channel_id=1, source_target_pairs={{0,8},{1,9},{2,10},{3,11},{4,12},{5,13},{6,14},{7,15},{8,0},{9,1},... | collective-permute-start | bytes 36872 | tf_op jit(solution)/shard_map/ppermute | solution.py:32
  180.7 5.9 %collective-permute-start.31 = (f32[96,32]{1,0:T(8,128)S(1)}, f32[96,32]{1,0:T(8,128)S(1)}, u32[]{:S(2)}, u32[]{:S(2)}) collective-permute-start(f32[96,32]{1,0:T(8,128)S(1)} %add.82), channel_id=1, source_target_pairs={{0,12},{1,13},{2,14},{3,15},{4,8},{5,9},{6,10},{7,11},{8,4},{9,5},... | collective-permute-start | bytes 36872 | tf_op jit(solution)/shard_map/ppermute | solution.py:32
  (10 other events, 105.5 us)

commit v2 on v1

--- a/solution.py
+++ b/solution.py
@@ -12,6 +12,7 @@
 precise = lax.Precision.HIGHEST
 SMEM = pl.BlockSpec(memory_space=pltpu.SMEM)
 VMEM = pl.BlockSpec(memory_space=pltpu.VMEM)
+ANY = pl.BlockSpec(memory_space=pl.ANY)
 UNROLL = 16
 
 
@@ -52,7 +53,13 @@
 
 def gather_panel(panel):
     low, shift, wide = stages(lax.axis_size("rows"))
-    arrays = [jnp.stack([panel] + [swap(panel, far << shift) for far in range(1, wide)])]
+    return [panel] + [swap(panel, far << shift) for far in range(1, wide)]
+
+
+def spread_panels(pieces, token):
+    low, shift, wide = stages(lax.axis_size("rows"))
+    step = max(1, wide // 2)
+    arrays = [stacked(pieces[at : at + step], token) for at in range(0, wide, step)]
     for bit in reversed(low):
         arrays = arrays + [swap(array, 1 << bit) for array in arrays]
     return arrays
@@ -60,16 +67,45 @@
 
 def reduce_panels(kept, sent):
     low, shift, wide = stages(lax.axis_size("rows"))
-    for bit in low:
+    for bit in low[:-1]:
         arrived = swap(sent, 1 << bit)
         half = kept.shape[0] // 2
-        if bit != low[-1]:
-            sent = (kept[half:] + arrived[half:]).astype(jnp.bfloat16)
-            kept = kept[:half] + arrived[:half]
+        kept, sent = added(kept, arrived)
+    near, far = sent[: wide // 2], sent[wide // 2 :]
+    arrived = [swap(far, 1 << low[-1]), swap(near, 1 << low[-1])]
+    return kept, arrived
+
+
+def finish_panels(kept, arrived):
+    low, shift, wide = stages(lax.axis_size("rows"))
+    far, near = arrived
     terms = []
-    for far in range(wide - 1, 0, -1):
-        terms.append(swap((kept[far] + arrived[far]).astype(jnp.bfloat16), far << shift))
-    return [kept[0], arrived[0]] + terms
+    for place in range(wide - 1, 0, -1):
+        part = far[place - wide // 2] if place >= wide // 2 else near[place]
+        terms.append(swap((kept[place] + part).astype(jnp.bfloat16), place << shift))
+    return [kept[0], near[0]] + terms
+
+
+def added_kernel(kept_ref, arrived_ref, near_ref, far_ref):
+    half = near_ref.shape[0]
+    near_ref[...] = kept_ref[:half] + arrived_ref[:half].astype(jnp.float32)
+    far_ref[...] = (kept_ref[half:] + arrived_ref[half:].astype(jnp.float32)).astype(jnp.bfloat16)
+
+
+def added(kept, arrived):
+    half, width, here = kept.shape[0] // 2, *kept.shape[1:]
+    shape = jax.ShapeDtypeStruct
+    return call(added_kernel, (shape((half, width, here), jnp.float32), shape((half, width, here), jnp.bfloat16)), kept, arrived, name="added")
+
+
+def stacked_kernel(*refs):
+    for index, ref in enumerate(refs[:-2]):
+        refs[-1][index] = ref[...]
+
+
+def stacked(pieces, token):
+    out = jax.ShapeDtypeStruct((len(pieces), *pieces[0].shape), pieces[0].dtype)
+    return call(stacked_kernel, out, *pieces, token, name="stacked", specs=[VMEM] * len(pieces) + [ANY])
 
 
 def reduce_small(array):
@@ -140,7 +176,7 @@
 
 def combine_kernel(links_ref, panel_ref, forward_ref, *refs):
     term_refs, (out_ref, high_ref, low_ref) = refs[:-3], refs[-3:]
-    out = links_ref[...] * panel_ref[...] + forward_ref[...]
+    out = (links_ref[...] - 1.0) * panel_ref[...] + forward_ref[...]
     for ref in term_refs:
         out = out + ref[...].astype(jnp.float32)
     out_ref[...] = out
@@ -149,7 +185,7 @@
     low_ref[...] = (out - high.astype(jnp.float32)).astype(jnp.bfloat16)
 
 
-def gram_kernel(left_ref, right_ref, out_ref):
+def gram_kernel(left_ref, right_ref, token_ref, out_ref):
     both = jnp.concatenate([left_ref[...], right_ref[...]], axis=0)
     out_ref[...] = product_t(both, both)
 
@@ -171,14 +207,16 @@
     return factor, found[:, width:]
 
 
-def first_coefficients_kernel(gram_ref, coupling_ref, factor_ref, mix_ref):
+def first_coefficients_kernel(gram_ref, token_ref, coupling_ref, factor_ref, mix_ref):
     width = gram_ref.shape[0] // 2
     gram = gram_ref[...]
     _, inverse0 = factor_of(gram[:width, :width])
     coupling = product_t(product(inverse0, gram[:width, width:]), inverse0)
     image = product_t(product(inverse0, gram[width:, width:]), inverse0)
     factor, inverse1 = factor_of(image - t_product(coupling, coupling))
-    coupling_ref[...] = coupling
+    rows = lax.broadcasted_iota(jnp.int32, (width, width), 0)
+    columns = lax.broadcasted_iota(jnp.int32, (width, width), 1)
+    coupling_ref[...] = coupling + (rows == columns).astype(jnp.float32)
     factor_ref[...] = factor
     after = product(inverse1, inverse0)
     before = -product(inverse1, t_product(coupling, inverse0))
@@ -187,7 +225,7 @@
         [
             jnp.concatenate([inverse0, none, none], axis=1),
             jnp.concatenate([before, after, none], axis=1),
-            jnp.concatenate([none, before, after], axis=1),
+            jnp.concatenate([before, before, after], axis=1),
         ],
         axis=0,
     )
@@ -224,7 +262,7 @@
         in_specs=specs or [VMEM] * len(args),
         out_specs=jax.tree.map(lambda _: VMEM, out),
         scratch_shapes=list(scratch),
-        compiler_params=pltpu.CompilerParams(vmem_limit_bytes=40 << 20),
+        compiler_params=pltpu.CompilerParams(vmem_limit_bytes=22 << 20),
         cost_estimate=cost,
         name=name,
     )(*args)
@@ -265,23 +303,25 @@
         )
 
     def applied(high, low):
-        groups = gather_panel(high)
+        pieces = gather_panel(high)
         kept, sent = backward(high, low)
-        terms = reduce_panels(kept, sent)
-        return [forward(groups)] + terms
+        kept, arrived = reduce_panels(kept, sent)
+        groups = spread_panels(pieces, arrived[1])
+        terms = finish_panels(kept, arrived)
+        return [forward(groups)] + terms, arrived[1]
 
     panel = shape((width, here), f32)
     half = shape((width, here), bf16)
     small = shape((width, width), f32)
     high, low = call(split_kernel, (half, half), start_panel, name="split")
-    terms = applied(high, low)
+    terms, _ = applied(high, low)
     first, high, low = call(combine_kernel, (panel, half, half), links, start_panel, *terms, name="combine")
-    gram = call(gram_kernel, shape((2 * width, 2 * width), f32), start_panel, first, name="gram")
+    terms, token = applied(high, low)
+    gram = call(gram_kernel, shape((2 * width, 2 * width), f32), start_panel, first, token, name="gram", specs=[VMEM, VMEM, ANY])
     gram = reduce_small(gram)
     coupling1, factor1, mix = call(
-        first_coefficients_kernel, (small, small, shape((3 * width, 3 * width), f32)), gram, name="coefficients"
-    )
-    terms = applied(high, low)
+        first_coefficients_kernel, (small, small, shape((3 * width, 3 * width), f32)), gram, terms[0], name="coefficients", specs=[VMEM, ANY]
+    )
     basis, gram = call(
         basis_kernel, (shape((3 * width, here), f32), shape((3 * width, width), f32)), mix, start_panel, first, links, *terms, name="basis"
     )

time: 192 us -> 134 us (0.70)
  waiting for transfers between devices: 97 us -> 50 us
  Pallas kernels: 47.5 us -> 31.9 us
  local copies, waits for them, and re-layouts: 3.55 us -> 8.21 us
    ppermute x32 -> x40, waiting for transfers between devices: 91.7 us -> 44.7 us  [swap(): lax.ppermute(array, 'rows', [(place, place ^ offset) for place in range(c...]
    pallas_call x10 -> x16, Pallas kernels: 47.5 us -> 31.9 us  [call(): pl.pallas_call(kernel, out_shape=out, in_specs=specs or [VMEM] * len(args...]
    unnamed x18 -> x22, local copies, waits for them, and re-layouts: 2.94 us -> 7.52 us
    ppermute x32 -> x40, starting transfers between devices: 32.9 us -> 34.1 us  [swap(): lax.ppermute(array, 'rows', [(place, place ^ offset) for place in range(c...]
  transfers between devices with their start and end apart: 33 -> 41, of which waited for: 23 -> 22; matrix products, arithmetic and copies ran while one was open for 0% -> 0% of each run, Pallas kernels for 13% -> 13%
where the time goes in v2:
time: 134 us
  waiting for transfers between devices  50 us (37%)
  starting transfers between devices  41.5 us (31%)
  Pallas kernels  31.9 us (24%)
  local copies, waits for them, and re-layouts  8.21 us (6%)
  other arithmetic  1.54 us (1%)
    ppermute x40, waiting for transfers between devices, swap(): lax.ppermute(array, 'rows', [(place, place ^ offset) for place in range(c...  44.7 us
    ppermute x40, starting transfers between devices, swap(): lax.ppermute(array, 'rows', [(place, place ^ offset) for place in range(c...  34.1 us
    pallas_call x16, Pallas kernels, call(): pl.pallas_call(kernel, out_shape=out, in_specs=specs or [VMEM] * len(args...  31.9 us
    unnamed x22, local copies, waits for them, and re-layouts  7.52 us
    all_to_all x1, starting transfers between devices, on_device(): lax.all_to_all(send_list[0], 'rows', split_axis=0, concat_axis=0, tiled=T...  7.37 us
    all_to_all x1, waiting for transfers between devices, on_device(): lax.all_to_all(send_list[0], 'rows', split_axis=0, concat_axis=0, tiled=T...  5.33 us
  transfers between devices with their start and end apart: 41, of which 22 were waited for; matrix products, arithmetic and copies ran while one was open for 0% of the time, Pallas kernels for 13%

profile of v2, /device:TPU:0, one launch (start us, length us, event | category | flops | bytes accessed | tf_op | source)
XLA Modules:
  0.0 134.1 jit_solution(914857289864914106)
XLA Ops:
  0.6 7.4 %all-to-all-start = ((s32[16,1,16]{2,1,0:T(1,128)}), s32[16,1,16]{2,1,0:T(1,128)S(1)}, u32[]{:S(2)}, u32[]{:S(2)}) async-start(s32[16,1,16]{2,1,0:T(1,128)} %bitcast.33), calls=%async_computation | async-start | bytes 16384 | tf_op jit(solution)/shard_map/all_to_all | solution.py:281
  9.0 5.3 %all-to-all-done = s32[16,1,16]{2,1,0:T(1,128)S(1)} async-done(((s32[16,1,16]{2,1,0:T(1,128)}), s32[16,1,16]{2,1,0:T(1,128)S(1)}, u32[]{:S(2)}, u32[]{:S(2)}) %all-to-all-start) | async-done | bytes 1056 | tf_op jit(solution)/shard_map/all_to_all | solution.py:281
  15.6 4.6 %copy-done = bf16[96,256,256]{2,1,0:T(8,128)(2,1)S(1)} copy-done((bf16[96,256,256]{2,1,0:T(8,128)(2,1)S(1)}, bf16[96,256,256]{2,1,0:T(8,128)(2,1)}, u32[]{:S(2)}) %copy-start) | copy-done | bytes 12582936
  22.2 4.1 %backward.2 = (f32[8,32,2048]{2,1,0:T(8,128)S(1)}, bf16[8,32,2048]{2,1,0:T(8,128)(2,1)S(1)}) custom-call(s32[1]{0:T(128)} %bitcast.1.me_ref, s32[96]{0:T(128)S(1)} %copy-done.5, s32[96]{0:T(128)S(1)} %copy-done.7, s32[256]{0:T(256)S(1)} %reshape.35.list_ref, s32[16]{0:T(128)S(1)} %copy-done.9, bf16[32,2048]{1,0:T(8,128)(2,1)S(1)} %get-tuple-element.24.high_ref.refs_0_, ...), custom_call_target="tpu_custom_call" | custom-call | flops 1610612736 | bytes 12582912 | tf_op jit(solution)/shard_map/backward/pallas_call | solution.py:259
  26.3 2.6 %collective-permute-done.1.arrived_ref = bf16[8,32,2048]{2,1,0:T(8,128)(2,1)S(1)} collective-permute-done((bf16[8,32,2048]{2,1,0:T(8,128)(2,1)S(1)}, bf16[8,32,2048]{2,1,0:T(8,128)(2,1)S(1)}, u32[]{:S(2)}, u32[]{:S(2)}) %collective-permute-start.1) | collective-permute-done | bytes 1048608 | tf_op jit(solution)/shard_map/ppermute | solution.py:33
  32.5 3.3 %collective-permute-start.4 = (bf16[32,2048]{1,0:T(8,128)(2,1)S(1)}, bf16[32,2048]{1,0:T(8,128)(2,1)S(1)}, u32[]{:S(2)}, u32[]{:S(2)}) collective-permute-start(bf16[32,2048]{1,0:T(8,128)(2,1)S(1)} %get-tuple-element.24.high_ref.refs_0_), channel_id=1, source_target_pairs={{0,12},{1,13},{2,14},{3,15},{4,8},{5,9},{6,10},{7,11},{8,4},{9,5},... | collective-permute-start | bytes 393224 | tf_op jit(solution)/shard_map/ppermute | solution.py:33
  35.7 2.1 %collective-permute-done.refs_1_ = bf16[32,2048]{1,0:T(8,128)(2,1)S(1)} collective-permute-done((bf16[32,2048]{1,0:T(8,128)(2,1)S(1)}, bf16[32,2048]{1,0:T(8,128)(2,1)S(1)}, u32[]{:S(2)}, u32[]{:S(2)}) %collective-permute-start) | collective-permute-done | bytes 131104 | tf_op jit(solution)/shard_map/ppermute | solution.py:33
  39.0 5.4 %collective-permute-done.3.refs_0_ = bf16[32,2048]{1,0:T(8,128)(2,1)S(1)} collective-permute-done((bf16[32,2048]{1,0:T(8,128)(2,1)S(1)}, bf16[32,2048]{1,0:T(8,128)(2,1)S(1)}, u32[]{:S(2)}, u32[]{:S(2)}) %collective-permute-start.3) | collective-permute-done | bytes 131104 | tf_op jit(solution)/shard_map/ppermute | solution.py:33
  45.1 1.7 %collective-permute-start.12 = (bf16[32,2048]{1,0:T(8,128)(2,1)S(1)}, bf16[32,2048]{1,0:T(8,128)(2,1)S(1)}, u32[]{:S(2)}, u32[]{:S(2)}) collective-permute-start(bf16[32,2048]{1,0:T(8,128)(2,1)S(1)} %get-tuple-element.48), channel_id=1, source_target_pairs={{0,12},{1,13},{2,14},{3,15},{4,8},{5,9},{6,10},{7,11},{8,4},{9,5},... | collective-permute-start | bytes 393224 | tf_op jit(solution)/shard_map/ppermute | solution.py:33
  46.8 2.9 %collective-permute-done.5.refs_2_ = bf16[2,32,2048]{2,1,0:T(8,128)(2,1)S(1)} collective-permute-done((bf16[2,32,2048]{2,1,0:T(8,128)(2,1)S(1)}, bf16[2,32,2048]{2,1,0:T(8,128)(2,1)S(1)}, u32[]{:S(2)}, u32[]{:S(2)}) %collective-permute-start.5) | collective-permute-done | bytes 262176 | tf_op jit(solution)/shard_map/ppermute | solution.py:33
  49.7 4.8 %collective-permute-done.6.refs_3_ = bf16[2,32,2048]{2,1,0:T(8,128)(2,1)S(1)} collective-permute-done((bf16[2,32,2048]{2,1,0:T(8,128)(2,1)S(1)}, bf16[2,32,2048]{2,1,0:T(8,128)(2,1)S(1)}, u32[]{:S(2)}, u32[]{:S(2)}) %collective-permute-start.6) | collective-permute-done | bytes 262176 | tf_op jit(solution)/shard_map/ppermute | solution.py:33
  56.0 5.2 %forward.2.forward_ref = f32[32,2048]{1,0:T(8,128)S(1)} custom-call(s32[1]{0:T(128)} %bitcast.1.me_ref, s32[96]{0:T(128)S(1)} %copy-done.6, s32[96]{0:T(128)S(1)} %copy-done.8, s32[256]{0:T(256)S(1)} %reshape.35.list_ref, s32[16]{0:T(128)S(1)} %copy-done.10, bf16[96,256,256]{2,1,0:T(8,128)(2,1)S(1)} %copy-done.1, bf16[2,32,2048]{2,1,0:T(8,128)(2,1)S(1)} %stacked.4.refs_0_, ...), custom_call_target="tpu_custom_call" | custom-call | flops 1610612736 | bytes 12582912 | tf_op jit(solution)/shard_map/forward/pallas_call | solution.py:259
  61.2 2.9 %collective-permute-done.13.refs_3_ = bf16[32,2048]{1,0:T(8,128)(2,1)S(1)} collective-permute-done((bf16[32,2048]{1,0:T(8,128)(2,1)S(1)}, bf16[32,2048]{1,0:T(8,128)(2,1)S(1)}, u32[]{:S(2)}, u32[]{:S(2)}) %collective-permute-start.13) | collective-permute-done | bytes 131104 | tf_op jit(solution)/shard_map/ppermute | solution.py:33
  64.3 4.1 %backward.3 = (f32[8,32,2048]{2,1,0:T(8,128)S(1)}, bf16[8,32,2048]{2,1,0:T(8,128)(2,1)S(1)}) custom-call(s32[1]{0:T(128)} %bitcast.1.me_ref, s32[96]{0:T(128)S(1)} %copy-done.6, s32[96]{0:T(128)S(1)} %copy-done.8, s32[256]{0:T(256)S(1)} %reshape.35.list_ref, s32[16]{0:T(128)S(1)} %copy-done.10, bf16[32,2048]{1,0:T(8,128)(2,1)S(1)} %get-tuple-element.31.high_ref.refs_0_, ...), custom_call_target="tpu_custom_call" | custom-call | flops 1610612736 | bytes 12582912 | tf_op jit(solution)/shard_map/backward/pallas_call | solution.py:259
  68.6 2.6 %collective-permute-done.15.arrived_ref = bf16[8,32,2048]{2,1,0:T(8,128)(2,1)S(1)} collective-permute-done((bf16[8,32,2048]{2,1,0:T(8,128)(2,1)S(1)}, bf16[8,32,2048]{2,1,0:T(8,128)(2,1)S(1)}, u32[]{:S(2)}, u32[]{:S(2)}) %collective-permute-start.15) | collective-permute-done | bytes 1048608 | tf_op jit(solution)/shard_map/ppermute | solution.py:33
  74.8 3.1 %collective-permute-start.24 = (bf16[32,2048]{1,0:T(8,128)(2,1)S(1)}, bf16[32,2048]{1,0:T(8,128)(2,1)S(1)}, u32[]{:S(2)}, u32[]{:S(2)}) collective-permute-start(bf16[32,2048]{1,0:T(8,128)(2,1)S(1)} %get-tuple-element.31.high_ref.refs_0_), channel_id=1, source_target_pairs={{0,12},{1,13},{2,14},{3,15},{4,8},{5,9},{6,10},{7,11},{8,4},{9,5},... | collective-permute-start | bytes 393224 | tf_op jit(solution)/shard_map/ppermute | solution.py:33
  77.9 2.7 %collective-permute-done.16.token_ref.refs_2_ = bf16[2,32,2048]{2,1,0:T(8,128)(2,1)S(1)} collective-permute-done((bf16[2,32,2048]{2,1,0:T(8,128)(2,1)S(1)}, bf16[2,32,2048]{2,1,0:T(8,128)(2,1)S(1)}, u32[]{:S(2)}, u32[]{:S(2)}) %collective-permute-start.16) | collective-permute-done | bytes 262176 | tf_op jit(solution)/shard_map/ppermute | solution.py:33
  84.6 1.7 %collective-permute-done.23.refs_0_ = bf16[32,2048]{1,0:T(8,128)(2,1)S(1)} collective-permute-done((bf16[32,2048]{1,0:T(8,128)(2,1)S(1)}, bf16[32,2048]{1,0:T(8,128)(2,1)S(1)}, u32[]{:S(2)}, u32[]{:S(2)}) %collective-permute-start.23) | collective-permute-done | bytes 131104 | tf_op jit(solution)/shard_map/ppermute | solution.py:33
  87.0 2.5 %collective-permute-start.20 = (f32[64,64]{1,0:T(8,128)S(1)}, f32[64,64]{1,0:T(8,128)S(1)}, u32[]{:S(2)}, u32[]{:S(2)}) collective-permute-start(f32[64,64]{1,0:T(8,128)S(1)} %add.58), channel_id=1, source_target_pairs={{0,8},{1,9},{2,10},{3,11},{4,12},{5,13},{6,14},{7,15},{8,0},{9,1},... | collective-permute-start | bytes 49160 | tf_op jit(solution)/shard_map/ppermute | solution.py:33
  89.4 2.0 %collective-permute-start.21 = (f32[64,64]{1,0:T(8,128)S(1)}, f32[64,64]{1,0:T(8,128)S(1)}, u32[]{:S(2)}, u32[]{:S(2)}) collective-permute-start(f32[64,64]{1,0:T(8,128)S(1)} %add.58), channel_id=1, source_target_pairs={{0,12},{1,13},{2,14},{3,15},{4,8},{5,9},{6,10},{7,11},{8,4},{9,5},... | collective-permute-start | bytes 49160 | tf_op jit(solution)/shard_map/ppermute | solution.py:33
  92.5 2.6 %collective-permute-done.21 = f32[64,64]{1,0:T(8,128)S(1)} collective-permute-done((f32[64,64]{1,0:T(8,128)S(1)}, f32[64,64]{1,0:T(8,128)S(1)}, u32[]{:S(2)}, u32[]{:S(2)}) %collective-permute-start.21) | collective-permute-done | bytes 16416 | tf_op jit(solution)/shard_map/ppermute | solution.py:33
  95.2 2.2 %collective-permute-done.26.refs_3_ = bf16[2,32,2048]{2,1,0:T(8,128)(2,1)S(1)} collective-permute-done((bf16[2,32,2048]{2,1,0:T(8,128)(2,1)S(1)}, bf16[2,32,2048]{2,1,0:T(8,128)(2,1)S(1)}, u32[]{:S(2)}, u32[]{:S(2)}) %collective-permute-start.26) | collective-permute-done | bytes 262176 | tf_op jit(solution)/shard_map/ppermute | solution.py:33
  97.4 1.7 %collective-permute-done.19 = f32[64,64]{1,0:T(8,128)S(1)} collective-permute-done((f32[64,64]{1,0:T(8,128)S(1)}, f32[64,64]{1,0:T(8,128)S(1)}, u32[]{:S(2)}, u32[]{:S(2)}) %collective-permute-start.19) | collective-permute-done | bytes 16416 | tf_op jit(solution)/shard_map/ppermute | solution.py:33
  99.1 2.0 %collective-permute-start.32 = (bf16[32,2048]{1,0:T(8,128)(2,1)S(1)}, bf16[32,2048]{1,0:T(8,128)(2,1)S(1)}, u32[]{:S(2)}, u32[]{:S(2)}) collective-permute-start(bf16[32,2048]{1,0:T(8,128)(2,1)S(1)} %get-tuple-element.46), channel_id=1, source_target_pairs={{0,12},{1,13},{2,14},{3,15},{4,8},{5,9},{6,10},{7,11},{8,4},{9,5},... | collective-permute-start | bytes 393224 | tf_op jit(solution)/shard_map/ppermute | solution.py:33
  101.2 2.3 %collective-permute-start.34 = (bf16[32,2048]{1,0:T(8,128)(2,1)S(1)}, bf16[32,2048]{1,0:T(8,128)(2,1)S(1)}, u32[]{:S(2)}, u32[]{:S(2)}) collective-permute-start(bf16[32,2048]{1,0:T(8,128)(2,1)S(1)} %get-tuple-element.49), channel_id=1, source_target_pairs={{0,4},{1,5},{2,6},{3,7},{4,0},{5,1},{6,2},{7,3},{8,12},{9,13},{10,... | collective-permute-start | bytes 393224 | tf_op jit(solution)/shard_map/ppermute | solution.py:33
  103.6 5.2 %forward.3.token_ref.forward_ref = f32[32,2048]{1,0:T(8,128)S(1)} custom-call(s32[1]{0:T(128)} %bitcast.1.me_ref, s32[96]{0:T(128)S(1)} %copy-done.6, s32[96]{0:T(128)S(1)} %copy-done.8, s32[256]{0:T(256)S(1)} %reshape.35.list_ref, s32[16]{0:T(128)S(1)} %copy-done.10, bf16[96,256,256]{2,1,0:T(8,128)(2,1)S(1)} %copy-done.1, ...), custom_call_target="tpu_custom_call" | custom-call | flops 1610612736 | bytes 12582912 | tf_op jit(solution)/shard_map/forward/pallas_call | solution.py:259
  108.7 6.2 %coefficients.1 = (f32[32,32]{1,0:T(8,128)S(1)}, f32[32,32]{1,0:T(8,128)S(1)}, f32[96,96]{1,0:T(8,128)S(1)}) custom-call(f32[64,64]{1,0:T(8,128)S(1)} %add_add_fusion.1.gram_ref, f32[32,2048]{1,0:T(8,128)S(1)} %forward.3.token_ref.forward_ref), custom_call_target="tpu_custom_call" | custom-call | tf_op jit(solution)/shard_map/coefficients/pallas_call | solution.py:259
  115.0 1.6 %basis.1 = (f32[96,2048]{1,0:T(8,128)S(1)}, f32[96,32]{1,0:T(8,128)S(1)}) custom-call(f32[96,96]{1,0:T(8,128)S(1)} %get-tuple-element.36.mix_ref, f32[32,2048]{1,0:T(8,128)S(1)} %copy-done.3, f32[32,2048]{1,0:T(8,128)S(1)} %get-tuple-element.30.right_ref.first_ref, f32[1,2048]{1,0:T(1,128)S(1)} %bitcast.29, f32[32,2048]{1,0:T(8,128)S(1)} %forward.3.token_ref.forward_ref, ...), custom_call_target="tpu_custom_call" | custom-call | tf_op jit(solution)/shard_map/basis/pallas_call | solution.py:259
  119.4 2.6 %collective-permute-done.36 = f32[96,32]{1,0:T(8,128)S(1)} collective-permute-done((f32[96,32]{1,0:T(8,128)S(1)}, f32[96,32]{1,0:T(8,128)S(1)}, u32[]{:S(2)}, u32[]{:S(2)}) %collective-permute-start.36) | collective-permute-done | bytes 12320 | tf_op jit(solution)/shard_map/ppermute | solution.py:33
  122.8 1.8 %collective-permute-start.39 = (f32[96,32]{1,0:T(8,128)S(1)}, f32[96,32]{1,0:T(8,128)S(1)}, u32[]{:S(2)}, u32[]{:S(2)}) collective-permute-start(f32[96,32]{1,0:T(8,128)S(1)} %add.66), channel_id=1, source_target_pairs={{0,12},{1,13},{2,14},{3,15},{4,8},{5,9},{6,10},{7,11},{8,4},{9,5},... | collective-permute-start | bytes 36872 | tf_op jit(solution)/shard_map/ppermute | solution.py:33
  125.6 1.9 %collective-permute-done.38 = f32[96,32]{1,0:T(8,128)S(1)} collective-permute-done((f32[96,32]{1,0:T(8,128)S(1)}, f32[96,32]{1,0:T(8,128)S(1)}, u32[]{:S(2)}, u32[]{:S(2)}) %collective-permute-start.38) | collective-permute-done | bytes 12320 | tf_op jit(solution)/shard_map/ppermute | solution.py:33
  129.2 4.3 %last.1 = (f32[32,2048]{1,0:T(8,128)}, f32[32,32]{1,0:T(8,128)S(1)}, f32[32,32]{1,0:T(8,128)S(1)}) custom-call(f32[96,32]{1,0:T(8,128)S(1)} %add_add_fusion.gram_ref, f32[32,32]{1,0:T(8,128)S(1)} %get-tuple-element.39.factor_ref, f32[96,2048]{1,0:T(8,128)S(1)} %get-tuple-element.40.basis_ref), custom_call_target="tpu_custom_call" | custom-call | tf_op jit(solution)/shard_map/last/pallas_call | solution.py:259
  (104 shorter events, 27.7 us)
Async XLA Ops:
  0.6 13.7 %all-to-all-start = ((s32[16,1,16]{2,1,0:T(1,128)}), s32[16,1,16]{2,1,0:T(1,128)S(1)}, u32[]{:S(2)}, u32[]{:S(2)}) async-start(s32[16,1,16]{2,1,0:T(1,128)} %bitcast.33), calls=%async_computation | async-start | bytes 16384 | tf_op jit(solution)/shard_map/all_to_all | solution.py:281
  29.2 9.2 %collective-permute-start.2 = (bf16[2,32,2048]{2,1,0:T(8,128)(2,1)S(1)}, bf16[2,32,2048]{2,1,0:T(8,128)(2,1)S(1)}, u32[]{:S(2)}, u32[]{:S(2)}) collective-permute-start(bf16[2,32,2048]{2,1,0:T(8,128)(2,1)S(1)} %get-tuple-element.56), channel_id=1, source_target_pairs={{0,2},{1,3},{2,0},{3,1},{4,6},{5,7},{6,4},{7,5},{8,10},{9,11},{10,... | collective-permute-start | bytes 786440 | tf_op jit(solution)/shard_map/ppermute | solution.py:33
  29.8 15.2 %collective-permute-start.11 = (bf16[2,32,2048]{2,1,0:T(8,128)(2,1)S(1)}, bf16[2,32,2048]{2,1,0:T(8,128)(2,1)S(1)}, u32[]{:S(2)}, u32[]{:S(2)}) collective-permute-start(bf16[2,32,2048]{2,1,0:T(8,128)(2,1)S(1)} %get-tuple-element.55), channel_id=1, source_target_pairs={{0,2},{1,3},{2,0},{3,1},{4,6},{5,7},{6,4},{7,5},{8,10},{9,11},{10,... | collective-permute-start | bytes 786440 | tf_op jit(solution)/shard_map/ppermute | solution.py:33
  31.3 6.5 %collective-permute-start = (bf16[32,2048]{1,0:T(8,128)(2,1)S(1)}, bf16[32,2048]{1,0:T(8,128)(2,1)S(1)}, u32[]{:S(2)}, u32[]{:S(2)}) collective-permute-start(bf16[32,2048]{1,0:T(8,128)(2,1)S(1)} %get-tuple-element.24.high_ref.refs_0_), channel_id=1, source_target_pairs={{0,4},{1,5},{2,6},{3,7},{4,0},{5,1},{6,2},{7,3},{8,12},{9,13},{10,... | collective-permute-start | bytes 393224 | tf_op jit(solution)/shard_map/ppermute | solution.py:33
  31.8 12.6 %collective-permute-start.3 = (bf16[32,2048]{1,0:T(8,128)(2,1)S(1)}, bf16[32,2048]{1,0:T(8,128)(2,1)S(1)}, u32[]{:S(2)}, u32[]{:S(2)}) collective-permute-start(bf16[32,2048]{1,0:T(8,128)(2,1)S(1)} %get-tuple-element.24.high_ref.refs_0_), channel_id=1, source_target_pairs={{0,8},{1,9},{2,10},{3,11},{4,12},{5,13},{6,14},{7,15},{8,0},{9,1},... | collective-permute-start | bytes 393224 | tf_op jit(solution)/shard_map/ppermute | solution.py:33
  32.5 12.0 %collective-permute-start.4 = (bf16[32,2048]{1,0:T(8,128)(2,1)S(1)}, bf16[32,2048]{1,0:T(8,128)(2,1)S(1)}, u32[]{:S(2)}, u32[]{:S(2)}) collective-permute-start(bf16[32,2048]{1,0:T(8,128)(2,1)S(1)} %get-tuple-element.24.high_ref.refs_0_), channel_id=1, source_target_pairs={{0,12},{1,13},{2,14},{3,15},{4,8},{5,9},{6,10},{7,11},{8,4},{9,5},... | collective-permute-start | bytes 393224 | tf_op jit(solution)/shard_map/ppermute | solution.py:33
  38.5 11.2 %collective-permute-start.5 = (bf16[2,32,2048]{2,1,0:T(8,128)(2,1)S(1)}, bf16[2,32,2048]{2,1,0:T(8,128)(2,1)S(1)}, u32[]{:S(2)}, u32[]{:S(2)}) collective-permute-start(bf16[2,32,2048]{2,1,0:T(8,128)(2,1)S(1)} %stacked.4.refs_0_), channel_id=1, source_target_pairs={{0,2},{1,3},{2,0},{3,1},{4,6},{5,7},{6,4},{7,5},{8,10},{9,11},{10,... | collective-permute-start | bytes 786440 | tf_op jit(solution)/shard_map/ppermute | solution.py:33
  39.0 15.5 %collective-permute-start.7 = (bf16[2,32,2048]{2,1,0:T(8,128)(2,1)S(1)}, bf16[2,32,2048]{2,1,0:T(8,128)(2,1)S(1)}, u32[]{:S(2)}, u32[]{:S(2)}) collective-permute-start(bf16[2,32,2048]{2,1,0:T(8,128)(2,1)S(1)} %stacked.4.refs_0_), channel_id=1, source_target_pairs={{0,1},{1,0},{2,3},{3,2},{4,5},{5,4},{6,7},{7,6},{8,9},{9,8},{10,11... | collective-permute-start | bytes 786440 | tf_op jit(solution)/shard_map/ppermute | solution.py:33
  44.4 10.1 %collective-permute-start.6 = (bf16[2,32,2048]{2,1,0:T(8,128)(2,1)S(1)}, bf16[2,32,2048]{2,1,0:T(8,128)(2,1)S(1)}, u32[]{:S(2)}, u32[]{:S(2)}) collective-permute-start(bf16[2,32,2048]{2,1,0:T(8,128)(2,1)S(1)} %stacked.5.refs_1_), channel_id=1, source_target_pairs={{0,2},{1,3},{2,0},{3,1},{4,6},{5,7},{6,4},{7,5},{8,10},{9,11},{10,... | collective-permute-start | bytes 786440 | tf_op jit(solution)/shard_map/ppermute | solution.py:33
  45.0 10.1 %collective-permute-start.8 = (bf16[2,32,2048]{2,1,0:T(8,128)(2,1)S(1)}, bf16[2,32,2048]{2,1,0:T(8,128)(2,1)S(1)}, u32[]{:S(2)}, u32[]{:S(2)}) collective-permute-start(bf16[2,32,2048]{2,1,0:T(8,128)(2,1)S(1)} %stacked.5.refs_1_), channel_id=1, source_target_pairs={{0,1},{1,0},{2,3},{3,2},{4,5},{5,4},{6,7},{7,6},{8,9},{9,8},{10,11... | collective-permute-start | bytes 786440 | tf_op jit(solution)/shard_map/ppermute | solution.py:33
  45.1 16.1 %collective-permute-start.12 = (bf16[32,2048]{1,0:T(8,128)(2,1)S(1)}, bf16[32,2048]{1,0:T(8,128)(2,1)S(1)}, u32[]{:S(2)}, u32[]{:S(2)}) collective-permute-start(bf16[32,2048]{1,0:T(8,128)(2,1)S(1)} %get-tuple-element.48), channel_id=1, source_target_pairs={{0,12},{1,13},{2,14},{3,15},{4,8},{5,9},{6,10},{7,11},{8,4},{9,5},... | collective-permute-start | bytes 393224 | tf_op jit(solution)/shard_map/ppermute | solution.py:33
  49.7 6.0 %collective-permute-start.9 = (bf16[2,32,2048]{2,1,0:T(8,128)(2,1)S(1)}, bf16[2,32,2048]{2,1,0:T(8,128)(2,1)S(1)}, u32[]{:S(2)}, u32[]{:S(2)}) collective-permute-start(bf16[2,32,2048]{2,1,0:T(8,128)(2,1)S(1)} %collective-permute-done.5.refs_2_), channel_id=1, source_target_pairs={{0,1},{1,0},{2,3},{3,2},{4,5},{5,4},{6,7},{7,6},{8,9},{9,8},{10,11... | collective-permute-start | bytes 786440 | tf_op jit(solution)/shard_map/ppermute | solution.py:33
  54.5 9.6 %collective-permute-start.13 = (bf16[32,2048]{1,0:T(8,128)(2,1)S(1)}, bf16[32,2048]{1,0:T(8,128)(2,1)S(1)}, u32[]{:S(2)}, u32[]{:S(2)}) collective-permute-start(bf16[32,2048]{1,0:T(8,128)(2,1)S(1)} %get-tuple-element.47), channel_id=1, source_target_pairs={{0,8},{1,9},{2,10},{3,11},{4,12},{5,13},{6,14},{7,15},{8,0},{9,1},... | collective-permute-start | bytes 393224 | tf_op jit(solution)/shard_map/ppermute | solution.py:33
  55.1 9.0 %collective-permute-start.14 = (bf16[32,2048]{1,0:T(8,128)(2,1)S(1)}, bf16[32,2048]{1,0:T(8,128)(2,1)S(1)}, u32[]{:S(2)}, u32[]{:S(2)}) collective-permute-start(bf16[32,2048]{1,0:T(8,128)(2,1)S(1)} %get-tuple-element.51), channel_id=1, source_target_pairs={{0,4},{1,5},{2,6},{3,7},{4,0},{5,1},{6,2},{7,3},{8,12},{9,13},{10,... | collective-permute-start | bytes 393224 | tf_op jit(solution)/shard_map/ppermute | solution.py:33
  71.4 9.2 %collective-permute-start.16 = (bf16[2,32,2048]{2,1,0:T(8,128)(2,1)S(1)}, bf16[2,32,2048]{2,1,0:T(8,128)(2,1)S(1)}, u32[]{:S(2)}, u32[]{:S(2)}) collective-permute-start(bf16[2,32,2048]{2,1,0:T(8,128)(2,1)S(1)} %get-tuple-element.54), channel_id=1, source_target_pairs={{0,2},{1,3},{2,0},{3,1},{4,6},{5,7},{6,4},{7,5},{8,10},{9,11},{10,... | collective-permute-start | bytes 786440 | tf_op jit(solution)/shard_map/ppermute | solution.py:33
  72.0 17.4 %collective-permute-start.31 = (bf16[2,32,2048]{2,1,0:T(8,128)(2,1)S(1)}, bf16[2,32,2048]{2,1,0:T(8,128)(2,1)S(1)}, u32[]{:S(2)}, u32[]{:S(2)}) collective-permute-start(bf16[2,32,2048]{2,1,0:T(8,128)(2,1)S(1)} %get-tuple-element.53), channel_id=1, source_target_pairs={{0,2},{1,3},{2,0},{3,1},{4,6},{5,7},{6,4},{7,5},{8,10},{9,11},{10,... | collective-permute-start | bytes 786440 | tf_op jit(solution)/shard_map/ppermute | solution.py:33
  73.5 9.5 %collective-permute-start.22 = (bf16[32,2048]{1,0:T(8,128)(2,1)S(1)}, bf16[32,2048]{1,0:T(8,128)(2,1)S(1)}, u32[]{:S(2)}, u32[]{:S(2)}) collective-permute-start(bf16[32,2048]{1,0:T(8,128)(2,1)S(1)} %get-tuple-element.31.high_ref.refs_0_), channel_id=1, source_target_pairs={{0,4},{1,5},{2,6},{3,7},{4,0},{5,1},{6,2},{7,3},{8,12},{9,13},{10,... | collective-permute-start | bytes 393224 | tf_op jit(solution)/shard_map/ppermute | solution.py:33
  73.5 12.8 %collective-permute-start.23 = (bf16[32,2048]{1,0:T(8,128)(2,1)S(1)}, bf16[32,2048]{1,0:T(8,128)(2,1)S(1)}, u32[]{:S(2)}, u32[]{:S(2)}) collective-permute-start(bf16[32,2048]{1,0:T(8,128)(2,1)S(1)} %get-tuple-element.31.high_ref.refs_0_), channel_id=1, source_target_pairs={{0,8},{1,9},{2,10},{3,11},{4,12},{5,13},{6,14},{7,15},{8,0},{9,1},... | collective-permute-start | bytes 393224 | tf_op jit(solution)/shard_map/ppermute | solution.py:33
  74.8 11.5 %collective-permute-start.24 = (bf16[32,2048]{1,0:T(8,128)(2,1)S(1)}, bf16[32,2048]{1,0:T(8,128)(2,1)S(1)}, u32[]{:S(2)}, u32[]{:S(2)}) collective-permute-start(bf16[32,2048]{1,0:T(8,128)(2,1)S(1)} %get-tuple-element.31.high_ref.refs_0_), channel_id=1, source_target_pairs={{0,12},{1,13},{2,14},{3,15},{4,8},{5,9},{6,10},{7,11},{8,4},{9,5},... | collective-permute-start | bytes 393224 | tf_op jit(solution)/shard_map/ppermute | solution.py:33
  83.0 12.1 %collective-permute-start.25 = (bf16[2,32,2048]{2,1,0:T(8,128)(2,1)S(1)}, bf16[2,32,2048]{2,1,0:T(8,128)(2,1)S(1)}, u32[]{:S(2)}, u32[]{:S(2)}) collective-permute-start(bf16[2,32,2048]{2,1,0:T(8,128)(2,1)S(1)} %stacked.6.refs_0_), channel_id=1, source_target_pairs={{0,2},{1,3},{2,0},{3,1},{4,6},{5,7},{6,4},{7,5},{8,10},{9,11},{10,... | collective-permute-start | bytes 786440 | tf_op jit(solution)/shard_map/ppermute | solution.py:33
  86.3 14.8 %collective-permute-start.27 = (bf16[2,32,2048]{2,1,0:T(8,128)(2,1)S(1)}, bf16[2,32,2048]{2,1,0:T(8,128)(2,1)S(1)}, u32[]{:S(2)}, u32[]{:S(2)}) collective-permute-start(bf16[2,32,2048]{2,1,0:T(8,128)(2,1)S(1)} %stacked.6.refs_0_), channel_id=1, source_target_pairs={{0,1},{1,0},{2,3},{3,2},{4,5},{5,4},{6,7},{7,6},{8,9},{9,8},{10,11... | collective-permute-start | bytes 786440 | tf_op jit(solution)/shard_map/ppermute | solution.py:33
  86.3 11.0 %collective-permute-start.26 = (bf16[2,32,2048]{2,1,0:T(8,128)(2,1)S(1)}, bf16[2,32,2048]{2,1,0:T(8,128)(2,1)S(1)}, u32[]{:S(2)}, u32[]{:S(2)}) collective-permute-start(bf16[2,32,2048]{2,1,0:T(8,128)(2,1)S(1)} %stacked.7.refs_1_), channel_id=1, source_target_pairs={{0,2},{1,3},{2,0},{3,1},{4,6},{5,7},{6,4},{7,5},{8,10},{9,11},{10,... | collective-permute-start | bytes 786440 | tf_op jit(solution)/shard_map/ppermute | solution.py:33
  87.0 5.5 %collective-permute-start.20 = (f32[64,64]{1,0:T(8,128)S(1)}, f32[64,64]{1,0:T(8,128)S(1)}, u32[]{:S(2)}, u32[]{:S(2)}) collective-permute-start(f32[64,64]{1,0:T(8,128)S(1)} %add.58), channel_id=1, source_target_pairs={{0,8},{1,9},{2,10},{3,11},{4,12},{5,13},{6,14},{7,15},{8,0},{9,1},... | collective-permute-start | bytes 49160 | tf_op jit(solution)/shard_map/ppermute | solution.py:33
  89.4 5.7 %collective-permute-start.21 = (f32[64,64]{1,0:T(8,128)S(1)}, f32[64,64]{1,0:T(8,128)S(1)}, u32[]{:S(2)}, u32[]{:S(2)}) collective-permute-start(f32[64,64]{1,0:T(8,128)S(1)} %add.58), channel_id=1, source_target_pairs={{0,12},{1,13},{2,14},{3,15},{4,8},{5,9},{6,10},{7,11},{8,4},{9,5},... | collective-permute-start | bytes 49160 | tf_op jit(solution)/shard_map/ppermute | solution.py:33
  92.5 8.7 %collective-permute-start.28 = (bf16[2,32,2048]{2,1,0:T(8,128)(2,1)S(1)}, bf16[2,32,2048]{2,1,0:T(8,128)(2,1)S(1)}, u32[]{:S(2)}, u32[]{:S(2)}) collective-permute-start(bf16[2,32,2048]{2,1,0:T(8,128)(2,1)S(1)} %stacked.7.refs_1_), channel_id=1, source_target_pairs={{0,1},{1,0},{2,3},{3,2},{4,5},{5,4},{6,7},{7,6},{8,9},{9,8},{10,11... | collective-permute-start | bytes 786440 | tf_op jit(solution)/shard_map/ppermute | solution.py:33
  95.2 8.4 %collective-permute-start.29 = (bf16[2,32,2048]{2,1,0:T(8,128)(2,1)S(1)}, bf16[2,32,2048]{2,1,0:T(8,128)(2,1)S(1)}, u32[]{:S(2)}, u32[]{:S(2)}) collective-permute-start(bf16[2,32,2048]{2,1,0:T(8,128)(2,1)S(1)} %collective-permute-done.25.refs_2_), channel_id=1, source_target_pairs={{0,1},{1,0},{2,3},{3,2},{4,5},{5,4},{6,7},{7,6},{8,9},{9,8},{10,11... | collective-permute-start | bytes 786440 | tf_op jit(solution)/shard_map/ppermute | solution.py:33
  97.4 6.2 %collective-permute-start.30 = (bf16[2,32,2048]{2,1,0:T(8,128)(2,1)S(1)}, bf16[2,32,2048]{2,1,0:T(8,128)(2,1)S(1)}, u32[]{:S(2)}, u32[]{:S(2)}) collective-permute-start(bf16[2,32,2048]{2,1,0:T(8,128)(2,1)S(1)} %collective-permute-done.26.refs_3_), channel_id=1, source_target_pairs={{0,1},{1,0},{2,3},{3,2},{4,5},{5,4},{6,7},{7,6},{8,9},{9,8},{10,11... | collective-permute-start | bytes 786440 | tf_op jit(solution)/shard_map/ppermute | solution.py:33
  99.1 15.9 %collective-permute-start.32 = (bf16[32,2048]{1,0:T(8,128)(2,1)S(1)}, bf16[32,2048]{1,0:T(8,128)(2,1)S(1)}, u32[]{:S(2)}, u32[]{:S(2)}) collective-permute-start(bf16[32,2048]{1,0:T(8,128)(2,1)S(1)} %get-tuple-element.46), channel_id=1, source_target_pairs={{0,12},{1,13},{2,14},{3,15},{4,8},{5,9},{6,10},{7,11},{8,4},{9,5},... | collective-permute-start | bytes 393224 | tf_op jit(solution)/shard_map/ppermute | solution.py:33
  101.1 13.8 %collective-permute-start.33 = (bf16[32,2048]{1,0:T(8,128)(2,1)S(1)}, bf16[32,2048]{1,0:T(8,128)(2,1)S(1)}, u32[]{:S(2)}, u32[]{:S(2)}) collective-permute-start(bf16[32,2048]{1,0:T(8,128)(2,1)S(1)} %get-tuple-element.45), channel_id=1, source_target_pairs={{0,8},{1,9},{2,10},{3,11},{4,12},{5,13},{6,14},{7,15},{8,0},{9,1},... | collective-permute-start | bytes 393224 | tf_op jit(solution)/shard_map/ppermute | solution.py:33
  101.2 13.7 %collective-permute-start.34 = (bf16[32,2048]{1,0:T(8,128)(2,1)S(1)}, bf16[32,2048]{1,0:T(8,128)(2,1)S(1)}, u32[]{:S(2)}, u32[]{:S(2)}) collective-permute-start(bf16[32,2048]{1,0:T(8,128)(2,1)S(1)} %get-tuple-element.49), channel_id=1, source_target_pairs={{0,4},{1,5},{2,6},{3,7},{4,0},{5,1},{6,2},{7,3},{8,12},{9,13},{10,... | collective-permute-start | bytes 393224 | tf_op jit(solution)/shard_map/ppermute | solution.py:33
  122.1 5.5 %collective-permute-start.38 = (f32[96,32]{1,0:T(8,128)S(1)}, f32[96,32]{1,0:T(8,128)S(1)}, u32[]{:S(2)}, u32[]{:S(2)}) collective-permute-start(f32[96,32]{1,0:T(8,128)S(1)} %add.66), channel_id=1, source_target_pairs={{0,8},{1,9},{2,10},{3,11},{4,12},{5,13},{6,14},{7,15},{8,0},{9,1},... | collective-permute-start | bytes 36872 | tf_op jit(solution)/shard_map/ppermute | solution.py:33
  122.8 6.0 %collective-permute-start.39 = (f32[96,32]{1,0:T(8,128)S(1)}, f32[96,32]{1,0:T(8,128)S(1)}, u32[]{:S(2)}, u32[]{:S(2)}) collective-permute-start(f32[96,32]{1,0:T(8,128)S(1)} %add.66), channel_id=1, source_target_pairs={{0,12},{1,13},{2,14},{3,15},{4,8},{5,9},{6,10},{7,11},{8,4},{9,5},... | collective-permute-start | bytes 36872 | tf_op jit(solution)/shard_map/ppermute | solution.py:33
  (20 other events, 166.7 us)

commit v3 on v1

v3 whole, which is shorter than its diff:
```python
import functools
import math

import jax
import jax.numpy as jnp
import numpy as np
from jax import lax
from jax.experimental import pallas as pl
from jax.experimental.pallas import tpu as pltpu
from jax.sharding import PartitionSpec as P

precise = lax.Precision.HIGHEST
SMEM = pl.BlockSpec(memory_space=pltpu.SMEM)
VMEM = pl.BlockSpec(memory_space=pltpu.VMEM)
ANY = pl.BlockSpec(memory_space=pl.ANY)
UNROLL = 16
STEP = 16
ITERS = 2


def product(left, right):
    return lax.dot_general(left, right, (((1,), (0,)), ((), ())), precision=precise, preferred_element_type=jnp.float32)


def product_t(left, right):
    return lax.dot_general(left, right, (((1,), (1,)), ((), ())), precision=precise, preferred_element_type=jnp.float32)


def t_product(left, right):
    return lax.dot_general(left, right, (((0,), (0,)), ((), ())), precision=precise, preferred_element_type=jnp.float32)


def swap(array, offset):
    count = lax.axis_size("rows")
    return lax.ppermute(array, "rows", [(place, place ^ offset) for place in range(count)])


def stages(count):
    bits = count.bit_length() - 1
    top = min(2, bits)
    return list(range(bits - top)), bits - top, 1 << top


def positions(count):
    low, shift, wide = stages(count)
    bits = count.bit_length() - 1
    place = []
    for offset in range(count):
        spot = offset >> shift
        for bit in low:
            spot += ((offset >> bit) & 1) << (bits - 1 - bit)
        place.append(spot)
    return np.array(place, np.int32)


def joined_kernel(near_ref, far_ref, out_ref):
    half = near_ref.shape[0]
    out_ref[:half] = near_ref[...]
    out_ref[half:] = far_ref[...]


def gather_lists(own, beside):
    lists, order = own, [0]
    for bit in reversed(range(lax.axis_size("rows").bit_length() - 1)):
        arrived = swap(lists, 1 << bit)
        out = jax.ShapeDtypeStruct((2 * lists.shape[0], lists.shape[1]), lists.dtype)
        lists = call(joined_kernel, out, lists, arrived, name="joined")
        if len(order) == 1:
            found = beside(lists)
        order = order + [offset | 1 << bit for offset in order]
    return lists, np.argsort(np.array(order)).astype(np.int32), found


def gather_orders(count):
    low, shift, wide = stages(count)
    x = 1 << low[-1]
    early = [[0, x], [1 << shift, 1 << shift | x], [2 << shift, 3 << shift]]
    late = [[2 << shift | x, 3 << shift | x]]
    for bit in reversed(low[:-1]):
        early = early + [[offset | 1 << bit for offset in offsets] for offsets in early]
        late = late + [[offset | 1 << bit for offset in offsets] for offsets in late]
    return early, late


def gather_panels(panel, near, tokens, forward):
    low, shift, wide = stages(lax.axis_size("rows"))
    x = 1 << low[-1]
    fars = [swap(panel, 2 << shift), swap(panel, 3 << shift)]
    pair = stacked([panel, near], tokens[0])
    early = [pair, swap(pair, 1 << shift), stacked(fars, tokens[1])]
    late = swap(early[2], x)
    for bit in reversed(low[:-1]):
        early = early + [swap(array, 1 << bit) for array in early]
    count = 2 * len(early)
    out = forward(early, 0, None)
    late = [stacked([late[0], late[1]], out)]
    for bit in reversed(low[:-1]):
        late = late + [swap(array, 1 << bit) for array in late]
    return forward(late, count, out)


def reduce_panels(kept, sent):
    low, shift, wide = stages(lax.axis_size("rows"))
    x = 1 << low[-1]
    for bit in low[:-2]:
        arrived = swap(sent, 1 << bit)
        half = kept.shape[0] // 2
        sent = (kept[half:] + arrived[half:]).astype(jnp.bfloat16)
        kept = kept[:half] + arrived[:half]
    arrived = swap(sent, 1 << low[-2])
    kept, over_x, over_z = added(kept, arrived)
    return kept, swap(over_x, x), swap(over_z, 1 << shift)


def finish_panels(kept, over_x, over_z):
    low, shift, wide = stages(lax.axis_size("rows"))
    x = 1 << low[-1]
    terms = [swap((kept[2 + far] + over_x[far]).astype(jnp.bfloat16), (2 + far) << shift) for far in (1, 0)]
    return [kept[0], over_z[0], swap((kept[1] + over_z[1]).astype(jnp.bfloat16), x)] + terms


def added_kernel(kept_ref, arrived_ref, out_ref, over_x_ref, over_z_ref):
    def total(place):
        return kept_ref[place] + arrived_ref[place].astype(jnp.float32)

    for index, place in enumerate((0, 4, 2, 3)):
        out_ref[index] = total(place)
    for index, place in enumerate((6, 7)):
        over_x_ref[index] = total(place).astype(jnp.bfloat16)
    for index, place in enumerate((1, 5)):
        over_z_ref[index] = total(place).astype(jnp.bfloat16)


def added(kept, arrived):
    shape = jax.ShapeDtypeStruct
    half = shape((2, *kept.shape[1:]), jnp.bfloat16)
    return call(added_kernel, (shape((4, *kept.shape[1:]), jnp.float32), half, half), kept, arrived, name="added")


def stacked_kernel(*refs):
    for index, ref in enumerate(refs[:-2]):
        refs[-1][index] = ref[...]


def stacked(pieces, token):
    out = jax.ShapeDtypeStruct((len(pieces), *pieces[0].shape), pieces[0].dtype)
    return call(stacked_kernel, out, *pieces, token, name="stacked", specs=[VMEM] * len(pieces) + [ANY])


def reduce_small(array):
    low, shift, wide = stages(lax.axis_size("rows"))
    for bit in low:
        array = array + swap(array, 1 << bit)
    others = [swap(array, far << shift) for far in range(1, wide)]
    total = array + others[0]
    if wide == 4:
        total = total + (others[1] + others[2])
    return total


def tile_place(tile, fixed_ref, list_ref, sizes):
    count, capacity, tiles, tile_size = sizes
    me = fixed_ref[0]
    slot = fixed_ref[1 + 2 * count + tiles + tile]
    offset = (slot // capacity) ^ me
    block = list_ref[fixed_ref[1 + count + offset], me * capacity + slot % capacity]
    row = fixed_ref[1 + 2 * count + tile]
    own = pl.ds(pl.multiple_of(row * tile_size, tile_size), tile_size)
    other = pl.ds(pl.multiple_of(block * tile_size, tile_size), tile_size)
    return own, fixed_ref[1 + offset], other


def backward_product(tile, row, high_ref, low_ref, tiles_ref):
    tile_size = tiles_ref.shape[1]
    width = high_ref.shape[0]
    own = pl.ds(pl.multiple_of(row * tile_size, tile_size), tile_size)
    left = jnp.concatenate([high_ref[:, own], low_ref[:, own]], axis=0)
    both = jnp.dot(left, tiles_ref[tile], preferred_element_type=jnp.float32)
    return both[:width] + both[width:]


def over_tiles(tiles, body):
    def some(step, carry):
        for u in range(UNROLL):
            body(step * UNROLL + u)
        return carry

    lax.fori_loop(0, tiles // UNROLL, some, 0)


def products_kernel(rows_ref, start_ref, tiles_ref, token_ref, out_ref, held_ref, high_ref, low_ref, panel, arrived):
    tiles = out_ref.shape[0]
    whole = pltpu.make_async_copy(start_ref, panel, arrived.at[tiles // UNROLL])

    def copy(chunk):
        some = pl.ds(chunk * UNROLL, UNROLL)
        return pltpu.make_async_copy(tiles_ref.at[some], held_ref.at[some], arrived.at[chunk])

    whole.start()
    for chunk in range(tiles // UNROLL):
        copy(chunk).start()
    whole.wait()
    split_kernel(panel, high_ref, low_ref)
    for chunk in range(tiles // UNROLL):
        copy(chunk).wait()
        for tile in range(chunk * UNROLL, (chunk + 1) * UNROLL):
            out_ref[tile] = backward_product(tile, rows_ref[tile], high_ref, low_ref, held_ref)


def sums_kernel(fixed_ref, list_ref, products_ref, token_ref, kept_ref, sent_ref, total, *, sizes):
    half = kept_ref.shape[0]
    total[...] = jnp.zeros_like(total)

    def one(tile):
        own, piece, other = tile_place(tile, fixed_ref, list_ref, sizes)
        total[piece, :, other] += products_ref[tile].astype(total.dtype)

    over_tiles(sizes[2], one)
    kept_ref[...] = total[:half].astype(kept_ref.dtype)
    sent_ref[...] = total[half:].astype(sent_ref.dtype)


def backward_kernel(fixed_ref, list_ref, high_ref, low_ref, tiles_ref, kept_ref, sent_ref, total, *, sizes):
    count, _, tiles, _ = sizes
    half = kept_ref.shape[0]
    total[...] = jnp.zeros_like(total)

    def one(tile):
        own, piece, other = tile_place(tile, fixed_ref, list_ref, sizes)
        found = backward_product(tile, fixed_ref[1 + 2 * count + tile], high_ref, low_ref, tiles_ref)
        total[piece, :, other] += found.astype(total.dtype)

    over_tiles(tiles, one)
    kept_ref[...] = total[:half].astype(kept_ref.dtype)
    sent_ref[...] = total[half:].astype(sent_ref.dtype)


def plan_kernel(fixed_ref, list_ref, plan_ref, *, sizes, early):
    count, capacity, tiles, _ = sizes
    me = fixed_ref[0]

    def one(tile, found):
        front, back = found
        slot = fixed_ref[1 + 2 * count + tiles + tile]
        offset = (slot // capacity) ^ me
        block = list_ref[fixed_ref[1 + count + offset], me * capacity + slot % capacity]
        piece = fixed_ref[1 + 2 * count + 2 * tiles + offset]
        first = piece < early
        place = jnp.where(first, front, back)
        plan_ref[place] = ((tile * 256 + piece) * 16 + fixed_ref[1 + 2 * count + tile]) * 16 + block
        more = first.astype(jnp.int32)
        return front + more, back - (1 - more)

    front, _ = lax.fori_loop(0, tiles, one, (0, tiles - 1))
    plan_ref[tiles] = front


def forward_kernel(plan_ref, tiles_ref, *refs, groups, base, late):
    group_refs, (out_ref, pieces) = refs[:groups], refs[-2:]
    tiles, tile_size, _ = tiles_ref.shape
    for group, ref in enumerate(group_refs):
        pieces[group * 2 : (group + 1) * 2] = ref[...]
    out_ref[...] = refs[groups][...] if late else jnp.zeros_like(out_ref)
    front = plan_ref[tiles]
    start, end = (front, tiles) if late else (0, front)

    def some(step, carry):
        for u in range(8):
            at = start + step * 8 + u
            packed = plan_ref[jnp.minimum(at, tiles - 1)]
            block, row, piece, tile = packed % 16, packed // 16 % 16, packed // 256 % 256, packed // 65536
            piece = jnp.clip(piece - base, 0, groups * 2 - 1)
            own = pl.ds(pl.multiple_of(row * tile_size, tile_size), tile_size)
            other = pl.ds(pl.multiple_of(block * tile_size, tile_size), tile_size)
            found = lax.dot_general(
                pieces[piece, :, other], tiles_ref[tile], (((1,), (1,)), ((), ())), preferred_element_type=jnp.float32
            )
            out_ref[:, own] += jnp.where(at < end, found, 0.0)
        return carry

    lax.fori_loop(0, (end - start + 7) // 8, some, 0)


def split_kernel(whole_ref, high_ref, low_ref):
    high = whole_ref[...].astype(jnp.bfloat16)
    high_ref[...] = high
    low_ref[...] = (whole_ref[...] - high.astype(jnp.float32)).astype(jnp.bfloat16)


def combine_kernel(links_ref, panel_ref, forward_ref, *refs):
    term_refs, (out_ref, high_ref, low_ref) = refs[:-3], refs[-3:]
    out = (links_ref[...] - 1.0) * panel_ref[...] + forward_ref[...]
    for ref in term_refs:
        out = out + ref[...].astype(jnp.float32)
    out_ref[...] = out
    high = out.astype(jnp.bfloat16)
    high_ref[...] = high
    low_ref[...] = (out - high.astype(jnp.float32)).astype(jnp.bfloat16)


def factor_of(gram):
    width = gram.shape[0]
    lanes = -(-width // 128) * 128
    rows = lax.broadcasted_iota(jnp.int32, (width, lanes), 0)
    columns = lax.broadcasted_iota(jnp.int32, (width, lanes), 1)
    left = jnp.concatenate([gram, jnp.zeros((width, lanes - width), jnp.float32)], axis=1)
    right = (rows == columns).astype(jnp.float32)
    upper, inverse = [], []
    for at in range(0, width, STEP):
        spread = [jnp.broadcast_to(left[:, at + i : at + i + 1], left.shape) for i in range(STEP)]
        lefts, rights, factors = [], [], []
        for i in range(STEP):
            row, other, column = left[i : i + 1], right[i : i + 1], spread[i]
            for k in range(i):
                part = factors[k][i : i + 1]
                row = row - part * lefts[k]
                other = other - part * rights[k]
                column = column - part * factors[k]
            scale = lax.rsqrt(column[i : i + 1])
            lefts.append(row * scale)
            rights.append(other * scale)
            factors.append(column * scale)
        upper += lefts
        inverse += rights
        left, right = left[STEP:], right[STEP:]
        if at + STEP < width:
            for i in range(STEP):
                factor = factors[i][STEP:]
                left = left - factor * lefts[i]
                right = right - factor * rights[i]
    upper = jnp.concatenate(upper, axis=0)[:, :width]
    inverse = jnp.concatenate(inverse, axis=0)[:, :width]
    return jnp.where(rows[:, :width] >= columns[:, :width], upper.T, 0.0), inverse


def gram_kernel(links_ref, start_ref, first_ref, forward_ref, *refs):
    term_refs, (panels_ref, gram_ref) = refs[:-2], refs[-2:]
    width = start_ref.shape[0]
    second = links_ref[...] * first_ref[...] + forward_ref[...]
    for ref in term_refs:
        second = second + ref[...].astype(jnp.float32)
    panels_ref[:width] = start_ref[...]
    panels_ref[width : 2 * width] = first_ref[...]
    panels_ref[2 * width :] = second
    gram_ref[...] = product_t(panels_ref[...], panels_ref[...])


def last_kernel(gram_ref, panels_ref, out_ref, couplings_ref, factors_ref, *, scale):
    width = out_ref.shape[0]
    factor, inverse = factor_of(gram_ref[...])
    out_ref[...] = product(inverse[2 * width :] * scale, panels_ref[...])

    def block(of, row, column):
        return of[row * width : (row + 1) * width, column * width : (column + 1) * width]

    rows = lax.broadcasted_iota(jnp.int32, (width, width), 0)
    columns = lax.broadcasted_iota(jnp.int32, (width, width), 1)
    unit = (rows == columns).astype(jnp.float32)
    couplings_ref[0] = product(block(inverse, 0, 0), block(factor, 1, 0)).T + unit
    turned = product(block(inverse, 1, 0), block(factor, 1, 1)) + product(block(inverse, 1, 1), block(factor, 2, 1))
    couplings_ref[1] = turned.T
    factors_ref[0] = jnp.where(rows >= columns, product(block(inverse, 0, 0), block(factor, 1, 1)), 0.0)
    factors_ref[1] = jnp.where(rows >= columns, product(block(inverse, 1, 1), block(factor, 2, 2)), 0.0)


def room_for(*arrays):
    return (2 << 20) + sum(math.prod(array.shape) * jnp.dtype(array.dtype).itemsize for array in arrays)


def call(kernel, out, *args, name, scratch=(), specs=None, cost=None):
    return pl.pallas_call(
        kernel,
        out_shape=out,
        in_specs=specs or [VMEM] * len(args),
        out_specs=jax.tree.map(lambda _: VMEM, out),
        scratch_shapes=list(scratch),
        compiler_params=pltpu.CompilerParams(vmem_limit_bytes=room_for(*args, *jax.tree.leaves(out), *scratch)),
        cost_estimate=cost,
        name=name,
    )(*args)


def on_device(tile_values, tile_rows, tile_slots, send_list, self_links, start_panel):
    count = lax.axis_size("rows")
    width, here = start_panel.shape
    tiles, tile_size, _ = tile_values.shape
    capacity = send_list.shape[2]
    f32, bf16 = jnp.float32, jnp.bfloat16
    shape = jax.ShapeDtypeStruct
    links = self_links[None, :]
    me = lax.axis_index("rows").astype(jnp.int32).reshape(1)
    panel = shape((width, here), f32)
    half = shape((width, here), bf16)
    cost = pl.CostEstimate(flops=2 * tiles * width * tile_size * tile_size, bytes_accessed=1 << 10, transcendentals=0)

    def first_products(token):
        return pl.pallas_call(
            products_kernel,
            out_shape=(shape((tiles, width, tile_size), f32), pltpu.VMEM(tile_values.shape, bf16), half, half),
            in_specs=[SMEM, ANY, ANY, ANY],
            out_specs=(VMEM,) * 4,
            scratch_shapes=[pltpu.VMEM((width, here), f32), pltpu.SemaphoreType.DMA((tiles // UNROLL + 1,))],
            compiler_params=pltpu.CompilerParams(vmem_limit_bytes=room_for(tile_values, panel, panel, shape((tiles, width, tile_size), f32))),
            cost_estimate=cost,
            name="products",
        )(
            tile_rows, pltpu.with_memory_space_constraint(start_panel, pltpu.HBM),
            pltpu.with_memory_space_constraint(tile_values, pltpu.HBM), token,
        )

    lists, list_place, (products, held, high, low) = gather_lists(send_list.reshape(1, -1), first_products)
    orders = gather_orders(count)
    order = [offset for group in orders for offsets in group for offset in offsets]
    gathered_place = np.argsort(np.array(order)).astype(np.int32)
    early_pieces = 2 * len(orders[0])
    fixed = jnp.concatenate(
        [me, jnp.asarray(positions(count)), jnp.asarray(list_place), tile_rows, tile_slots, jnp.asarray(gathered_place)]
    )
    indices = (fixed, lists)
    sizes = (count, capacity, tiles, tile_size)
    spec = [SMEM] * len(indices)
    total_type = f32 if count <= 16 else bf16

    sums = (shape((count // 2, width, here), total_type), shape((count // 2, width, here), bf16))
    scratch = [pltpu.VMEM((count, width, here), total_type)]

    def first_sums(token):
        return call(
            functools.partial(sums_kernel, sizes=sizes), sums, *indices, products, token,
            name="sums", specs=spec + [VMEM, ANY], scratch=scratch, cost=cost,
        )

    def backward(high, low, token):
        return call(
            functools.partial(backward_kernel, sizes=sizes), sums, *indices, high, low, held,
            name="backward", specs=spec + [VMEM] * 3, scratch=scratch, cost=cost,
        )

    plan = pl.pallas_call(
        functools.partial(plan_kernel, sizes=sizes, early=early_pieces),
        out_shape=shape((tiles + 1,), jnp.int32), in_specs=spec, out_specs=SMEM, name="plan",
        compiler_params=pltpu.CompilerParams(vmem_limit_bytes=1 << 20),
    )(*indices)

    def forward(groups, base, before):
        late = before is not None
        return call(
            functools.partial(forward_kernel, groups=len(groups), base=base, late=late),
            shape((width, here), f32),
            plan, held, *groups, *([before] if late else []),
            name="late" if late else "early", specs=[SMEM] + [VMEM] * (1 + len(groups) + late),
            scratch=[pltpu.VMEM((2 * len(groups), width, here), bf16)], cost=cost,
        )

    def applied(high, sums):
        near = swap(high, 1 << stages(count)[0][-1])
        kept, over_x, over_z = reduce_panels(*sums(high))
        terms = finish_panels(kept, over_x, over_z)
        return [gather_panels(high, near, (kept, over_x), forward)] + terms

    terms = applied(high, first_sums)
    first, high, low = call(combine_kernel, (panel, half, half), links, start_panel, *terms, name="combine")
    terms = applied(high, functools.partial(backward, high, low))
    all_panels = (ITERS + 1) * width
    panels, gram = call(
        gram_kernel, (shape((all_panels, here), f32), shape((all_panels, all_panels), f32)), links, start_panel, first, *terms, name="gram"
    )
    both = shape((ITERS, width, width), f32)
    return call(
        functools.partial(last_kernel, scale=math.sqrt(here * count)), (panel, both, both), reduce_small(gram), panels, name="last"
    )


def solution(mesh):
    placed = (
        P(("groups", "rows"), None, None),
        P(("groups", "rows")),
        P(("groups", "rows")),
        P(("groups", "rows"), None, None),
        P(("groups", "rows")),
        P(None, ("groups", "rows")),
    )
    return jax.shard_map(
        on_device,
        mesh=mesh,
        in_specs=placed,
        out_specs=(P(None, ("groups", "rows")), P("groups", None, None), P("groups", None, None)),
        check_vma=False,
    )
```

time: 192 us -> 129 us (0.67)
  waiting for transfers between devices: 97 us -> 46.9 us
  Pallas kernels: 47.5 us -> 35 us
  starting transfers between devices: 40.3 us -> 43.1 us
  other arithmetic: 2.23 us -> 0.24 us
    ppermute x32 -> x39, waiting for transfers between devices: 91.7 us -> 46.9 us  [swap(): lax.ppermute(array, 'rows', [(place, place ^ offset) for place in range(c...]
    pallas_call x10 -> x21, Pallas kernels: 47.5 us -> 25.2 us  [call(): pl.pallas_call(kernel, out_shape=out, in_specs=specs or [VMEM] * len(args...]
    ppermute x32 -> x39, starting transfers between devices: 32.9 us -> 43.1 us  [swap(): lax.ppermute(array, 'rows', [(place, place ^ offset) for place in range(c...]
    pallas_call x0 -> x2, Pallas kernels: none -> 9.82 us  [the longest x1 6.35 us: first_products(): pl.pallas_call(products_kernel, out_shape=(shape((tiles, width, tile_size...]
    all_to_all x1 -> x0, starting transfers between devices: 7.37 us -> none  [on_device(): lax.all_to_all(send_list[0], 'rows', split_axis=0, concat_axis=0, tiled=T...]
    all_to_all x1 -> x0, waiting for transfers between devices: 5.32 us -> none  [on_device(): lax.all_to_all(send_list[0], 'rows', split_axis=0, concat_axis=0, tiled=T...]
    unnamed x18 -> x6, local copies, waits for them, and re-layouts: 2.94 us -> 0.66 us
  transfers between devices with their start and end apart: 33 -> 39, of which waited for: 23 -> 21; matrix products, arithmetic and copies ran while one was open for 0% -> 1% of each run, Pallas kernels for 13% -> 18%
where the time goes in v3:
time: 129 us
  waiting for transfers between devices  46.9 us (36%)
  starting transfers between devices  43.1 us (33%)
  Pallas kernels  35 us (27%)
  local copies, waits for them, and re-layouts  2.29 us (2%)
    ppermute x39, waiting for transfers between devices, swap(): lax.ppermute(array, 'rows', [(place, place ^ offset) for place in range(c...  46.9 us
    ppermute x39, starting transfers between devices, swap(): lax.ppermute(array, 'rows', [(place, place ^ offset) for place in range(c...  43.1 us
    pallas_call x21, Pallas kernels, call(): pl.pallas_call(kernel, out_shape=out, in_specs=specs or [VMEM] * len(args...  25.2 us
    pallas_call x1, Pallas kernels, first_products(): pl.pallas_call(products_kernel, out_shape=(shape((tiles, width, tile_size...  6.35 us
    pallas_call x1, Pallas kernels, on_device(): pl.pallas_call(functools.partial(plan_kernel, sizes=sizes, early=early_pi...  3.48 us
  transfers between devices with their start and end apart: 39, of which 21 were waited for; matrix products, arithmetic and copies ran while one was open for 1% of the time, Pallas kernels for 18%

profile of v3, /device:TPU:0, one launch (start us, length us, event | category | flops | bytes accessed | tf_op | source)
XLA Modules:
  0.0 128.5 jit_solution(14749819899704079992)
XLA Ops:
  1.4 4.0 %collective-permute-start = (s32[1,256]{1,0:T(1,128)S(1)}, s32[1,256]{1,0:T(1,128)S(1)}, u32[]{:S(2)}, u32[]{:S(2)}) collective-permute-start(s32[1,256]{1,0:T(1,128)S(1)} %reshape.31.near_ref), channel_id=1, source_target_pairs={{0,8},{1,9},{2,10},{3,11},{4,12},{5,13},{6,14},{7,15},{8,0},{9,1},... | collective-permute-start | bytes 3080 | tf_op jit(solution)/shard_map/ppermute | solution.py:35
  7.0 1.9 %collective-permute-start.1 = (s32[2,256]{1,0:T(2,128)S(1)}, s32[2,256]{1,0:T(2,128)S(1)}, u32[]{:S(2)}, u32[]{:S(2)}) collective-permute-start(s32[2,256]{1,0:T(2,128)S(1)} %joined.4.near_ref.token_ref), channel_id=1, source_target_pairs={{0,4},{1,5},{2,6},{3,7},{4,0},{5,1},{6,2},{7,3},{8,12},{9,13},{10,... | collective-permute-start | bytes 6152 | tf_op jit(solution)/shard_map/ppermute | solution.py:35
  8.9 1.7 %collective-permute-done.1.far_ref = s32[2,256]{1,0:T(2,128)S(1)} collective-permute-done((s32[2,256]{1,0:T(2,128)S(1)}, s32[2,256]{1,0:T(2,128)S(1)}, u32[]{:S(2)}, u32[]{:S(2)}) %collective-permute-start.1) | collective-permute-done | bytes 2080 | tf_op jit(solution)/shard_map/ppermute | solution.py:35
  10.6 1.8 %collective-permute-start.2 = (s32[4,256]{1,0:T(4,128)S(1)}, s32[4,256]{1,0:T(4,128)S(1)}, u32[]{:S(2)}, u32[]{:S(2)}) collective-permute-start(s32[4,256]{1,0:T(4,128)S(1)} %joined.5.near_ref), channel_id=1, source_target_pairs={{0,2},{1,3},{2,0},{3,1},{4,6},{5,7},{6,4},{7,5},{8,10},{9,11},{10,... | collective-permute-start | bytes 12296 | tf_op jit(solution)/shard_map/ppermute | solution.py:35
  14.9 6.3 %products.1 = (f32[96,32,256]{2,1,0:T(8,128)S(1)}, bf16[96,256,256]{2,1,0:T(8,128)(2,1)S(1)}, bf16[32,2048]{1,0:T(8,128)(2,1)S(1)}, bf16[32,2048]{1,0:T(8,128)(2,1)}) custom-call(s32[96]{0:T(128)S(1)} %copy-done.2, f32[32,2048]{1,0:T(8,128)} %start_ref.3, bf16[96,256,256]{2,1,0:T(8,128)(2,1)} %tiles_ref.1, s32[2,256]{1,0:T(2,128)S(1)} %joined.4.near_ref.token_ref), custom_call_target="tpu_custom_call" | custom-call | flops 402653184 | bytes 1024 | tf_op jit(solution)/shard_map/products/pallas_call | solution.py:397
  21.2 2.5 %sums.1 = (f32[8,32,2048]{2,1,0:T(8,128)S(1)}, bf16[8,32,2048]{2,1,0:T(8,128)(2,1)S(1)}) custom-call(s32[241]{0:T(256)S(1)} %concatenate.3.fixed_ref, s32[16,256]{1,0:T(8,128)S(1)} %joined.7.list_ref, f32[96,32,256]{2,1,0:T(8,128)S(1)} %get-tuple-element.23.products_ref, bf16[32,2048]{1,0:T(8,128)(2,1)S(1)} %get-tuple-element.22.token_ref.refs_0_), custom_call_target="tpu_custom_call" | custom-call | flops 402653184 | bytes 1024 | tf_op jit(solution)/shard_map/sums/pallas_call | solution.py:371
  24.3 2.3 %collective-permute-done.6.arrived_ref = bf16[8,32,2048]{2,1,0:T(8,128)(2,1)S(1)} collective-permute-done((bf16[8,32,2048]{2,1,0:T(8,128)(2,1)S(1)}, bf16[8,32,2048]{2,1,0:T(8,128)(2,1)S(1)}, u32[]{:S(2)}, u32[]{:S(2)}) %collective-permute-start.6) | collective-permute-done | bytes 1048608 | tf_op jit(solution)/shard_map/ppermute | solution.py:35
  26.9 1.9 %collective-permute-start.7 = (bf16[2,32,2048]{2,1,0:T(8,128)(2,1)S(1)}, bf16[2,32,2048]{2,1,0:T(8,128)(2,1)S(1)}, u32[]{:S(2)}, u32[]{:S(2)}) collective-permute-start(bf16[2,32,2048]{2,1,0:T(8,128)(2,1)S(1)} %get-tuple-element.26), channel_id=1, source_target_pairs={{0,2},{1,3},{2,0},{3,1},{4,6},{5,7},{6,4},{7,5},{8,10},{9,11},{10,... | collective-permute-start | bytes 786440 | tf_op jit(solution)/shard_map/ppermute | solution.py:35
  30.9 2.6 %collective-permute-start.4 = (bf16[32,2048]{1,0:T(8,128)(2,1)S(1)}, bf16[32,2048]{1,0:T(8,128)(2,1)S(1)}, u32[]{:S(2)}, u32[]{:S(2)}) collective-permute-start(bf16[32,2048]{1,0:T(8,128)(2,1)S(1)} %get-tuple-element.22.token_ref.refs_0_), channel_id=1, source_target_pairs={{0,8},{1,9},{2,10},{3,11},{4,12},{5,13},{6,14},{7,15},{8,0},{9,1},... | collective-permute-start | bytes 393224 | tf_op jit(solution)/shard_map/ppermute | solution.py:35
  33.5 3.5 %plan.1.plan_ref = s32[97]{0:T(128)S(1)} custom-call(s32[241]{0:T(256)S(1)} %concatenate.3.fixed_ref, s32[16,256]{1,0:T(8,128)S(1)} %joined.7.list_ref), custom_call_target="tpu_custom_call" | custom-call | tf_op jit(solution)/shard_map/plan/pallas_call | solution.py:439
  38.4 1.9 %collective-permute-start.10 = (bf16[2,32,2048]{2,1,0:T(8,128)(2,1)S(1)}, bf16[2,32,2048]{2,1,0:T(8,128)(2,1)S(1)}, u32[]{:S(2)}, u32[]{:S(2)}) collective-permute-start(bf16[2,32,2048]{2,1,0:T(8,128)(2,1)S(1)} %stacked.7.refs_0_), channel_id=1, source_target_pairs={{0,4},{1,5},{2,6},{3,7},{4,0},{5,1},{6,2},{7,3},{8,12},{9,13},{10,... | collective-permute-start | bytes 786440 | tf_op jit(solution)/shard_map/ppermute | solution.py:35
  40.3 5.3 %collective-permute-done.5.refs_1_ = bf16[32,2048]{1,0:T(8,128)(2,1)S(1)} collective-permute-done((bf16[32,2048]{1,0:T(8,128)(2,1)S(1)}, bf16[32,2048]{1,0:T(8,128)(2,1)S(1)}, u32[]{:S(2)}, u32[]{:S(2)}) %collective-permute-start.5) | collective-permute-done | bytes 131104 | tf_op jit(solution)/shard_map/ppermute | solution.py:35
  46.4 1.6 %collective-permute-start.16 = (bf16[32,2048]{1,0:T(8,128)(2,1)S(1)}, bf16[32,2048]{1,0:T(8,128)(2,1)S(1)}, u32[]{:S(2)}, u32[]{:S(2)}) collective-permute-start(bf16[32,2048]{1,0:T(8,128)(2,1)S(1)} %get-tuple-element.45), channel_id=1, source_target_pairs={{0,2},{1,3},{2,0},{3,1},{4,6},{5,7},{6,4},{7,5},{8,10},{9,11},{10,... | collective-permute-start | bytes 393224 | tf_op jit(solution)/shard_map/ppermute | solution.py:35
  49.2 2.7 %collective-permute-start.17 = (bf16[32,2048]{1,0:T(8,128)(2,1)S(1)}, bf16[32,2048]{1,0:T(8,128)(2,1)S(1)}, u32[]{:S(2)}, u32[]{:S(2)}) collective-permute-start(bf16[32,2048]{1,0:T(8,128)(2,1)S(1)} %get-tuple-element.42), channel_id=1, source_target_pairs={{0,12},{1,13},{2,14},{3,15},{4,8},{5,9},{6,10},{7,11},{8,4},{9,5},... | collective-permute-start | bytes 393224 | tf_op jit(solution)/shard_map/ppermute | solution.py:35
  51.9 3.0 %collective-permute-done.8 = bf16[2,32,2048]{2,1,0:T(8,128)(2,1)S(1)} collective-permute-done((bf16[2,32,2048]{2,1,0:T(8,128)(2,1)S(1)}, bf16[2,32,2048]{2,1,0:T(8,128)(2,1)S(1)}, u32[]{:S(2)}, u32[]{:S(2)}) %collective-permute-start.8) | collective-permute-done | bytes 262176 | tf_op jit(solution)/shard_map/ppermute | solution.py:35
  56.4 4.9 %early.2.refs_2_ = f32[32,2048]{1,0:T(8,128)S(1)} custom-call(s32[97]{0:T(128)S(1)} %plan.1.plan_ref, bf16[96,256,256]{2,1,0:T(8,128)(2,1)S(1)} %get-tuple-element.21.tiles_ref, bf16[2,32,2048]{2,1,0:T(8,128)(2,1)S(1)} %stacked.7.refs_0_, bf16[2,32,2048]{2,1,0:T(8,128)(2,1)S(1)} %collective-permute-done.10.refs_1_, bf16[2,32,2048]{2,1,0:T(8,128)(2,1)S(1)} %stacked.6.refs_2_, ...), custom_call_target="tpu_custom_call" | custom-call | flops 402653184 | bytes 1024 | tf_op jit(solution)/shard_map/early/pallas_call | solution.py:371
  64.7 4.3 %backward.1 = (f32[8,32,2048]{2,1,0:T(8,128)S(1)}, bf16[8,32,2048]{2,1,0:T(8,128)(2,1)S(1)}) custom-call(s32[241]{0:T(256)S(1)} %concatenate.3.fixed_ref, s32[16,256]{1,0:T(8,128)S(1)} %joined.7.list_ref, bf16[32,2048]{1,0:T(8,128)(2,1)S(1)} %get-tuple-element.30.high_ref.refs_0_, bf16[32,2048]{1,0:T(8,128)(2,1)S(1)} %get-tuple-element.31.low_ref, ...), custom_call_target="tpu_custom_call" | custom-call | flops 402653184 | bytes 1024 | tf_op jit(solution)/shard_map/backward/pallas_call | solution.py:371
  70.5 2.3 %collective-permute-done.21.arrived_ref = bf16[8,32,2048]{2,1,0:T(8,128)(2,1)S(1)} collective-permute-done((bf16[8,32,2048]{2,1,0:T(8,128)(2,1)S(1)}, bf16[8,32,2048]{2,1,0:T(8,128)(2,1)S(1)}, u32[]{:S(2)}, u32[]{:S(2)}) %collective-permute-start.21) | collective-permute-done | bytes 1048608 | tf_op jit(solution)/shard_map/ppermute | solution.py:35
  73.8 1.9 %collective-permute-start.24 = (bf16[32,2048]{1,0:T(8,128)(2,1)S(1)}, bf16[32,2048]{1,0:T(8,128)(2,1)S(1)}, u32[]{:S(2)}, u32[]{:S(2)}) collective-permute-start(bf16[32,2048]{1,0:T(8,128)(2,1)S(1)} %get-tuple-element.30.high_ref.refs_0_), channel_id=1, source_target_pairs={{0,2},{1,3},{2,0},{3,1},{4,6},{5,7},{6,4},{7,5},{8,10},{9,11},{10,... | collective-permute-start | bytes 393224 | tf_op jit(solution)/shard_map/ppermute | solution.py:35
  75.7 1.8 %collective-permute-start.19 = (bf16[32,2048]{1,0:T(8,128)(2,1)S(1)}, bf16[32,2048]{1,0:T(8,128)(2,1)S(1)}, u32[]{:S(2)}, u32[]{:S(2)}) collective-permute-start(bf16[32,2048]{1,0:T(8,128)(2,1)S(1)} %get-tuple-element.30.high_ref.refs_0_), channel_id=1, source_target_pairs={{0,8},{1,9},{2,10},{3,11},{4,12},{5,13},{6,14},{7,15},{8,0},{9,1},... | collective-permute-start | bytes 393224 | tf_op jit(solution)/shard_map/ppermute | solution.py:35
  77.4 2.0 %collective-permute-start.20 = (bf16[32,2048]{1,0:T(8,128)(2,1)S(1)}, bf16[32,2048]{1,0:T(8,128)(2,1)S(1)}, u32[]{:S(2)}, u32[]{:S(2)}) collective-permute-start(bf16[32,2048]{1,0:T(8,128)(2,1)S(1)} %get-tuple-element.30.high_ref.refs_0_), channel_id=1, source_target_pairs={{0,12},{1,13},{2,14},{3,15},{4,8},{5,9},{6,10},{7,11},{8,4},{9,5},... | collective-permute-start | bytes 393224 | tf_op jit(solution)/shard_map/ppermute | solution.py:35
  79.5 5.0 %collective-permute-done.24.refs_1_ = bf16[32,2048]{1,0:T(8,128)(2,1)S(1)} collective-permute-done((bf16[32,2048]{1,0:T(8,128)(2,1)S(1)}, bf16[32,2048]{1,0:T(8,128)(2,1)S(1)}, u32[]{:S(2)}, u32[]{:S(2)}) %collective-permute-start.24) | collective-permute-done | bytes 131104 | tf_op jit(solution)/shard_map/ppermute | solution.py:35
  84.9 2.8 %collective-permute-done.19.refs_0_ = bf16[32,2048]{1,0:T(8,128)(2,1)S(1)} collective-permute-done((bf16[32,2048]{1,0:T(8,128)(2,1)S(1)}, bf16[32,2048]{1,0:T(8,128)(2,1)S(1)}, u32[]{:S(2)}, u32[]{:S(2)}) %collective-permute-start.19) | collective-permute-done | bytes 131104 | tf_op jit(solution)/shard_map/ppermute | solution.py:35
  91.5 2.5 %collective-permute-done.25.refs_1_ = bf16[2,32,2048]{2,1,0:T(8,128)(2,1)S(1)} collective-permute-done((bf16[2,32,2048]{2,1,0:T(8,128)(2,1)S(1)}, bf16[2,32,2048]{2,1,0:T(8,128)(2,1)S(1)}, u32[]{:S(2)}, u32[]{:S(2)}) %collective-permute-start.25) | collective-permute-done | bytes 262176 | tf_op jit(solution)/shard_map/ppermute | solution.py:35
  95.5 2.9 %collective-permute-done.23 = bf16[2,32,2048]{2,1,0:T(8,128)(2,1)S(1)} collective-permute-done((bf16[2,32,2048]{2,1,0:T(8,128)(2,1)S(1)}, bf16[2,32,2048]{2,1,0:T(8,128)(2,1)S(1)}, u32[]{:S(2)}, u32[]{:S(2)}) %collective-permute-start.23) | collective-permute-done | bytes 262176 | tf_op jit(solution)/shard_map/ppermute | solution.py:35
  100.0 4.9 %early.3.refs_2_ = f32[32,2048]{1,0:T(8,128)S(1)} custom-call(s32[97]{0:T(128)S(1)} %plan.1.plan_ref, bf16[96,256,256]{2,1,0:T(8,128)(2,1)S(1)} %get-tuple-element.21.tiles_ref, bf16[2,32,2048]{2,1,0:T(8,128)(2,1)S(1)} %stacked.10.refs_0_, bf16[2,32,2048]{2,1,0:T(8,128)(2,1)S(1)} %collective-permute-done.25.refs_1_, ...), custom_call_target="tpu_custom_call" | custom-call | flops 402653184 | bytes 1024 | tf_op jit(solution)/shard_map/early/pallas_call | solution.py:371
  106.6 1.6 %late.3.forward_ref = f32[32,2048]{1,0:T(8,128)S(1)} custom-call(s32[97]{0:T(128)S(1)} %plan.1.plan_ref, bf16[96,256,256]{2,1,0:T(8,128)(2,1)S(1)} %get-tuple-element.21.tiles_ref, bf16[2,32,2048]{2,1,0:T(8,128)(2,1)S(1)} %stacked.11.refs_0_, bf16[2,32,2048]{2,1,0:T(8,128)(2,1)S(1)} %collective-permute-done.29.refs_1_, f32[32,2048]{1,0:T(8,128)S(1)} %early.3.refs_2_), custom_call_target="tpu_custom_call" | custom-call | flops 402653184 | bytes 1024 | tf_op jit(solution)/shard_map/late/pallas_call | solution.py:371
  111.8 3.7 %collective-permute-done.35 = f32[96,96]{1,0:T(8,128)S(1)} collective-permute-done((f32[96,96]{1,0:T(8,128)S(1)}, f32[96,96]{1,0:T(8,128)S(1)}, u32[]{:S(2)}, u32[]{:S(2)}) %collective-permute-start.35) | collective-permute-done | bytes 36896 | tf_op jit(solution)/shard_map/ppermute | solution.py:35
  116.8 2.0 %collective-permute-start.37 = (f32[96,96]{1,0:T(8,128)S(1)}, f32[96,96]{1,0:T(8,128)S(1)}, u32[]{:S(2)}, u32[]{:S(2)}) collective-permute-start(f32[96,96]{1,0:T(8,128)S(1)} %add.46), channel_id=1, source_target_pairs={{0,8},{1,9},{2,10},{3,11},{4,12},{5,13},{6,14},{7,15},{8,0},{9,1},... | collective-permute-start | bytes 110600 | tf_op jit(solution)/shard_map/ppermute | solution.py:35
  120.0 2.8 %collective-permute-done.37 = f32[96,96]{1,0:T(8,128)S(1)} collective-permute-done((f32[96,96]{1,0:T(8,128)S(1)}, f32[96,96]{1,0:T(8,128)S(1)}, u32[]{:S(2)}, u32[]{:S(2)}) %collective-permute-start.37) | collective-permute-done | bytes 36896 | tf_op jit(solution)/shard_map/ppermute | solution.py:35
  122.8 1.9 %collective-permute-done.38 = f32[96,96]{1,0:T(8,128)S(1)} collective-permute-done((f32[96,96]{1,0:T(8,128)S(1)}, f32[96,96]{1,0:T(8,128)S(1)}, u32[]{:S(2)}, u32[]{:S(2)}) %collective-permute-start.38) | collective-permute-done | bytes 36896 | tf_op jit(solution)/shard_map/ppermute | solution.py:35
  124.7 3.8 %last.1 = (f32[32,2048]{1,0:T(8,128)}, f32[2,32,32]{2,1,0:T(8,128)}, f32[2,32,32]{2,1,0:T(8,128)}) custom-call(f32[96,96]{1,0:T(8,128)S(1)} %add_add_fusion.gram_ref, f32[96,2048]{1,0:T(8,128)S(1)} %get-tuple-element.38.panels_ref), custom_call_target="tpu_custom_call" | custom-call | tf_op jit(solution)/shard_map/last/pallas_call | solution.py:371
  (86 shorter events, 33.3 us)
Async XLA Ops:
  1.4 5.6 %collective-permute-start = (s32[1,256]{1,0:T(1,128)S(1)}, s32[1,256]{1,0:T(1,128)S(1)}, u32[]{:S(2)}, u32[]{:S(2)}) collective-permute-start(s32[1,256]{1,0:T(1,128)S(1)} %reshape.31.near_ref), channel_id=1, source_target_pairs={{0,8},{1,9},{2,10},{3,11},{4,12},{5,13},{6,14},{7,15},{8,0},{9,1},... | collective-permute-start | bytes 3080 | tf_op jit(solution)/shard_map/ppermute | solution.py:35
  10.6 3.6 %collective-permute-start.2 = (s32[4,256]{1,0:T(4,128)S(1)}, s32[4,256]{1,0:T(4,128)S(1)}, u32[]{:S(2)}, u32[]{:S(2)}) collective-permute-start(s32[4,256]{1,0:T(4,128)S(1)} %joined.5.near_ref), channel_id=1, source_target_pairs={{0,2},{1,3},{2,0},{3,1},{4,6},{5,7},{6,4},{7,5},{8,10},{9,11},{10,... | collective-permute-start | bytes 12296 | tf_op jit(solution)/shard_map/ppermute | solution.py:35
  14.2 7.0 %collective-permute-start.3 = (s32[8,256]{1,0:T(8,128)S(1)}, s32[8,256]{1,0:T(8,128)S(1)}, u32[]{:S(2)}, u32[]{:S(2)}) collective-permute-start(s32[8,256]{1,0:T(8,128)S(1)} %joined.6.near_ref), channel_id=1, source_target_pairs={{0,1},{1,0},{2,3},{3,2},{4,5},{5,4},{6,7},{7,6},{8,9},{9,8},{10,11... | collective-permute-start | bytes 24584 | tf_op jit(solution)/shard_map/ppermute | solution.py:35
  26.9 18.8 %collective-permute-start.7 = (bf16[2,32,2048]{2,1,0:T(8,128)(2,1)S(1)}, bf16[2,32,2048]{2,1,0:T(8,128)(2,1)S(1)}, u32[]{:S(2)}, u32[]{:S(2)}) collective-permute-start(bf16[2,32,2048]{2,1,0:T(8,128)(2,1)S(1)} %get-tuple-element.26), channel_id=1, source_target_pairs={{0,2},{1,3},{2,0},{3,1},{4,6},{5,7},{6,4},{7,5},{8,10},{9,11},{10,... | collective-permute-start | bytes 786440 | tf_op jit(solution)/shard_map/ppermute | solution.py:35
  28.8 17.5 %collective-permute-start.15 = (bf16[2,32,2048]{2,1,0:T(8,128)(2,1)S(1)}, bf16[2,32,2048]{2,1,0:T(8,128)(2,1)S(1)}, u32[]{:S(2)}, u32[]{:S(2)}) collective-permute-start(bf16[2,32,2048]{2,1,0:T(8,128)(2,1)S(1)} %get-tuple-element.28), channel_id=1, source_target_pairs={{0,4},{1,5},{2,6},{3,7},{4,0},{5,1},{6,2},{7,3},{8,12},{9,13},{10,... | collective-permute-start | bytes 786440 | tf_op jit(solution)/shard_map/ppermute | solution.py:35
  30.3 8.1 %collective-permute-start.9 = (bf16[32,2048]{1,0:T(8,128)(2,1)S(1)}, bf16[32,2048]{1,0:T(8,128)(2,1)S(1)}, u32[]{:S(2)}, u32[]{:S(2)}) collective-permute-start(bf16[32,2048]{1,0:T(8,128)(2,1)S(1)} %get-tuple-element.22.token_ref.refs_0_), channel_id=1, source_target_pairs={{0,2},{1,3},{2,0},{3,1},{4,6},{5,7},{6,4},{7,5},{8,10},{9,11},{10,... | collective-permute-start | bytes 393224 | tf_op jit(solution)/shard_map/ppermute | solution.py:35
  30.9 9.4 %collective-permute-start.4 = (bf16[32,2048]{1,0:T(8,128)(2,1)S(1)}, bf16[32,2048]{1,0:T(8,128)(2,1)S(1)}, u32[]{:S(2)}, u32[]{:S(2)}) collective-permute-start(bf16[32,2048]{1,0:T(8,128)(2,1)S(1)} %get-tuple-element.22.token_ref.refs_0_), channel_id=1, source_target_pairs={{0,8},{1,9},{2,10},{3,11},{4,12},{5,13},{6,14},{7,15},{8,0},{9,1},... | collective-permute-start | bytes 393224 | tf_op jit(solution)/shard_map/ppermute | solution.py:35
  33.5 12.2 %collective-permute-start.5 = (bf16[32,2048]{1,0:T(8,128)(2,1)S(1)}, bf16[32,2048]{1,0:T(8,128)(2,1)S(1)}, u32[]{:S(2)}, u32[]{:S(2)}) collective-permute-start(bf16[32,2048]{1,0:T(8,128)(2,1)S(1)} %get-tuple-element.22.token_ref.refs_0_), channel_id=1, source_target_pairs={{0,12},{1,13},{2,14},{3,15},{4,8},{5,9},{6,10},{7,11},{8,4},{9,5},... | collective-permute-start | bytes 393224 | tf_op jit(solution)/shard_map/ppermute | solution.py:35
  38.4 10.7 %collective-permute-start.10 = (bf16[2,32,2048]{2,1,0:T(8,128)(2,1)S(1)}, bf16[2,32,2048]{2,1,0:T(8,128)(2,1)S(1)}, u32[]{:S(2)}, u32[]{:S(2)}) collective-permute-start(bf16[2,32,2048]{2,1,0:T(8,128)(2,1)S(1)} %stacked.7.refs_0_), channel_id=1, source_target_pairs={{0,4},{1,5},{2,6},{3,7},{4,0},{5,1},{6,2},{7,3},{8,12},{9,13},{10,... | collective-permute-start | bytes 786440 | tf_op jit(solution)/shard_map/ppermute | solution.py:35
  40.3 14.6 %collective-permute-start.11 = (bf16[2,32,2048]{2,1,0:T(8,128)(2,1)S(1)}, bf16[2,32,2048]{2,1,0:T(8,128)(2,1)S(1)}, u32[]{:S(2)}, u32[]{:S(2)}) collective-permute-start(bf16[2,32,2048]{2,1,0:T(8,128)(2,1)S(1)} %stacked.7.refs_0_), channel_id=1, source_target_pairs={{0,1},{1,0},{2,3},{3,2},{4,5},{5,4},{6,7},{7,6},{8,9},{9,8},{10,11... | collective-permute-start | bytes 786440 | tf_op jit(solution)/shard_map/ppermute | solution.py:35
  45.6 10.8 %collective-permute-start.13 = (bf16[2,32,2048]{2,1,0:T(8,128)(2,1)S(1)}, bf16[2,32,2048]{2,1,0:T(8,128)(2,1)S(1)}, u32[]{:S(2)}, u32[]{:S(2)}) collective-permute-start(bf16[2,32,2048]{2,1,0:T(8,128)(2,1)S(1)} %stacked.6.refs_2_), channel_id=1, source_target_pairs={{0,1},{1,0},{2,3},{3,2},{4,5},{5,4},{6,7},{7,6},{8,9},{9,8},{10,11... | collective-permute-start | bytes 786440 | tf_op jit(solution)/shard_map/ppermute | solution.py:35
  45.7 9.2 %collective-permute-start.8 = (bf16[2,32,2048]{2,1,0:T(8,128)(2,1)S(1)}, bf16[2,32,2048]{2,1,0:T(8,128)(2,1)S(1)}, u32[]{:S(2)}, u32[]{:S(2)}) collective-permute-start(bf16[2,32,2048]{2,1,0:T(8,128)(2,1)S(1)} %stacked.6.refs_2_), channel_id=1, source_target_pairs={{0,2},{1,3},{2,0},{3,1},{4,6},{5,7},{6,4},{7,5},{8,10},{9,11},{10,... | collective-permute-start | bytes 786440 | tf_op jit(solution)/shard_map/ppermute | solution.py:35
  46.4 18.1 %collective-permute-start.16 = (bf16[32,2048]{1,0:T(8,128)(2,1)S(1)}, bf16[32,2048]{1,0:T(8,128)(2,1)S(1)}, u32[]{:S(2)}, u32[]{:S(2)}) collective-permute-start(bf16[32,2048]{1,0:T(8,128)(2,1)S(1)} %get-tuple-element.45), channel_id=1, source_target_pairs={{0,2},{1,3},{2,0},{3,1},{4,6},{5,7},{6,4},{7,5},{8,10},{9,11},{10,... | collective-permute-start | bytes 393224 | tf_op jit(solution)/shard_map/ppermute | solution.py:35
  49.2 15.3 %collective-permute-start.17 = (bf16[32,2048]{1,0:T(8,128)(2,1)S(1)}, bf16[32,2048]{1,0:T(8,128)(2,1)S(1)}, u32[]{:S(2)}, u32[]{:S(2)}) collective-permute-start(bf16[32,2048]{1,0:T(8,128)(2,1)S(1)} %get-tuple-element.42), channel_id=1, source_target_pairs={{0,12},{1,13},{2,14},{3,15},{4,8},{5,9},{6,10},{7,11},{8,4},{9,5},... | collective-permute-start | bytes 393224 | tf_op jit(solution)/shard_map/ppermute | solution.py:35
  54.9 9.5 %collective-permute-start.18 = (bf16[32,2048]{1,0:T(8,128)(2,1)S(1)}, bf16[32,2048]{1,0:T(8,128)(2,1)S(1)}, u32[]{:S(2)}, u32[]{:S(2)}) collective-permute-start(bf16[32,2048]{1,0:T(8,128)(2,1)S(1)} %get-tuple-element.41), channel_id=1, source_target_pairs={{0,8},{1,9},{2,10},{3,11},{4,12},{5,13},{6,14},{7,15},{8,0},{9,1},... | collective-permute-start | bytes 393224 | tf_op jit(solution)/shard_map/ppermute | solution.py:35
  69.0 3.8 %collective-permute-start.21 = (bf16[8,32,2048]{2,1,0:T(8,128)(2,1)S(1)}, bf16[8,32,2048]{2,1,0:T(8,128)(2,1)S(1)}, u32[]{:S(2)}, u32[]{:S(2)}) collective-permute-start(bf16[8,32,2048]{2,1,0:T(8,128)(2,1)S(1)} %get-tuple-element.33), channel_id=1, source_target_pairs={{0,1},{1,0},{2,3},{3,2},{4,5},{5,4},{6,7},{7,6},{8,9},{9,8},{10,11... | collective-permute-start | bytes 3145736 | tf_op jit(solution)/shard_map/ppermute | solution.py:35
  73.0 16.1 %collective-permute-start.22 = (bf16[2,32,2048]{2,1,0:T(8,128)(2,1)S(1)}, bf16[2,32,2048]{2,1,0:T(8,128)(2,1)S(1)}, u32[]{:S(2)}, u32[]{:S(2)}) collective-permute-start(bf16[2,32,2048]{2,1,0:T(8,128)(2,1)S(1)} %get-tuple-element.34), channel_id=1, source_target_pairs={{0,2},{1,3},{2,0},{3,1},{4,6},{5,7},{6,4},{7,5},{8,10},{9,11},{10,... | collective-permute-start | bytes 786440 | tf_op jit(solution)/shard_map/ppermute | solution.py:35
  73.5 16.7 %collective-permute-start.30 = (bf16[2,32,2048]{2,1,0:T(8,128)(2,1)S(1)}, bf16[2,32,2048]{2,1,0:T(8,128)(2,1)S(1)}, u32[]{:S(2)}, u32[]{:S(2)}) collective-permute-start(bf16[2,32,2048]{2,1,0:T(8,128)(2,1)S(1)} %get-tuple-element.36), channel_id=1, source_target_pairs={{0,4},{1,5},{2,6},{3,7},{4,0},{5,1},{6,2},{7,3},{8,12},{9,13},{10,... | collective-permute-start | bytes 786440 | tf_op jit(solution)/shard_map/ppermute | solution.py:35
  73.8 10.7 %collective-permute-start.24 = (bf16[32,2048]{1,0:T(8,128)(2,1)S(1)}, bf16[32,2048]{1,0:T(8,128)(2,1)S(1)}, u32[]{:S(2)}, u32[]{:S(2)}) collective-permute-start(bf16[32,2048]{1,0:T(8,128)(2,1)S(1)} %get-tuple-element.30.high_ref.refs_0_), channel_id=1, source_target_pairs={{0,2},{1,3},{2,0},{3,1},{4,6},{5,7},{6,4},{7,5},{8,10},{9,11},{10,... | collective-permute-start | bytes 393224 | tf_op jit(solution)/shard_map/ppermute | solution.py:35
  75.7 12.0 %collective-permute-start.19 = (bf16[32,2048]{1,0:T(8,128)(2,1)S(1)}, bf16[32,2048]{1,0:T(8,128)(2,1)S(1)}, u32[]{:S(2)}, u32[]{:S(2)}) collective-permute-start(bf16[32,2048]{1,0:T(8,128)(2,1)S(1)} %get-tuple-element.30.high_ref.refs_0_), channel_id=1, source_target_pairs={{0,8},{1,9},{2,10},{3,11},{4,12},{5,13},{6,14},{7,15},{8,0},{9,1},... | collective-permute-start | bytes 393224 | tf_op jit(solution)/shard_map/ppermute | solution.py:35
  77.4 11.7 %collective-permute-start.20 = (bf16[32,2048]{1,0:T(8,128)(2,1)S(1)}, bf16[32,2048]{1,0:T(8,128)(2,1)S(1)}, u32[]{:S(2)}, u32[]{:S(2)}) collective-permute-start(bf16[32,2048]{1,0:T(8,128)(2,1)S(1)} %get-tuple-element.30.high_ref.refs_0_), channel_id=1, source_target_pairs={{0,12},{1,13},{2,14},{3,15},{4,8},{5,9},{6,10},{7,11},{8,4},{9,5},... | collective-permute-start | bytes 393224 | tf_op jit(solution)/shard_map/ppermute | solution.py:35
  84.5 9.5 %collective-permute-start.25 = (bf16[2,32,2048]{2,1,0:T(8,128)(2,1)S(1)}, bf16[2,32,2048]{2,1,0:T(8,128)(2,1)S(1)}, u32[]{:S(2)}, u32[]{:S(2)}) collective-permute-start(bf16[2,32,2048]{2,1,0:T(8,128)(2,1)S(1)} %stacked.10.refs_0_), channel_id=1, source_target_pairs={{0,4},{1,5},{2,6},{3,7},{4,0},{5,1},{6,2},{7,3},{8,12},{9,13},{10,... | collective-permute-start | bytes 786440 | tf_op jit(solution)/shard_map/ppermute | solution.py:35
  87.6 10.8 %collective-permute-start.26 = (bf16[2,32,2048]{2,1,0:T(8,128)(2,1)S(1)}, bf16[2,32,2048]{2,1,0:T(8,128)(2,1)S(1)}, u32[]{:S(2)}, u32[]{:S(2)}) collective-permute-start(bf16[2,32,2048]{2,1,0:T(8,128)(2,1)S(1)} %stacked.10.refs_0_), channel_id=1, source_target_pairs={{0,1},{1,0},{2,3},{3,2},{4,5},{5,4},{6,7},{7,6},{8,9},{9,8},{10,11... | collective-permute-start | bytes 786440 | tf_op jit(solution)/shard_map/ppermute | solution.py:35
  89.1 10.8 %collective-permute-start.28 = (bf16[2,32,2048]{2,1,0:T(8,128)(2,1)S(1)}, bf16[2,32,2048]{2,1,0:T(8,128)(2,1)S(1)}, u32[]{:S(2)}, u32[]{:S(2)}) collective-permute-start(bf16[2,32,2048]{2,1,0:T(8,128)(2,1)S(1)} %stacked.9.refs_2_), channel_id=1, source_target_pairs={{0,1},{1,0},{2,3},{3,2},{4,5},{5,4},{6,7},{7,6},{8,9},{9,8},{10,11... | collective-permute-start | bytes 786440 | tf_op jit(solution)/shard_map/ppermute | solution.py:35
  89.2 9.2 %collective-permute-start.23 = (bf16[2,32,2048]{2,1,0:T(8,128)(2,1)S(1)}, bf16[2,32,2048]{2,1,0:T(8,128)(2,1)S(1)}, u32[]{:S(2)}, u32[]{:S(2)}) collective-permute-start(bf16[2,32,2048]{2,1,0:T(8,128)(2,1)S(1)} %stacked.9.refs_2_), channel_id=1, source_target_pairs={{0,2},{1,3},{2,0},{3,1},{4,6},{5,7},{6,4},{7,5},{8,10},{9,11},{10,... | collective-permute-start | bytes 786440 | tf_op jit(solution)/shard_map/ppermute | solution.py:35
  90.3 17.9 %collective-permute-start.31 = (bf16[32,2048]{1,0:T(8,128)(2,1)S(1)}, bf16[32,2048]{1,0:T(8,128)(2,1)S(1)}, u32[]{:S(2)}, u32[]{:S(2)}) collective-permute-start(bf16[32,2048]{1,0:T(8,128)(2,1)S(1)} %get-tuple-element.43), channel_id=1, source_target_pairs={{0,2},{1,3},{2,0},{3,1},{4,6},{5,7},{6,4},{7,5},{8,10},{9,11},{10,... | collective-permute-start | bytes 393224 | tf_op jit(solution)/shard_map/ppermute | solution.py:35
  94.0 14.2 %collective-permute-start.32 = (bf16[32,2048]{1,0:T(8,128)(2,1)S(1)}, bf16[32,2048]{1,0:T(8,128)(2,1)S(1)}, u32[]{:S(2)}, u32[]{:S(2)}) collective-permute-start(bf16[32,2048]{1,0:T(8,128)(2,1)S(1)} %get-tuple-element.40), channel_id=1, source_target_pairs={{0,12},{1,13},{2,14},{3,15},{4,8},{5,9},{6,10},{7,11},{8,4},{9,5},... | collective-permute-start | bytes 393224 | tf_op jit(solution)/shard_map/ppermute | solution.py:35
  98.4 9.8 %collective-permute-start.33 = (bf16[32,2048]{1,0:T(8,128)(2,1)S(1)}, bf16[32,2048]{1,0:T(8,128)(2,1)S(1)}, u32[]{:S(2)}, u32[]{:S(2)}) collective-permute-start(bf16[32,2048]{1,0:T(8,128)(2,1)S(1)} %get-tuple-element.39), channel_id=1, source_target_pairs={{0,8},{1,9},{2,10},{3,11},{4,12},{5,13},{6,14},{7,15},{8,0},{9,1},... | collective-permute-start | bytes 393224 | tf_op jit(solution)/shard_map/ppermute | solution.py:35
  111.4 4.1 %collective-permute-start.35 = (f32[96,96]{1,0:T(8,128)S(1)}, f32[96,96]{1,0:T(8,128)S(1)}, u32[]{:S(2)}, u32[]{:S(2)}) collective-permute-start(f32[96,96]{1,0:T(8,128)S(1)} %add.45), channel_id=1, source_target_pairs={{0,2},{1,3},{2,0},{3,1},{4,6},{5,7},{6,4},{7,5},{8,10},{9,11},{10,... | collective-permute-start | bytes 110600 | tf_op jit(solution)/shard_map/ppermute | solution.py:35
  115.5 4.5 %collective-permute-start.36 = (f32[96,96]{1,0:T(8,128)S(1)}, f32[96,96]{1,0:T(8,128)S(1)}, u32[]{:S(2)}, u32[]{:S(2)}) collective-permute-start(f32[96,96]{1,0:T(8,128)S(1)} %add.46), channel_id=1, source_target_pairs={{0,4},{1,5},{2,6},{3,7},{4,0},{5,1},{6,2},{7,3},{8,12},{9,13},{10,... | collective-permute-start | bytes 110600 | tf_op jit(solution)/shard_map/ppermute | solution.py:35
  116.8 6.0 %collective-permute-start.37 = (f32[96,96]{1,0:T(8,128)S(1)}, f32[96,96]{1,0:T(8,128)S(1)}, u32[]{:S(2)}, u32[]{:S(2)}) collective-permute-start(f32[96,96]{1,0:T(8,128)S(1)} %add.46), channel_id=1, source_target_pairs={{0,8},{1,9},{2,10},{3,11},{4,12},{5,13},{6,14},{7,15},{8,0},{9,1},... | collective-permute-start | bytes 110600 | tf_op jit(solution)/shard_map/ppermute | solution.py:35
  118.8 5.9 %collective-permute-start.38 = (f32[96,96]{1,0:T(8,128)S(1)}, f32[96,96]{1,0:T(8,128)S(1)}, u32[]{:S(2)}, u32[]{:S(2)}) collective-permute-start(f32[96,96]{1,0:T(8,128)S(1)} %add.46), channel_id=1, source_target_pairs={{0,12},{1,13},{2,14},{3,15},{4,8},{5,9},{6,10},{7,11},{8,4},{9,5},... | collective-permute-start | bytes 110600 | tf_op jit(solution)/shard_map/ppermute | solution.py:35
  (10 other events, 21.8 us)

commit v4 on v3

--- a/solution.py
+++ b/solution.py
@@ -74,8 +74,8 @@
 def gather_orders(count):
     low, shift, wide = stages(count)
     x = 1 << low[-1]
-    early = [[0, x], [1 << shift, 1 << shift | x], [2 << shift, 3 << shift]]
-    late = [[2 << shift | x, 3 << shift | x]]
+    early = [[0, x], [2 << shift, 3 << shift]]
+    late = [[1 << shift, 1 << shift | x], [2 << shift | x, 3 << shift | x]]
     for bit in reversed(low[:-1]):
         early = early + [[offset | 1 << bit for offset in offsets] for offsets in early]
         late = late + [[offset | 1 << bit for offset in offsets] for offsets in late]
@@ -87,13 +87,14 @@
     x = 1 << low[-1]
     fars = [swap(panel, 2 << shift), swap(panel, 3 << shift)]
     pair = stacked([panel, near], tokens[0])
-    early = [pair, swap(pair, 1 << shift), stacked(fars, tokens[1])]
-    late = swap(early[2], x)
+    early = [pair, stacked(fars, tokens[1])]
+    beside = swap(pair, 1 << shift)
+    late = swap(early[1], x)
     for bit in reversed(low[:-1]):
         early = early + [swap(array, 1 << bit) for array in early]
     count = 2 * len(early)
     out = forward(early, 0, None)
-    late = [stacked([late[0], late[1]], out)]
+    late = [stacked([beside[0], beside[1]], out), stacked([late[0], late[1]], out)]
     for bit in reversed(low[:-1]):
         late = late + [swap(array, 1 << bit) for array in late]
     return forward(late, count, out)
@@ -158,12 +159,19 @@
     return total
 
 
+def parted(number, size):
+    if size & (size - 1):
+        return number // size, number % size
+    return lax.shift_right_logical(number, size.bit_length() - 1), number & (size - 1)
+
+
 def tile_place(tile, fixed_ref, list_ref, sizes):
     count, capacity, tiles, tile_size = sizes
     me = fixed_ref[0]
     slot = fixed_ref[1 + 2 * count + tiles + tile]
-    offset = (slot // capacity) ^ me
-    block = list_ref[fixed_ref[1 + count + offset], me * capacity + slot % capacity]
+    sender, within = parted(slot, capacity)
+    offset = sender ^ me
+    block = list_ref[fixed_ref[1 + count + offset], me * capacity + within]
     row = fixed_ref[1 + 2 * count + tile]
     own = pl.ds(pl.multiple_of(row * tile_size, tile_size), tile_size)
     other = pl.ds(pl.multiple_of(block * tile_size, tile_size), tile_size)
@@ -242,8 +250,9 @@
     def one(tile, found):
         front, back = found
         slot = fixed_ref[1 + 2 * count + tiles + tile]
-        offset = (slot // capacity) ^ me
-        block = list_ref[fixed_ref[1 + count + offset], me * capacity + slot % capacity]
+        sender, within = parted(slot, capacity)
+        offset = sender ^ me
+        block = list_ref[fixed_ref[1 + count + offset], me * capacity + within]
         piece = fixed_ref[1 + 2 * count + 2 * tiles + offset]
         first = piece < early
         place = jnp.where(first, front, back)
@@ -268,7 +277,9 @@
         for u in range(8):
             at = start + step * 8 + u
             packed = plan_ref[jnp.minimum(at, tiles - 1)]
-            block, row, piece, tile = packed % 16, packed // 16 % 16, packed // 256 % 256, packed // 65536
+            rest, block = parted(packed, 16)
+            rest, row = parted(rest, 16)
+            tile, piece = parted(rest, 256)
             piece = jnp.clip(piece - base, 0, groups * 2 - 1)
             own = pl.ds(pl.multiple_of(row * tile_size, tile_size), tile_size)
             other = pl.ds(pl.multiple_of(block * tile_size, tile_size), tile_size)
@@ -342,12 +353,34 @@
     panels_ref[:width] = start_ref[...]
     panels_ref[width : 2 * width] = first_ref[...]
     panels_ref[2 * width :] = second
-    gram_ref[...] = product_t(panels_ref[...], panels_ref[...])
+    gram = product_t(panels_ref[...], panels_ref[...])
+
+    def block(row, column):
+        return gram[row * width : (row + 1) * width, column * width : (column + 1) * width]
+
+    gram_ref[:width] = jnp.concatenate([block(0, 0), block(1, 0), block(1, 1), block(2, 0)], axis=1)
+    half = width // 2
+    others = [part for of in (block(2, 1), block(2, 2)) for part in (of[:half], of[half:])]
+    gram_ref[width:] = jnp.concatenate(others, axis=1)
 
 
 def last_kernel(gram_ref, panels_ref, out_ref, couplings_ref, factors_ref, *, scale):
     width = out_ref.shape[0]
-    factor, inverse = factor_of(gram_ref[...])
+    def sent(place):
+        return gram_ref[:width, place * width : (place + 1) * width]
+
+    def halves(place):
+        return jnp.concatenate([gram_ref[width:, at * width : (at + 1) * width] for at in (place, place + 1)], axis=0)
+
+    gram = jnp.concatenate(
+        [
+            jnp.concatenate([sent(0), sent(1).T, sent(3).T], axis=1),
+            jnp.concatenate([sent(1), sent(2), halves(0).T], axis=1),
+            jnp.concatenate([sent(3), halves(0), halves(2)], axis=1),
+        ],
+        axis=0,
+    )
+    factor, inverse = factor_of(gram)
     out_ref[...] = product(inverse[2 * width :] * scale, panels_ref[...])
 
     def block(of, row, column):
@@ -456,14 +489,14 @@
         near = swap(high, 1 << stages(count)[0][-1])
         kept, over_x, over_z = reduce_panels(*sums(high))
         terms = finish_panels(kept, over_x, over_z)
-        return [gather_panels(high, near, (kept, over_x), forward)] + terms
+        return [gather_panels(high, near, (kept, kept), forward)] + terms
 
     terms = applied(high, first_sums)
     first, high, low = call(combine_kernel, (panel, half, half), links, start_panel, *terms, name="combine")
     terms = applied(high, functools.partial(backward, high, low))
     all_panels = (ITERS + 1) * width
     panels, gram = call(
-        gram_kernel, (shape((all_panels, here), f32), shape((all_panels, all_panels), f32)), links, start_panel, first, *terms, name="gram"
+        gram_kernel, (shape((all_panels, here), f32), shape((width + width // 2, 4 * width), f32)), links, start_panel, first, *terms, name="gram"
     )
     both = shape((ITERS, width, width), f32)
     return call(

time: 129 us -> 126 us (0.977)
  waiting for transfers between devices: 46.9 us -> 40.3 us
  starting transfers between devices: 43.1 us -> 47.4 us
    ppermute x39, waiting for transfers between devices: 46.9 us -> 40.3 us  [swap(): lax.ppermute(array, 'rows', [(place, place ^ offset) for place in range(c...]
    ppermute x39, starting transfers between devices: 43.1 us -> 47.4 us  [swap(): lax.ppermute(array, 'rows', [(place, place ^ offset) for place in range(c...]
    pallas_call x21 -> x23, Pallas kernels: 25.2 us -> 25.5 us  [call(): pl.pallas_call(kernel, out_shape=out, in_specs=specs or [VMEM] * len(args...]
  transfers between devices with their start and end apart: 39 -> 39, of which waited for: 21 -> 17; matrix products, arithmetic and copies ran while one was open for 1% -> 1% of each run, Pallas kernels for 18% -> 18%
where the time goes in v4:
time: 126 us
  starting transfers between devices  47.4 us (38%)
  waiting for transfers between devices  40.3 us (32%)
  Pallas kernels  34.8 us (28%)
  local copies, waits for them, and re-layouts  2.33 us (2%)
    ppermute x39, starting transfers between devices, swap(): lax.ppermute(array, 'rows', [(place, place ^ offset) for place in range(c...  47.4 us
    ppermute x39, waiting for transfers between devices, swap(): lax.ppermute(array, 'rows', [(place, place ^ offset) for place in range(c...  40.3 us
    pallas_call x23, Pallas kernels, call(): pl.pallas_call(kernel, out_shape=out, in_specs=specs or [VMEM] * len(args...  25.5 us
    pallas_call x1, Pallas kernels, first_products(): pl.pallas_call(products_kernel, out_shape=(shape((tiles, width, tile_size...  6.35 us
    pallas_call x1, Pallas kernels, on_device(): pl.pallas_call(functools.partial(plan_kernel, sizes=sizes, early=early_pi...  2.92 us
  transfers between devices with their start and end apart: 39, of which 17 were waited for; matrix products, arithmetic and copies ran while one was open for 1% of the time, Pallas kernels for 18%

profile of v4, /device:TPU:0, one launch (start us, length us, event | category | flops | bytes accessed | tf_op | source)
XLA Modules:
  0.0 126.1 jit_solution(11702403503654041215)
XLA Ops:
  1.4 4.0 %collective-permute-start = (s32[1,256]{1,0:T(1,128)S(1)}, s32[1,256]{1,0:T(1,128)S(1)}, u32[]{:S(2)}, u32[]{:S(2)}) collective-permute-start(s32[1,256]{1,0:T(1,128)S(1)} %reshape.31.near_ref), channel_id=1, source_target_pairs={{0,8},{1,9},{2,10},{3,11},{4,12},{5,13},{6,14},{7,15},{8,0},{9,1},... | collective-permute-start | bytes 3080 | tf_op jit(solution)/shard_map/ppermute | solution.py:35
  7.0 1.9 %collective-permute-start.1 = (s32[2,256]{1,0:T(2,128)S(1)}, s32[2,256]{1,0:T(2,128)S(1)}, u32[]{:S(2)}, u32[]{:S(2)}) collective-permute-start(s32[2,256]{1,0:T(2,128)S(1)} %joined.4.near_ref.token_ref), channel_id=1, source_target_pairs={{0,4},{1,5},{2,6},{3,7},{4,0},{5,1},{6,2},{7,3},{8,12},{9,13},{10,... | collective-permute-start | bytes 6152 | tf_op jit(solution)/shard_map/ppermute | solution.py:35
  8.9 1.7 %collective-permute-done.1.far_ref = s32[2,256]{1,0:T(2,128)S(1)} collective-permute-done((s32[2,256]{1,0:T(2,128)S(1)}, s32[2,256]{1,0:T(2,128)S(1)}, u32[]{:S(2)}, u32[]{:S(2)}) %collective-permute-start.1) | collective-permute-done | bytes 2080 | tf_op jit(solution)/shard_map/ppermute | solution.py:35
  10.6 1.8 %collective-permute-start.2 = (s32[4,256]{1,0:T(4,128)S(1)}, s32[4,256]{1,0:T(4,128)S(1)}, u32[]{:S(2)}, u32[]{:S(2)}) collective-permute-start(s32[4,256]{1,0:T(4,128)S(1)} %joined.5.near_ref), channel_id=1, source_target_pairs={{0,2},{1,3},{2,0},{3,1},{4,6},{5,7},{6,4},{7,5},{8,10},{9,11},{10,... | collective-permute-start | bytes 12296 | tf_op jit(solution)/shard_map/ppermute | solution.py:35
  14.9 6.3 %products.1 = (f32[96,32,256]{2,1,0:T(8,128)S(1)}, bf16[96,256,256]{2,1,0:T(8,128)(2,1)S(1)}, bf16[32,2048]{1,0:T(8,128)(2,1)S(1)}, bf16[32,2048]{1,0:T(8,128)(2,1)}) custom-call(s32[96]{0:T(128)S(1)} %copy-done.2, f32[32,2048]{1,0:T(8,128)} %start_ref.3, bf16[96,256,256]{2,1,0:T(8,128)(2,1)} %tiles_ref.1, s32[2,256]{1,0:T(2,128)S(1)} %joined.4.near_ref.token_ref), custom_call_target="tpu_custom_call" | custom-call | flops 402653184 | bytes 1024 | tf_op jit(solution)/shard_map/products/pallas_call | solution.py:430
  21.2 2.1 %sums.1 = (f32[8,32,2048]{2,1,0:T(8,128)S(1)}, bf16[8,32,2048]{2,1,0:T(8,128)(2,1)S(1)}) custom-call(s32[241]{0:T(256)S(1)} %concatenate.3.fixed_ref, s32[16,256]{1,0:T(8,128)S(1)} %joined.7.list_ref, f32[96,32,256]{2,1,0:T(8,128)S(1)} %get-tuple-element.23.products_ref, bf16[32,2048]{1,0:T(8,128)(2,1)S(1)} %get-tuple-element.22.token_ref.refs_0_), custom_call_target="tpu_custom_call" | custom-call | flops 402653184 | bytes 1024 | tf_op jit(solution)/shard_map/sums/pallas_call | solution.py:404
  23.9 2.3 %collective-permute-done.5.arrived_ref = bf16[8,32,2048]{2,1,0:T(8,128)(2,1)S(1)} collective-permute-done((bf16[8,32,2048]{2,1,0:T(8,128)(2,1)S(1)}, bf16[8,32,2048]{2,1,0:T(8,128)(2,1)S(1)}, u32[]{:S(2)}, u32[]{:S(2)}) %collective-permute-start.5) | collective-permute-done | bytes 1048608 | tf_op jit(solution)/shard_map/ppermute | solution.py:35
  26.4 2.0 %collective-permute-start.14 = (bf16[2,32,2048]{2,1,0:T(8,128)(2,1)S(1)}, bf16[2,32,2048]{2,1,0:T(8,128)(2,1)S(1)}, u32[]{:S(2)}, u32[]{:S(2)}) collective-permute-start(bf16[2,32,2048]{2,1,0:T(8,128)(2,1)S(1)} %get-tuple-element.27), channel_id=1, source_target_pairs={{0,4},{1,5},{2,6},{3,7},{4,0},{5,1},{6,2},{7,3},{8,12},{9,13},{10,... | collective-permute-start | bytes 786440 | tf_op jit(solution)/shard_map/ppermute | solution.py:35
  29.9 2.6 %collective-permute-start.7 = (bf16[32,2048]{1,0:T(8,128)(2,1)S(1)}, bf16[32,2048]{1,0:T(8,128)(2,1)S(1)}, u32[]{:S(2)}, u32[]{:S(2)}) collective-permute-start(bf16[32,2048]{1,0:T(8,128)(2,1)S(1)} %get-tuple-element.22.token_ref.refs_0_), channel_id=1, source_target_pairs={{0,8},{1,9},{2,10},{3,11},{4,12},{5,13},{6,14},{7,15},{8,0},{9,1},... | collective-permute-start | bytes 393224 | tf_op jit(solution)/shard_map/ppermute | solution.py:35
  33.0 2.9 %plan.1.plan_ref = s32[97]{0:T(128)S(1)} custom-call(s32[241]{0:T(256)S(1)} %concatenate.3.fixed_ref, s32[16,256]{1,0:T(8,128)S(1)} %joined.7.list_ref), custom_call_target="tpu_custom_call" | custom-call | tf_op jit(solution)/shard_map/plan/pallas_call | solution.py:472
  36.0 1.9 %collective-permute-done.7.refs_0_ = bf16[32,2048]{1,0:T(8,128)(2,1)S(1)} collective-permute-done((bf16[32,2048]{1,0:T(8,128)(2,1)S(1)}, bf16[32,2048]{1,0:T(8,128)(2,1)S(1)}, u32[]{:S(2)}, u32[]{:S(2)}) %collective-permute-start.7) | collective-permute-done | bytes 131104 | tf_op jit(solution)/shard_map/ppermute | solution.py:35
  37.9 5.2 %collective-permute-done.8.refs_1_ = bf16[32,2048]{1,0:T(8,128)(2,1)S(1)} collective-permute-done((bf16[32,2048]{1,0:T(8,128)(2,1)S(1)}, bf16[32,2048]{1,0:T(8,128)(2,1)S(1)}, u32[]{:S(2)}, u32[]{:S(2)}) %collective-permute-start.8) | collective-permute-done | bytes 131104 | tf_op jit(solution)/shard_map/ppermute | solution.py:35
  47.7 2.5 %collective-permute-start.17 = (bf16[32,2048]{1,0:T(8,128)(2,1)S(1)}, bf16[32,2048]{1,0:T(8,128)(2,1)S(1)}, u32[]{:S(2)}, u32[]{:S(2)}) collective-permute-start(bf16[32,2048]{1,0:T(8,128)(2,1)S(1)} %get-tuple-element.42), channel_id=1, source_target_pairs={{0,12},{1,13},{2,14},{3,15},{4,8},{5,9},{6,10},{7,11},{8,4},{9,5},... | collective-permute-start | bytes 393224 | tf_op jit(solution)/shard_map/ppermute | solution.py:35
  50.2 4.1 %early.2.refs_2_.refs_4_ = f32[32,2048]{1,0:T(8,128)S(1)} custom-call(s32[97]{0:T(128)S(1)} %plan.1.plan_ref, bf16[96,256,256]{2,1,0:T(8,128)(2,1)S(1)} %get-tuple-element.21.tiles_ref, bf16[2,32,2048]{2,1,0:T(8,128)(2,1)S(1)} %stacked.8.refs_0_, bf16[2,32,2048]{2,1,0:T(8,128)(2,1)S(1)} %stacked.9.refs_1_, ...), custom_call_target="tpu_custom_call" | custom-call | flops 402653184 | bytes 1024 | tf_op jit(solution)/shard_map/early/pallas_call | solution.py:404
  54.4 3.8 %collective-permute-done.6 = bf16[2,32,2048]{2,1,0:T(8,128)(2,1)S(1)} collective-permute-done((bf16[2,32,2048]{2,1,0:T(8,128)(2,1)S(1)}, bf16[2,32,2048]{2,1,0:T(8,128)(2,1)S(1)}, u32[]{:S(2)}, u32[]{:S(2)}) %collective-permute-start.6) | collective-permute-done | bytes 262176 | tf_op jit(solution)/shard_map/ppermute | solution.py:35
  59.8 2.4 %late.2.forward_ref = f32[32,2048]{1,0:T(8,128)S(1)} custom-call(s32[97]{0:T(128)S(1)} %plan.1.plan_ref, bf16[96,256,256]{2,1,0:T(8,128)(2,1)S(1)} %get-tuple-element.21.tiles_ref, bf16[2,32,2048]{2,1,0:T(8,128)(2,1)S(1)} %stacked.10.refs_0_, bf16[2,32,2048]{2,1,0:T(8,128)(2,1)S(1)} %stacked.11.refs_1_, ...), custom_call_target="tpu_custom_call" | custom-call | flops 402653184 | bytes 1024 | tf_op jit(solution)/shard_map/late/pallas_call | solution.py:404
  62.4 4.3 %backward.1 = (f32[8,32,2048]{2,1,0:T(8,128)S(1)}, bf16[8,32,2048]{2,1,0:T(8,128)(2,1)S(1)}) custom-call(s32[241]{0:T(256)S(1)} %concatenate.3.fixed_ref, s32[16,256]{1,0:T(8,128)S(1)} %joined.7.list_ref, bf16[32,2048]{1,0:T(8,128)(2,1)S(1)} %get-tuple-element.30.high_ref.refs_0_, bf16[32,2048]{1,0:T(8,128)(2,1)S(1)} %get-tuple-element.31.low_ref, ...), custom_call_target="tpu_custom_call" | custom-call | flops 402653184 | bytes 1024 | tf_op jit(solution)/shard_map/backward/pallas_call | solution.py:404
  67.8 2.3 %collective-permute-done.20.arrived_ref = bf16[8,32,2048]{2,1,0:T(8,128)(2,1)S(1)} collective-permute-done((bf16[8,32,2048]{2,1,0:T(8,128)(2,1)S(1)}, bf16[8,32,2048]{2,1,0:T(8,128)(2,1)S(1)}, u32[]{:S(2)}, u32[]{:S(2)}) %collective-permute-start.20) | collective-permute-done | bytes 1048608 | tf_op jit(solution)/shard_map/ppermute | solution.py:35
  70.5 3.3 %collective-permute-start.31 = (bf16[2,32,2048]{2,1,0:T(8,128)(2,1)S(1)}, bf16[2,32,2048]{2,1,0:T(8,128)(2,1)S(1)}, u32[]{:S(2)}, u32[]{:S(2)}) collective-permute-start(bf16[2,32,2048]{2,1,0:T(8,128)(2,1)S(1)} %get-tuple-element.36), channel_id=1, source_target_pairs={{0,2},{1,3},{2,0},{3,1},{4,6},{5,7},{6,4},{7,5},{8,10},{9,11},{10,... | collective-permute-start | bytes 786440 | tf_op jit(solution)/shard_map/ppermute | solution.py:35
  75.3 2.7 %collective-permute-start.23 = (bf16[32,2048]{1,0:T(8,128)(2,1)S(1)}, bf16[32,2048]{1,0:T(8,128)(2,1)S(1)}, u32[]{:S(2)}, u32[]{:S(2)}) collective-permute-start(bf16[32,2048]{1,0:T(8,128)(2,1)S(1)} %get-tuple-element.30.high_ref.refs_0_), channel_id=1, source_target_pairs={{0,12},{1,13},{2,14},{3,15},{4,8},{5,9},{6,10},{7,11},{8,4},{9,5},... | collective-permute-start | bytes 393224 | tf_op jit(solution)/shard_map/ppermute | solution.py:35
  78.0 8.6 %collective-permute-done.22.refs_0_ = bf16[32,2048]{1,0:T(8,128)(2,1)S(1)} collective-permute-done((bf16[32,2048]{1,0:T(8,128)(2,1)S(1)}, bf16[32,2048]{1,0:T(8,128)(2,1)S(1)}, u32[]{:S(2)}, u32[]{:S(2)}) %collective-permute-start.22) | collective-permute-done | bytes 131104 | tf_op jit(solution)/shard_map/ppermute | solution.py:35
  87.6 2.1 %collective-permute-start.21 = (bf16[2,32,2048]{2,1,0:T(8,128)(2,1)S(1)}, bf16[2,32,2048]{2,1,0:T(8,128)(2,1)S(1)}, u32[]{:S(2)}, u32[]{:S(2)}) collective-permute-start(bf16[2,32,2048]{2,1,0:T(8,128)(2,1)S(1)} %stacked.12.refs_0_), channel_id=1, source_target_pairs={{0,4},{1,5},{2,6},{3,7},{4,0},{5,1},{6,2},{7,3},{8,12},{9,13},{10,... | collective-permute-start | bytes 786440 | tf_op jit(solution)/shard_map/ppermute | solution.py:35
  89.8 1.7 %collective-permute-start.30 = (bf16[32,2048]{1,0:T(8,128)(2,1)S(1)}, bf16[32,2048]{1,0:T(8,128)(2,1)S(1)}, u32[]{:S(2)}, u32[]{:S(2)}) collective-permute-start(bf16[32,2048]{1,0:T(8,128)(2,1)S(1)} %get-tuple-element.43), channel_id=1, source_target_pairs={{0,2},{1,3},{2,0},{3,1},{4,6},{5,7},{6,4},{7,5},{8,10},{9,11},{10,... | collective-permute-start | bytes 393224 | tf_op jit(solution)/shard_map/ppermute | solution.py:35
  93.0 4.1 %early.3.refs_2_.refs_4_ = f32[32,2048]{1,0:T(8,128)S(1)} custom-call(s32[97]{0:T(128)S(1)} %plan.1.plan_ref, bf16[96,256,256]{2,1,0:T(8,128)(2,1)S(1)} %get-tuple-element.21.tiles_ref, bf16[2,32,2048]{2,1,0:T(8,128)(2,1)S(1)} %stacked.12.refs_0_, bf16[2,32,2048]{2,1,0:T(8,128)(2,1)S(1)} %stacked.13.refs_1_, ...), custom_call_target="tpu_custom_call" | custom-call | flops 402653184 | bytes 1024 | tf_op jit(solution)/shard_map/early/pallas_call | solution.py:404
  99.2 2.5 %late.3.forward_ref = f32[32,2048]{1,0:T(8,128)S(1)} custom-call(s32[97]{0:T(128)S(1)} %plan.1.plan_ref, bf16[96,256,256]{2,1,0:T(8,128)(2,1)S(1)} %get-tuple-element.21.tiles_ref, bf16[2,32,2048]{2,1,0:T(8,128)(2,1)S(1)} %stacked.14.refs_0_, bf16[2,32,2048]{2,1,0:T(8,128)(2,1)S(1)} %stacked.15.refs_1_, ...), custom_call_target="tpu_custom_call" | custom-call | flops 402653184 | bytes 1024 | tf_op jit(solution)/shard_map/late/pallas_call | solution.py:404
  101.7 3.2 %collective-permute-done.33.refs_4_ = bf16[32,2048]{1,0:T(8,128)(2,1)S(1)} collective-permute-done((bf16[32,2048]{1,0:T(8,128)(2,1)S(1)}, bf16[32,2048]{1,0:T(8,128)(2,1)S(1)}, u32[]{:S(2)}, u32[]{:S(2)}) %collective-permute-start.33) | collective-permute-done | bytes 131104 | tf_op jit(solution)/shard_map/ppermute | solution.py:35
  107.1 5.4 %collective-permute-start.35 = (f32[48,128]{1,0:T(8,128)S(1)}, f32[48,128]{1,0:T(8,128)S(1)}, u32[]{:S(2)}, u32[]{:S(2)}) collective-permute-start(f32[48,128]{1,0:T(8,128)S(1)} %add.45), channel_id=1, source_target_pairs={{0,2},{1,3},{2,0},{3,1},{4,6},{5,7},{6,4},{7,5},{8,10},{9,11},{10,... | collective-permute-start | bytes 73736 | tf_op jit(solution)/shard_map/ppermute | solution.py:35
  112.5 1.8 %collective-permute-done.35 = f32[48,128]{1,0:T(8,128)S(1)} collective-permute-done((f32[48,128]{1,0:T(8,128)S(1)}, f32[48,128]{1,0:T(8,128)S(1)}, u32[]{:S(2)}, u32[]{:S(2)}) %collective-permute-start.35) | collective-permute-done | bytes 24608 | tf_op jit(solution)/shard_map/ppermute | solution.py:35
  114.3 1.7 %collective-permute-start.37 = (f32[48,128]{1,0:T(8,128)S(1)}, f32[48,128]{1,0:T(8,128)S(1)}, u32[]{:S(2)}, u32[]{:S(2)}) collective-permute-start(f32[48,128]{1,0:T(8,128)S(1)} %add.46), channel_id=1, source_target_pairs={{0,8},{1,9},{2,10},{3,11},{4,12},{5,13},{6,14},{7,15},{8,0},{9,1},... | collective-permute-start | bytes 73736 | tf_op jit(solution)/shard_map/ppermute | solution.py:35
  116.1 2.6 %collective-permute-start.38 = (f32[48,128]{1,0:T(8,128)S(1)}, f32[48,128]{1,0:T(8,128)S(1)}, u32[]{:S(2)}, u32[]{:S(2)}) collective-permute-start(f32[48,128]{1,0:T(8,128)S(1)} %add.46), channel_id=1, source_target_pairs={{0,12},{1,13},{2,14},{3,15},{4,8},{5,9},{6,10},{7,11},{8,4},{9,5},... | collective-permute-start | bytes 73736 | tf_op jit(solution)/shard_map/ppermute | solution.py:35
  119.4 2.3 %collective-permute-done.38 = f32[48,128]{1,0:T(8,128)S(1)} collective-permute-done((f32[48,128]{1,0:T(8,128)S(1)}, f32[48,128]{1,0:T(8,128)S(1)}, u32[]{:S(2)}, u32[]{:S(2)}) %collective-permute-start.38) | collective-permute-done | bytes 24608 | tf_op jit(solution)/shard_map/ppermute | solution.py:35
  121.7 4.4 %last.1 = (f32[32,2048]{1,0:T(8,128)}, f32[2,32,32]{2,1,0:T(8,128)}, f32[2,32,32]{2,1,0:T(8,128)}) custom-call(f32[48,128]{1,0:T(8,128)S(1)} %add_add_fusion.gram_ref, f32[96,2048]{1,0:T(8,128)S(1)} %get-tuple-element.38.panels_ref), custom_call_target="tpu_custom_call" | custom-call | tf_op jit(solution)/shard_map/last/pallas_call | solution.py:404
  (90 shorter events, 24.4 us)
Async XLA Ops:
  1.4 5.6 %collective-permute-start = (s32[1,256]{1,0:T(1,128)S(1)}, s32[1,256]{1,0:T(1,128)S(1)}, u32[]{:S(2)}, u32[]{:S(2)}) collective-permute-start(s32[1,256]{1,0:T(1,128)S(1)} %reshape.31.near_ref), channel_id=1, source_target_pairs={{0,8},{1,9},{2,10},{3,11},{4,12},{5,13},{6,14},{7,15},{8,0},{9,1},... | collective-permute-start | bytes 3080 | tf_op jit(solution)/shard_map/ppermute | solution.py:35
  10.6 3.6 %collective-permute-start.2 = (s32[4,256]{1,0:T(4,128)S(1)}, s32[4,256]{1,0:T(4,128)S(1)}, u32[]{:S(2)}, u32[]{:S(2)}) collective-permute-start(s32[4,256]{1,0:T(4,128)S(1)} %joined.5.near_ref), channel_id=1, source_target_pairs={{0,2},{1,3},{2,0},{3,1},{4,6},{5,7},{6,4},{7,5},{8,10},{9,11},{10,... | collective-permute-start | bytes 12296 | tf_op jit(solution)/shard_map/ppermute | solution.py:35
  14.2 7.0 %collective-permute-start.3 = (s32[8,256]{1,0:T(8,128)S(1)}, s32[8,256]{1,0:T(8,128)S(1)}, u32[]{:S(2)}, u32[]{:S(2)}) collective-permute-start(s32[8,256]{1,0:T(8,128)S(1)} %joined.6.near_ref), channel_id=1, source_target_pairs={{0,1},{1,0},{2,3},{3,2},{4,5},{5,4},{6,7},{7,6},{8,9},{9,8},{10,11... | collective-permute-start | bytes 24584 | tf_op jit(solution)/shard_map/ppermute | solution.py:35
  26.4 18.7 %collective-permute-start.14 = (bf16[2,32,2048]{2,1,0:T(8,128)(2,1)S(1)}, bf16[2,32,2048]{2,1,0:T(8,128)(2,1)S(1)}, u32[]{:S(2)}, u32[]{:S(2)}) collective-permute-start(bf16[2,32,2048]{2,1,0:T(8,128)(2,1)S(1)} %get-tuple-element.27), channel_id=1, source_target_pairs={{0,4},{1,5},{2,6},{3,7},{4,0},{5,1},{6,2},{7,3},{8,12},{9,13},{10,... | collective-permute-start | bytes 786440 | tf_op jit(solution)/shard_map/ppermute | solution.py:35
  28.4 17.6 %collective-permute-start.16 = (bf16[2,32,2048]{2,1,0:T(8,128)(2,1)S(1)}, bf16[2,32,2048]{2,1,0:T(8,128)(2,1)S(1)}, u32[]{:S(2)}, u32[]{:S(2)}) collective-permute-start(bf16[2,32,2048]{2,1,0:T(8,128)(2,1)S(1)} %get-tuple-element.28), channel_id=1, source_target_pairs={{0,2},{1,3},{2,0},{3,1},{4,6},{5,7},{6,4},{7,5},{8,10},{9,11},{10,... | collective-permute-start | bytes 786440 | tf_op jit(solution)/shard_map/ppermute | solution.py:35
  29.9 8.0 %collective-permute-start.7 = (bf16[32,2048]{1,0:T(8,128)(2,1)S(1)}, bf16[32,2048]{1,0:T(8,128)(2,1)S(1)}, u32[]{:S(2)}, u32[]{:S(2)}) collective-permute-start(bf16[32,2048]{1,0:T(8,128)(2,1)S(1)} %get-tuple-element.22.token_ref.refs_0_), channel_id=1, source_target_pairs={{0,8},{1,9},{2,10},{3,11},{4,12},{5,13},{6,14},{7,15},{8,0},{9,1},... | collective-permute-start | bytes 393224 | tf_op jit(solution)/shard_map/ppermute | solution.py:35
  32.5 10.7 %collective-permute-start.8 = (bf16[32,2048]{1,0:T(8,128)(2,1)S(1)}, bf16[32,2048]{1,0:T(8,128)(2,1)S(1)}, u32[]{:S(2)}, u32[]{:S(2)}) collective-permute-start(bf16[32,2048]{1,0:T(8,128)(2,1)S(1)} %get-tuple-element.22.token_ref.refs_0_), channel_id=1, source_target_pairs={{0,12},{1,13},{2,14},{3,15},{4,8},{5,9},{6,10},{7,11},{8,4},{9,5},... | collective-permute-start | bytes 393224 | tf_op jit(solution)/shard_map/ppermute | solution.py:35
  32.7 12.1 %collective-permute-start.4 = (bf16[32,2048]{1,0:T(8,128)(2,1)S(1)}, bf16[32,2048]{1,0:T(8,128)(2,1)S(1)}, u32[]{:S(2)}, u32[]{:S(2)}) collective-permute-start(bf16[32,2048]{1,0:T(8,128)(2,1)S(1)} %get-tuple-element.22.token_ref.refs_0_), channel_id=1, source_target_pairs={{0,2},{1,3},{2,0},{3,1},{4,6},{5,7},{6,4},{7,5},{8,10},{9,11},{10,... | collective-permute-start | bytes 393224 | tf_op jit(solution)/shard_map/ppermute | solution.py:35
  43.2 4.5 %collective-permute-start.10 = (bf16[2,32,2048]{2,1,0:T(8,128)(2,1)S(1)}, bf16[2,32,2048]{2,1,0:T(8,128)(2,1)S(1)}, u32[]{:S(2)}, u32[]{:S(2)}) collective-permute-start(bf16[2,32,2048]{2,1,0:T(8,128)(2,1)S(1)} %stacked.9.refs_1_), channel_id=1, source_target_pairs={{0,1},{1,0},{2,3},{3,2},{4,5},{5,4},{6,7},{7,6},{8,9},{9,8},{10,11... | collective-permute-start | bytes 786440 | tf_op jit(solution)/shard_map/ppermute | solution.py:35
  43.3 11.0 %collective-permute-start.11 = (bf16[2,32,2048]{2,1,0:T(8,128)(2,1)S(1)}, bf16[2,32,2048]{2,1,0:T(8,128)(2,1)S(1)}, u32[]{:S(2)}, u32[]{:S(2)}) collective-permute-start(bf16[2,32,2048]{2,1,0:T(8,128)(2,1)S(1)} %stacked.9.refs_1_), channel_id=1, source_target_pairs={{0,2},{1,3},{2,0},{3,1},{4,6},{5,7},{6,4},{7,5},{8,10},{9,11},{10,... | collective-permute-start | bytes 786440 | tf_op jit(solution)/shard_map/ppermute | solution.py:35
  44.8 5.3 %collective-permute-start.9 = (bf16[2,32,2048]{2,1,0:T(8,128)(2,1)S(1)}, bf16[2,32,2048]{2,1,0:T(8,128)(2,1)S(1)}, u32[]{:S(2)}, u32[]{:S(2)}) collective-permute-start(bf16[2,32,2048]{2,1,0:T(8,128)(2,1)S(1)} %stacked.8.refs_0_), channel_id=1, source_target_pairs={{0,1},{1,0},{2,3},{3,2},{4,5},{5,4},{6,7},{7,6},{8,9},{9,8},{10,11... | collective-permute-start | bytes 786440 | tf_op jit(solution)/shard_map/ppermute | solution.py:35
  45.1 13.1 %collective-permute-start.6 = (bf16[2,32,2048]{2,1,0:T(8,128)(2,1)S(1)}, bf16[2,32,2048]{2,1,0:T(8,128)(2,1)S(1)}, u32[]{:S(2)}, u32[]{:S(2)}) collective-permute-start(bf16[2,32,2048]{2,1,0:T(8,128)(2,1)S(1)} %stacked.8.refs_0_), channel_id=1, source_target_pairs={{0,4},{1,5},{2,6},{3,7},{4,0},{5,1},{6,2},{7,3},{8,12},{9,13},{10,... | collective-permute-start | bytes 786440 | tf_op jit(solution)/shard_map/ppermute | solution.py:35
  46.1 16.1 %collective-permute-start.15 = (bf16[32,2048]{1,0:T(8,128)(2,1)S(1)}, bf16[32,2048]{1,0:T(8,128)(2,1)S(1)}, u32[]{:S(2)}, u32[]{:S(2)}) collective-permute-start(bf16[32,2048]{1,0:T(8,128)(2,1)S(1)} %get-tuple-element.45), channel_id=1, source_target_pairs={{0,2},{1,3},{2,0},{3,1},{4,6},{5,7},{6,4},{7,5},{8,10},{9,11},{10,... | collective-permute-start | bytes 393224 | tf_op jit(solution)/shard_map/ppermute | solution.py:35
  47.7 14.5 %collective-permute-start.17 = (bf16[32,2048]{1,0:T(8,128)(2,1)S(1)}, bf16[32,2048]{1,0:T(8,128)(2,1)S(1)}, u32[]{:S(2)}, u32[]{:S(2)}) collective-permute-start(bf16[32,2048]{1,0:T(8,128)(2,1)S(1)} %get-tuple-element.42), channel_id=1, source_target_pairs={{0,12},{1,13},{2,14},{3,15},{4,8},{5,9},{6,10},{7,11},{8,4},{9,5},... | collective-permute-start | bytes 393224 | tf_op jit(solution)/shard_map/ppermute | solution.py:35
  50.2 12.1 %collective-permute-start.18 = (bf16[32,2048]{1,0:T(8,128)(2,1)S(1)}, bf16[32,2048]{1,0:T(8,128)(2,1)S(1)}, u32[]{:S(2)}, u32[]{:S(2)}) collective-permute-start(bf16[32,2048]{1,0:T(8,128)(2,1)S(1)} %get-tuple-element.41), channel_id=1, source_target_pairs={{0,8},{1,9},{2,10},{3,11},{4,12},{5,13},{6,14},{7,15},{8,0},{9,1},... | collective-permute-start | bytes 393224 | tf_op jit(solution)/shard_map/ppermute | solution.py:35
  54.3 4.0 %collective-permute-start.13 = (bf16[2,32,2048]{2,1,0:T(8,128)(2,1)S(1)}, bf16[2,32,2048]{2,1,0:T(8,128)(2,1)S(1)}, u32[]{:S(2)}, u32[]{:S(2)}) collective-permute-start(bf16[2,32,2048]{2,1,0:T(8,128)(2,1)S(1)} %stacked.11.refs_1_), channel_id=1, source_target_pairs={{0,1},{1,0},{2,3},{3,2},{4,5},{5,4},{6,7},{7,6},{8,9},{9,8},{10,11... | collective-permute-start | bytes 786440 | tf_op jit(solution)/shard_map/ppermute | solution.py:35
  70.3 17.3 %collective-permute-start.29 = (bf16[2,32,2048]{2,1,0:T(8,128)(2,1)S(1)}, bf16[2,32,2048]{2,1,0:T(8,128)(2,1)S(1)}, u32[]{:S(2)}, u32[]{:S(2)}) collective-permute-start(bf16[2,32,2048]{2,1,0:T(8,128)(2,1)S(1)} %get-tuple-element.35), channel_id=1, source_target_pairs={{0,4},{1,5},{2,6},{3,7},{4,0},{5,1},{6,2},{7,3},{8,12},{9,13},{10,... | collective-permute-start | bytes 786440 | tf_op jit(solution)/shard_map/ppermute | solution.py:35
  70.5 19.2 %collective-permute-start.31 = (bf16[2,32,2048]{2,1,0:T(8,128)(2,1)S(1)}, bf16[2,32,2048]{2,1,0:T(8,128)(2,1)S(1)}, u32[]{:S(2)}, u32[]{:S(2)}) collective-permute-start(bf16[2,32,2048]{2,1,0:T(8,128)(2,1)S(1)} %get-tuple-element.36), channel_id=1, source_target_pairs={{0,2},{1,3},{2,0},{3,1},{4,6},{5,7},{6,4},{7,5},{8,10},{9,11},{10,... | collective-permute-start | bytes 786440 | tf_op jit(solution)/shard_map/ppermute | solution.py:35
  73.7 12.9 %collective-permute-start.22 = (bf16[32,2048]{1,0:T(8,128)(2,1)S(1)}, bf16[32,2048]{1,0:T(8,128)(2,1)S(1)}, u32[]{:S(2)}, u32[]{:S(2)}) collective-permute-start(bf16[32,2048]{1,0:T(8,128)(2,1)S(1)} %get-tuple-element.30.high_ref.refs_0_), channel_id=1, source_target_pairs={{0,8},{1,9},{2,10},{3,11},{4,12},{5,13},{6,14},{7,15},{8,0},{9,1},... | collective-permute-start | bytes 393224 | tf_op jit(solution)/shard_map/ppermute | solution.py:35
  75.3 11.3 %collective-permute-start.23 = (bf16[32,2048]{1,0:T(8,128)(2,1)S(1)}, bf16[32,2048]{1,0:T(8,128)(2,1)S(1)}, u32[]{:S(2)}, u32[]{:S(2)}) collective-permute-start(bf16[32,2048]{1,0:T(8,128)(2,1)S(1)} %get-tuple-element.30.high_ref.refs_0_), channel_id=1, source_target_pairs={{0,12},{1,13},{2,14},{3,15},{4,8},{5,9},{6,10},{7,11},{8,4},{9,5},... | collective-permute-start | bytes 393224 | tf_op jit(solution)/shard_map/ppermute | solution.py:35
  78.0 9.3 %collective-permute-start.19 = (bf16[32,2048]{1,0:T(8,128)(2,1)S(1)}, bf16[32,2048]{1,0:T(8,128)(2,1)S(1)}, u32[]{:S(2)}, u32[]{:S(2)}) collective-permute-start(bf16[32,2048]{1,0:T(8,128)(2,1)S(1)} %get-tuple-element.30.high_ref.refs_0_), channel_id=1, source_target_pairs={{0,2},{1,3},{2,0},{3,1},{4,6},{5,7},{6,4},{7,5},{8,10},{9,11},{10,... | collective-permute-start | bytes 393224 | tf_op jit(solution)/shard_map/ppermute | solution.py:35
  86.6 4.9 %collective-permute-start.25 = (bf16[2,32,2048]{2,1,0:T(8,128)(2,1)S(1)}, bf16[2,32,2048]{2,1,0:T(8,128)(2,1)S(1)}, u32[]{:S(2)}, u32[]{:S(2)}) collective-permute-start(bf16[2,32,2048]{2,1,0:T(8,128)(2,1)S(1)} %stacked.13.refs_1_), channel_id=1, source_target_pairs={{0,1},{1,0},{2,3},{3,2},{4,5},{5,4},{6,7},{7,6},{8,9},{9,8},{10,11... | collective-permute-start | bytes 786440 | tf_op jit(solution)/shard_map/ppermute | solution.py:35
  86.7 10.4 %collective-permute-start.26 = (bf16[2,32,2048]{2,1,0:T(8,128)(2,1)S(1)}, bf16[2,32,2048]{2,1,0:T(8,128)(2,1)S(1)}, u32[]{:S(2)}, u32[]{:S(2)}) collective-permute-start(bf16[2,32,2048]{2,1,0:T(8,128)(2,1)S(1)} %stacked.13.refs_1_), channel_id=1, source_target_pairs={{0,2},{1,3},{2,0},{3,1},{4,6},{5,7},{6,4},{7,5},{8,10},{9,11},{10,... | collective-permute-start | bytes 786440 | tf_op jit(solution)/shard_map/ppermute | solution.py:35
  87.4 5.6 %collective-permute-start.24 = (bf16[2,32,2048]{2,1,0:T(8,128)(2,1)S(1)}, bf16[2,32,2048]{2,1,0:T(8,128)(2,1)S(1)}, u32[]{:S(2)}, u32[]{:S(2)}) collective-permute-start(bf16[2,32,2048]{2,1,0:T(8,128)(2,1)S(1)} %stacked.12.refs_0_), channel_id=1, source_target_pairs={{0,1},{1,0},{2,3},{3,2},{4,5},{5,4},{6,7},{7,6},{8,9},{9,8},{10,11... | collective-permute-start | bytes 786440 | tf_op jit(solution)/shard_map/ppermute | solution.py:35
  87.6 9.6 %collective-permute-start.21 = (bf16[2,32,2048]{2,1,0:T(8,128)(2,1)S(1)}, bf16[2,32,2048]{2,1,0:T(8,128)(2,1)S(1)}, u32[]{:S(2)}, u32[]{:S(2)}) collective-permute-start(bf16[2,32,2048]{2,1,0:T(8,128)(2,1)S(1)} %stacked.12.refs_0_), channel_id=1, source_target_pairs={{0,4},{1,5},{2,6},{3,7},{4,0},{5,1},{6,2},{7,3},{8,12},{9,13},{10,... | collective-permute-start | bytes 786440 | tf_op jit(solution)/shard_map/ppermute | solution.py:35
  89.8 11.9 %collective-permute-start.30 = (bf16[32,2048]{1,0:T(8,128)(2,1)S(1)}, bf16[32,2048]{1,0:T(8,128)(2,1)S(1)}, u32[]{:S(2)}, u32[]{:S(2)}) collective-permute-start(bf16[32,2048]{1,0:T(8,128)(2,1)S(1)} %get-tuple-element.43), channel_id=1, source_target_pairs={{0,2},{1,3},{2,0},{3,1},{4,6},{5,7},{6,4},{7,5},{8,10},{9,11},{10,... | collective-permute-start | bytes 393224 | tf_op jit(solution)/shard_map/ppermute | solution.py:35
  91.5 10.2 %collective-permute-start.32 = (bf16[32,2048]{1,0:T(8,128)(2,1)S(1)}, bf16[32,2048]{1,0:T(8,128)(2,1)S(1)}, u32[]{:S(2)}, u32[]{:S(2)}) collective-permute-start(bf16[32,2048]{1,0:T(8,128)(2,1)S(1)} %get-tuple-element.40), channel_id=1, source_target_pairs={{0,12},{1,13},{2,14},{3,15},{4,8},{5,9},{6,10},{7,11},{8,4},{9,5},... | collective-permute-start | bytes 393224 | tf_op jit(solution)/shard_map/ppermute | solution.py:35
  92.9 11.9 %collective-permute-start.33 = (bf16[32,2048]{1,0:T(8,128)(2,1)S(1)}, bf16[32,2048]{1,0:T(8,128)(2,1)S(1)}, u32[]{:S(2)}, u32[]{:S(2)}) collective-permute-start(bf16[32,2048]{1,0:T(8,128)(2,1)S(1)} %get-tuple-element.39), channel_id=1, source_target_pairs={{0,8},{1,9},{2,10},{3,11},{4,12},{5,13},{6,14},{7,15},{8,0},{9,1},... | collective-permute-start | bytes 393224 | tf_op jit(solution)/shard_map/ppermute | solution.py:35
  107.1 7.3 %collective-permute-start.35 = (f32[48,128]{1,0:T(8,128)S(1)}, f32[48,128]{1,0:T(8,128)S(1)}, u32[]{:S(2)}, u32[]{:S(2)}) collective-permute-start(f32[48,128]{1,0:T(8,128)S(1)} %add.45), channel_id=1, source_target_pairs={{0,2},{1,3},{2,0},{3,1},{4,6},{5,7},{6,4},{7,5},{8,10},{9,11},{10,... | collective-permute-start | bytes 73736 | tf_op jit(solution)/shard_map/ppermute | solution.py:35
  114.3 4.4 %collective-permute-start.36 = (f32[48,128]{1,0:T(8,128)S(1)}, f32[48,128]{1,0:T(8,128)S(1)}, u32[]{:S(2)}, u32[]{:S(2)}) collective-permute-start(f32[48,128]{1,0:T(8,128)S(1)} %add.46), channel_id=1, source_target_pairs={{0,4},{1,5},{2,6},{3,7},{4,0},{5,1},{6,2},{7,3},{8,12},{9,13},{10,... | collective-permute-start | bytes 73736 | tf_op jit(solution)/shard_map/ppermute | solution.py:35
  114.3 5.1 %collective-permute-start.37 = (f32[48,128]{1,0:T(8,128)S(1)}, f32[48,128]{1,0:T(8,128)S(1)}, u32[]{:S(2)}, u32[]{:S(2)}) collective-permute-start(f32[48,128]{1,0:T(8,128)S(1)} %add.46), channel_id=1, source_target_pairs={{0,8},{1,9},{2,10},{3,11},{4,12},{5,13},{6,14},{7,15},{8,0},{9,1},... | collective-permute-start | bytes 73736 | tf_op jit(solution)/shard_map/ppermute | solution.py:35
  116.1 5.6 %collective-permute-start.38 = (f32[48,128]{1,0:T(8,128)S(1)}, f32[48,128]{1,0:T(8,128)S(1)}, u32[]{:S(2)}, u32[]{:S(2)}) collective-permute-start(f32[48,128]{1,0:T(8,128)S(1)} %add.46), channel_id=1, source_target_pairs={{0,12},{1,13},{2,14},{3,15},{4,8},{5,9},{6,10},{7,11},{8,4},{9,5},... | collective-permute-start | bytes 73736 | tf_op jit(solution)/shard_map/ppermute | solution.py:35
  (10 other events, 24.6 us)

commit v5 on v4

--- a/solution.py
+++ b/solution.py
@@ -74,8 +74,9 @@
 def gather_orders(count):
     low, shift, wide = stages(count)
     x = 1 << low[-1]
-    early = [[0, x], [2 << shift, 3 << shift]]
-    late = [[1 << shift, 1 << shift | x], [2 << shift | x, 3 << shift | x]]
+    fars = [far << shift for far in range(1, wide)]
+    early = [[0, x], fars]
+    late = [[far | x for far in fars]]
     for bit in reversed(low[:-1]):
         early = early + [[offset | 1 << bit for offset in offsets] for offsets in early]
         late = late + [[offset | 1 << bit for offset in offsets] for offsets in late]
@@ -85,19 +86,16 @@
 def gather_panels(panel, near, tokens, forward):
     low, shift, wide = stages(lax.axis_size("rows"))
     x = 1 << low[-1]
-    fars = [swap(panel, 2 << shift), swap(panel, 3 << shift)]
-    pair = stacked([panel, near], tokens[0])
-    early = [pair, stacked(fars, tokens[1])]
-    beside = swap(pair, 1 << shift)
+    fars = [swap(panel, far << shift) for far in range(1, wide)]
+    early = [stacked([panel, near], tokens[0]), stacked(fars, tokens[1])]
     late = swap(early[1], x)
     for bit in reversed(low[:-1]):
         early = early + [swap(array, 1 << bit) for array in early]
-    count = 2 * len(early)
     out = forward(early, 0, None)
-    late = [stacked([beside[0], beside[1]], out), stacked([late[0], late[1]], out)]
+    late = [whole(late, out)]
     for bit in reversed(low[:-1]):
         late = late + [swap(array, 1 << bit) for array in late]
-    return forward(late, count, out)
+    return forward(late, sum(array.shape[0] for array in early), out)
 
 
 def reduce_panels(kept, sent):
@@ -136,6 +134,15 @@
     shape = jax.ShapeDtypeStruct
     half = shape((2, *kept.shape[1:]), jnp.bfloat16)
     return call(added_kernel, (shape((4, *kept.shape[1:]), jnp.float32), half, half), kept, arrived, name="added")
+
+
+def whole_kernel(array_ref, token_ref, out_ref):
+    out_ref[...] = array_ref[...]
+
+
+def whole(array, token):
+    out = jax.ShapeDtypeStruct(array.shape, array.dtype)
+    return call(whole_kernel, out, array, token, name="whole", specs=[VMEM, ANY])
 
 
 def stacked_kernel(*refs):
@@ -267,8 +274,10 @@
 def forward_kernel(plan_ref, tiles_ref, *refs, groups, base, late):
     group_refs, (out_ref, pieces) = refs[:groups], refs[-2:]
     tiles, tile_size, _ = tiles_ref.shape
-    for group, ref in enumerate(group_refs):
-        pieces[group * 2 : (group + 1) * 2] = ref[...]
+    at = 0
+    for ref in group_refs:
+        pieces[at : at + ref.shape[0]] = ref[...]
+        at += ref.shape[0]
     out_ref[...] = refs[groups][...] if late else jnp.zeros_like(out_ref)
     front = plan_ref[tiles]
     start, end = (front, tiles) if late else (0, front)
@@ -280,7 +289,7 @@
             rest, block = parted(packed, 16)
             rest, row = parted(rest, 16)
             tile, piece = parted(rest, 256)
-            piece = jnp.clip(piece - base, 0, groups * 2 - 1)
+            piece = jnp.clip(piece - base, 0, pieces.shape[0] - 1)
             own = pl.ds(pl.multiple_of(row * tile_size, tile_size), tile_size)
             other = pl.ds(pl.multiple_of(block * tile_size, tile_size), tile_size)
             found = lax.dot_general(
@@ -445,7 +454,7 @@
     orders = gather_orders(count)
     order = [offset for group in orders for offsets in group for offset in offsets]
     gathered_place = np.argsort(np.array(order)).astype(np.int32)
-    early_pieces = 2 * len(orders[0])
+    early_pieces = sum(map(len, orders[0]))
     fixed = jnp.concatenate(
         [me, jnp.asarray(positions(count)), jnp.asarray(list_place), tile_rows, tile_slots, jnp.asarray(gathered_place)]
     )
@@ -482,7 +491,7 @@
             shape((width, here), f32),
             plan, held, *groups, *([before] if late else []),
             name="late" if late else "early", specs=[SMEM] + [VMEM] * (1 + len(groups) + late),
-            scratch=[pltpu.VMEM((2 * len(groups), width, here), bf16)], cost=cost,
+            scratch=[pltpu.VMEM((sum(group.shape[0] for group in groups), width, here), bf16)], cost=cost,
         )
 
     def applied(high, sums):

time: 126 us -> 121 us (0.960)
  starting transfers between devices: 47.4 us -> 41.1 us
    ppermute x39 -> x37, starting transfers between devices: 47.4 us -> 41.1 us  [swap(): lax.ppermute(array, 'rows', [(place, place ^ offset) for place in range(c...]
    ppermute x39 -> x37, waiting for transfers between devices: 40.3 us -> 40.9 us  [swap(): lax.ppermute(array, 'rows', [(place, place ^ offset) for place in range(c...]
    pallas_call x23 -> x21, Pallas kernels: 25.5 us -> 25.5 us  [call(): pl.pallas_call(kernel, out_shape=out, in_specs=specs or [VMEM] * len(args...]
  transfers between devices with their start and end apart: 39 -> 37, of which waited for: 17 -> 19; matrix products, arithmetic and copies ran while one was open for 1% -> 1% of each run, Pallas kernels for 18% -> 19%
where the time goes in v5:
time: 121 us; the launch traced here: 120 us
  starting transfers between devices  41.1 us (34%)
  waiting for transfers between devices  40.9 us (34%)
  Pallas kernels  34.8 us (29%)
  local copies, waits for them, and re-layouts  2.26 us (2%)
    ppermute x37, starting transfers between devices, swap(): lax.ppermute(array, 'rows', [(place, place ^ offset) for place in range(c...  41.1 us
    ppermute x37, waiting for transfers between devices, swap(): lax.ppermute(array, 'rows', [(place, place ^ offset) for place in range(c...  40.9 us
    pallas_call x21, Pallas kernels, call(): pl.pallas_call(kernel, out_shape=out, in_specs=specs or [VMEM] * len(args...  25.5 us
    pallas_call x1, Pallas kernels, first_products(): pl.pallas_call(products_kernel, out_shape=(shape((tiles, width, tile_size...  6.35 us
    pallas_call x1, Pallas kernels, on_device(): pl.pallas_call(functools.partial(plan_kernel, sizes=sizes, early=early_pi...  2.92 us
  transfers between devices with their start and end apart: 37, of which 19 were waited for; matrix products, arithmetic and copies ran while one was open for 1% of the time, Pallas kernels for 19%

profile of v5, /device:TPU:0, one launch (start us, length us, event | category | flops | bytes accessed | tf_op | source)
XLA Modules:
  0.0 120.2 jit_solution(3373635523188628688)
XLA Ops:
  1.4 4.0 %collective-permute-start = (s32[1,256]{1,0:T(1,128)S(1)}, s32[1,256]{1,0:T(1,128)S(1)}, u32[]{:S(2)}, u32[]{:S(2)}) collective-permute-start(s32[1,256]{1,0:T(1,128)S(1)} %reshape.31.near_ref), channel_id=1, source_target_pairs={{0,8},{1,9},{2,10},{3,11},{4,12},{5,13},{6,14},{7,15},{8,0},{9,1},... | collective-permute-start | bytes 3080 | tf_op jit(solution)/shard_map/ppermute | solution.py:35
  7.0 1.9 %collective-permute-start.1 = (s32[2,256]{1,0:T(2,128)S(1)}, s32[2,256]{1,0:T(2,128)S(1)}, u32[]{:S(2)}, u32[]{:S(2)}) collective-permute-start(s32[2,256]{1,0:T(2,128)S(1)} %joined.4.near_ref.token_ref), channel_id=1, source_target_pairs={{0,4},{1,5},{2,6},{3,7},{4,0},{5,1},{6,2},{7,3},{8,12},{9,13},{10,... | collective-permute-start | bytes 6152 | tf_op jit(solution)/shard_map/ppermute | solution.py:35
  8.9 1.7 %collective-permute-done.1.far_ref = s32[2,256]{1,0:T(2,128)S(1)} collective-permute-done((s32[2,256]{1,0:T(2,128)S(1)}, s32[2,256]{1,0:T(2,128)S(1)}, u32[]{:S(2)}, u32[]{:S(2)}) %collective-permute-start.1) | collective-permute-done | bytes 2080 | tf_op jit(solution)/shard_map/ppermute | solution.py:35
  10.6 1.8 %collective-permute-start.2 = (s32[4,256]{1,0:T(4,128)S(1)}, s32[4,256]{1,0:T(4,128)S(1)}, u32[]{:S(2)}, u32[]{:S(2)}) collective-permute-start(s32[4,256]{1,0:T(4,128)S(1)} %joined.5.near_ref), channel_id=1, source_target_pairs={{0,2},{1,3},{2,0},{3,1},{4,6},{5,7},{6,4},{7,5},{8,10},{9,11},{10,... | collective-permute-start | bytes 12296 | tf_op jit(solution)/shard_map/ppermute | solution.py:35
  14.9 6.3 %products.1 = (f32[96,32,256]{2,1,0:T(8,128)S(1)}, bf16[96,256,256]{2,1,0:T(8,128)(2,1)S(1)}, bf16[32,2048]{1,0:T(8,128)(2,1)S(1)}, bf16[32,2048]{1,0:T(8,128)(2,1)}) custom-call(s32[96]{0:T(128)S(1)} %copy-done.2, f32[32,2048]{1,0:T(8,128)} %start_ref.3, bf16[96,256,256]{2,1,0:T(8,128)(2,1)} %tiles_ref.1, s32[2,256]{1,0:T(2,128)S(1)} %joined.4.near_ref.token_ref), custom_call_target="tpu_custom_call" | custom-call | flops 402653184 | bytes 1024 | tf_op jit(solution)/shard_map/products/pallas_call | solution.py:439
  21.2 2.1 %sums.1 = (f32[8,32,2048]{2,1,0:T(8,128)S(1)}, bf16[8,32,2048]{2,1,0:T(8,128)(2,1)S(1)}) custom-call(s32[241]{0:T(256)S(1)} %concatenate.3.fixed_ref, s32[16,256]{1,0:T(8,128)S(1)} %joined.7.list_ref, f32[96,32,256]{2,1,0:T(8,128)S(1)} %get-tuple-element.23.products_ref, bf16[32,2048]{1,0:T(8,128)(2,1)S(1)} %get-tuple-element.22.token_ref.refs_0_), custom_call_target="tpu_custom_call" | custom-call | flops 402653184 | bytes 1024 | tf_op jit(solution)/shard_map/sums/pallas_call | solution.py:413
  23.9 1.9 %collective-permute-start.4 = (bf16[32,2048]{1,0:T(8,128)(2,1)S(1)}, bf16[32,2048]{1,0:T(8,128)(2,1)S(1)}, u32[]{:S(2)}, u32[]{:S(2)}) collective-permute-start(bf16[32,2048]{1,0:T(8,128)(2,1)S(1)} %get-tuple-element.22.token_ref.refs_0_), channel_id=1, source_target_pairs={{0,4},{1,5},{2,6},{3,7},{4,0},{5,1},{6,2},{7,3},{8,12},{9,13},{10,... | collective-permute-start | bytes 393224 | tf_op jit(solution)/shard_map/ppermute | solution.py:35
  26.4 2.0 %collective-permute-start.13 = (bf16[2,32,2048]{2,1,0:T(8,128)(2,1)S(1)}, bf16[2,32,2048]{2,1,0:T(8,128)(2,1)S(1)}, u32[]{:S(2)}, u32[]{:S(2)}) collective-permute-start(bf16[2,32,2048]{2,1,0:T(8,128)(2,1)S(1)} %get-tuple-element.27), channel_id=1, source_target_pairs={{0,4},{1,5},{2,6},{3,7},{4,0},{5,1},{6,2},{7,3},{8,12},{9,13},{10,... | collective-permute-start | bytes 786440 | tf_op jit(solution)/shard_map/ppermute | solution.py:35
  29.9 2.6 %collective-permute-start.5 = (bf16[32,2048]{1,0:T(8,128)(2,1)S(1)}, bf16[32,2048]{1,0:T(8,128)(2,1)S(1)}, u32[]{:S(2)}, u32[]{:S(2)}) collective-permute-start(bf16[32,2048]{1,0:T(8,128)(2,1)S(1)} %get-tuple-element.22.token_ref.refs_0_), channel_id=1, source_target_pairs={{0,8},{1,9},{2,10},{3,11},{4,12},{5,13},{6,14},{7,15},{8,0},{9,1},... | collective-permute-start | bytes 393224 | tf_op jit(solution)/shard_map/ppermute | solution.py:35
  33.0 2.9 %plan.1.plan_ref = s32[97]{0:T(128)S(1)} custom-call(s32[241]{0:T(256)S(1)} %concatenate.3.fixed_ref, s32[16,256]{1,0:T(8,128)S(1)} %joined.7.list_ref), custom_call_target="tpu_custom_call" | custom-call | tf_op jit(solution)/shard_map/plan/pallas_call | solution.py:481
  36.0 1.9 %collective-permute-done.5.refs_1_ = bf16[32,2048]{1,0:T(8,128)(2,1)S(1)} collective-permute-done((bf16[32,2048]{1,0:T(8,128)(2,1)S(1)}, bf16[32,2048]{1,0:T(8,128)(2,1)S(1)}, u32[]{:S(2)}, u32[]{:S(2)}) %collective-permute-start.5) | collective-permute-done | bytes 131104 | tf_op jit(solution)/shard_map/ppermute | solution.py:35
  37.9 5.2 %collective-permute-done.6.refs_2_ = bf16[32,2048]{1,0:T(8,128)(2,1)S(1)} collective-permute-done((bf16[32,2048]{1,0:T(8,128)(2,1)S(1)}, bf16[32,2048]{1,0:T(8,128)(2,1)S(1)}, u32[]{:S(2)}, u32[]{:S(2)}) %collective-permute-start.6) | collective-permute-done | bytes 131104 | tf_op jit(solution)/shard_map/ppermute | solution.py:35
  45.8 2.1 %collective-permute-start.16 = (bf16[32,2048]{1,0:T(8,128)(2,1)S(1)}, bf16[32,2048]{1,0:T(8,128)(2,1)S(1)}, u32[]{:S(2)}, u32[]{:S(2)}) collective-permute-start(bf16[32,2048]{1,0:T(8,128)(2,1)S(1)} %get-tuple-element.42), channel_id=1, source_target_pairs={{0,12},{1,13},{2,14},{3,15},{4,8},{5,9},{6,10},{7,11},{8,4},{9,5},... | collective-permute-start | bytes 393224 | tf_op jit(solution)/shard_map/ppermute | solution.py:35
  49.2 3.6 %early.2.token_ref.refs_2_ = f32[32,2048]{1,0:T(8,128)S(1)} custom-call(s32[97]{0:T(128)S(1)} %plan.1.plan_ref, bf16[96,256,256]{2,1,0:T(8,128)(2,1)S(1)} %get-tuple-element.21.tiles_ref, bf16[2,32,2048]{2,1,0:T(8,128)(2,1)S(1)} %stacked.5.refs_0_, bf16[3,32,2048]{2,1,0:T(8,128)(2,1)S(1)} %stacked.4.refs_1_, ...), custom_call_target="tpu_custom_call" | custom-call | flops 402653184 | bytes 1024 | tf_op jit(solution)/shard_map/early/pallas_call | solution.py:413
  52.8 2.4 %collective-permute-done.8.array_ref = bf16[3,32,2048]{2,1,0:T(8,128)(2,1)S(1)} collective-permute-done((bf16[3,32,2048]{2,1,0:T(8,128)(2,1)S(1)}, bf16[3,32,2048]{2,1,0:T(8,128)(2,1)S(1)}, u32[]{:S(2)}, u32[]{:S(2)}) %collective-permute-start.8) | collective-permute-done | bytes 393248 | tf_op jit(solution)/shard_map/ppermute | solution.py:35
  55.4 1.7 %collective-permute-done.12.refs_1_ = bf16[3,32,2048]{2,1,0:T(8,128)(2,1)S(1)} collective-permute-done((bf16[3,32,2048]{2,1,0:T(8,128)(2,1)S(1)}, bf16[3,32,2048]{2,1,0:T(8,128)(2,1)S(1)}, u32[]{:S(2)}, u32[]{:S(2)}) %collective-permute-start.12) | collective-permute-done | bytes 393248 | tf_op jit(solution)/shard_map/ppermute | solution.py:35
  57.1 2.8 %late.2.forward_ref = f32[32,2048]{1,0:T(8,128)S(1)} custom-call(s32[97]{0:T(128)S(1)} %plan.1.plan_ref, bf16[96,256,256]{2,1,0:T(8,128)(2,1)S(1)} %get-tuple-element.21.tiles_ref, bf16[3,32,2048]{2,1,0:T(8,128)(2,1)S(1)} %whole.2.refs_0_, bf16[3,32,2048]{2,1,0:T(8,128)(2,1)S(1)} %collective-permute-done.12.refs_1_, f32[32,2048]{1,0:T(8,128)S(1)} %early.2.token_ref.refs_2_), custom_call_target="tpu_custom_call" | custom-call | flops 402653184 | bytes 1024 | tf_op jit(solution)/shard_map/late/pallas_call | solution.py:413
  61.2 4.3 %backward.1 = (f32[8,32,2048]{2,1,0:T(8,128)S(1)}, bf16[8,32,2048]{2,1,0:T(8,128)(2,1)S(1)}) custom-call(s32[241]{0:T(256)S(1)} %concatenate.3.fixed_ref, s32[16,256]{1,0:T(8,128)S(1)} %joined.7.list_ref, bf16[32,2048]{1,0:T(8,128)(2,1)S(1)} %get-tuple-element.30.high_ref.refs_0_, bf16[32,2048]{1,0:T(8,128)(2,1)S(1)} %get-tuple-element.31.low_ref, ...), custom_call_target="tpu_custom_call" | custom-call | flops 402653184 | bytes 1024 | tf_op jit(solution)/shard_map/backward/pallas_call | solution.py:413
  66.4 1.8 %collective-permute-done.21.arrived_ref = bf16[8,32,2048]{2,1,0:T(8,128)(2,1)S(1)} collective-permute-done((bf16[8,32,2048]{2,1,0:T(8,128)(2,1)S(1)}, bf16[8,32,2048]{2,1,0:T(8,128)(2,1)S(1)}, u32[]{:S(2)}, u32[]{:S(2)}) %collective-permute-start.21) | collective-permute-done | bytes 1048608 | tf_op jit(solution)/shard_map/ppermute | solution.py:35
  69.6 2.5 %collective-permute-start.19 = (bf16[32,2048]{1,0:T(8,128)(2,1)S(1)}, bf16[32,2048]{1,0:T(8,128)(2,1)S(1)}, u32[]{:S(2)}, u32[]{:S(2)}) collective-permute-start(bf16[32,2048]{1,0:T(8,128)(2,1)S(1)} %get-tuple-element.30.high_ref.refs_0_), channel_id=1, source_target_pairs={{0,8},{1,9},{2,10},{3,11},{4,12},{5,13},{6,14},{7,15},{8,0},{9,1},... | collective-permute-start | bytes 393224 | tf_op jit(solution)/shard_map/ppermute | solution.py:35
  72.1 1.6 %collective-permute-start.20 = (bf16[32,2048]{1,0:T(8,128)(2,1)S(1)}, bf16[32,2048]{1,0:T(8,128)(2,1)S(1)}, u32[]{:S(2)}, u32[]{:S(2)}) collective-permute-start(bf16[32,2048]{1,0:T(8,128)(2,1)S(1)} %get-tuple-element.30.high_ref.refs_0_), channel_id=1, source_target_pairs={{0,12},{1,13},{2,14},{3,15},{4,8},{5,9},{6,10},{7,11},{8,4},{9,5},... | collective-permute-start | bytes 393224 | tf_op jit(solution)/shard_map/ppermute | solution.py:35
  74.9 3.6 %collective-permute-done.19.refs_1_ = bf16[32,2048]{1,0:T(8,128)(2,1)S(1)} collective-permute-done((bf16[32,2048]{1,0:T(8,128)(2,1)S(1)}, bf16[32,2048]{1,0:T(8,128)(2,1)S(1)}, u32[]{:S(2)}, u32[]{:S(2)}) %collective-permute-start.19) | collective-permute-done | bytes 131104 | tf_op jit(solution)/shard_map/ppermute | solution.py:35
  78.6 5.0 %collective-permute-done.20.refs_2_ = bf16[32,2048]{1,0:T(8,128)(2,1)S(1)} collective-permute-done((bf16[32,2048]{1,0:T(8,128)(2,1)S(1)}, bf16[32,2048]{1,0:T(8,128)(2,1)S(1)}, u32[]{:S(2)}, u32[]{:S(2)}) %collective-permute-start.20) | collective-permute-done | bytes 131104 | tf_op jit(solution)/shard_map/ppermute | solution.py:35
  86.2 2.1 %collective-permute-start.30 = (bf16[32,2048]{1,0:T(8,128)(2,1)S(1)}, bf16[32,2048]{1,0:T(8,128)(2,1)S(1)}, u32[]{:S(2)}, u32[]{:S(2)}) collective-permute-start(bf16[32,2048]{1,0:T(8,128)(2,1)S(1)} %get-tuple-element.40), channel_id=1, source_target_pairs={{0,12},{1,13},{2,14},{3,15},{4,8},{5,9},{6,10},{7,11},{8,4},{9,5},... | collective-permute-start | bytes 393224 | tf_op jit(solution)/shard_map/ppermute | solution.py:35
  88.9 3.7 %early.3.token_ref.refs_2_ = f32[32,2048]{1,0:T(8,128)S(1)} custom-call(s32[97]{0:T(128)S(1)} %plan.1.plan_ref, bf16[96,256,256]{2,1,0:T(8,128)(2,1)S(1)} %get-tuple-element.21.tiles_ref, bf16[2,32,2048]{2,1,0:T(8,128)(2,1)S(1)} %stacked.7.refs_0_, bf16[3,32,2048]{2,1,0:T(8,128)(2,1)S(1)} %stacked.6.refs_1_, ...), custom_call_target="tpu_custom_call" | custom-call | flops 402653184 | bytes 1024 | tf_op jit(solution)/shard_map/early/pallas_call | solution.py:413
  92.5 3.2 %collective-permute-done.22.array_ref = bf16[3,32,2048]{2,1,0:T(8,128)(2,1)S(1)} collective-permute-done((bf16[3,32,2048]{2,1,0:T(8,128)(2,1)S(1)}, bf16[3,32,2048]{2,1,0:T(8,128)(2,1)S(1)}, u32[]{:S(2)}, u32[]{:S(2)}) %collective-permute-start.22) | collective-permute-done | bytes 393248 | tf_op jit(solution)/shard_map/ppermute | solution.py:35
  95.8 1.7 %collective-permute-done.26.refs_1_ = bf16[3,32,2048]{2,1,0:T(8,128)(2,1)S(1)} collective-permute-done((bf16[3,32,2048]{2,1,0:T(8,128)(2,1)S(1)}, bf16[3,32,2048]{2,1,0:T(8,128)(2,1)S(1)}, u32[]{:S(2)}, u32[]{:S(2)}) %collective-permute-start.26) | collective-permute-done | bytes 393248 | tf_op jit(solution)/shard_map/ppermute | solution.py:35
  97.5 3.0 %late.3.forward_ref = f32[32,2048]{1,0:T(8,128)S(1)} custom-call(s32[97]{0:T(128)S(1)} %plan.1.plan_ref, bf16[96,256,256]{2,1,0:T(8,128)(2,1)S(1)} %get-tuple-element.21.tiles_ref, bf16[3,32,2048]{2,1,0:T(8,128)(2,1)S(1)} %whole.3.refs_0_, bf16[3,32,2048]{2,1,0:T(8,128)(2,1)S(1)} %collective-permute-done.26.refs_1_, f32[32,2048]{1,0:T(8,128)S(1)} %early.3.token_ref.refs_2_), custom_call_target="tpu_custom_call" | custom-call | flops 402653184 | bytes 1024 | tf_op jit(solution)/shard_map/late/pallas_call | solution.py:413
  104.5 2.5 %collective-permute-done.33 = f32[48,128]{1,0:T(8,128)S(1)} collective-permute-done((f32[48,128]{1,0:T(8,128)S(1)}, f32[48,128]{1,0:T(8,128)S(1)}, u32[]{:S(2)}, u32[]{:S(2)}) %collective-permute-start.33) | collective-permute-done | bytes 24608 | tf_op jit(solution)/shard_map/ppermute | solution.py:35
  107.5 2.7 %collective-permute-start.35 = (f32[48,128]{1,0:T(8,128)S(1)}, f32[48,128]{1,0:T(8,128)S(1)}, u32[]{:S(2)}, u32[]{:S(2)}) collective-permute-start(f32[48,128]{1,0:T(8,128)S(1)} %add.46), channel_id=1, source_target_pairs={{0,8},{1,9},{2,10},{3,11},{4,12},{5,13},{6,14},{7,15},{8,0},{9,1},... | collective-permute-start | bytes 73736 | tf_op jit(solution)/shard_map/ppermute | solution.py:35
  112.2 3.6 %collective-permute-done.36 = f32[48,128]{1,0:T(8,128)S(1)} collective-permute-done((f32[48,128]{1,0:T(8,128)S(1)}, f32[48,128]{1,0:T(8,128)S(1)}, u32[]{:S(2)}, u32[]{:S(2)}) %collective-permute-start.36) | collective-permute-done | bytes 24608 | tf_op jit(solution)/shard_map/ppermute | solution.py:35
  115.8 4.4 %last.1 = (f32[32,2048]{1,0:T(8,128)}, f32[2,32,32]{2,1,0:T(8,128)}, f32[2,32,32]{2,1,0:T(8,128)}) custom-call(f32[48,128]{1,0:T(8,128)S(1)} %add_add_fusion.gram_ref, f32[96,2048]{1,0:T(8,128)S(1)} %get-tuple-element.38.panels_ref), custom_call_target="tpu_custom_call" | custom-call | tf_op jit(solution)/shard_map/last/pallas_call | solution.py:413
  (80 shorter events, 26.6 us)
Async XLA Ops:
  1.4 5.6 %collective-permute-start = (s32[1,256]{1,0:T(1,128)S(1)}, s32[1,256]{1,0:T(1,128)S(1)}, u32[]{:S(2)}, u32[]{:S(2)}) collective-permute-start(s32[1,256]{1,0:T(1,128)S(1)} %reshape.31.near_ref), channel_id=1, source_target_pairs={{0,8},{1,9},{2,10},{3,11},{4,12},{5,13},{6,14},{7,15},{8,0},{9,1},... | collective-permute-start | bytes 3080 | tf_op jit(solution)/shard_map/ppermute | solution.py:35
  7.0 3.6 %collective-permute-start.1 = (s32[2,256]{1,0:T(2,128)S(1)}, s32[2,256]{1,0:T(2,128)S(1)}, u32[]{:S(2)}, u32[]{:S(2)}) collective-permute-start(s32[2,256]{1,0:T(2,128)S(1)} %joined.4.near_ref.token_ref), channel_id=1, source_target_pairs={{0,4},{1,5},{2,6},{3,7},{4,0},{5,1},{6,2},{7,3},{8,12},{9,13},{10,... | collective-permute-start | bytes 6152 | tf_op jit(solution)/shard_map/ppermute | solution.py:35
  10.6 3.6 %collective-permute-start.2 = (s32[4,256]{1,0:T(4,128)S(1)}, s32[4,256]{1,0:T(4,128)S(1)}, u32[]{:S(2)}, u32[]{:S(2)}) collective-permute-start(s32[4,256]{1,0:T(4,128)S(1)} %joined.5.near_ref), channel_id=1, source_target_pairs={{0,2},{1,3},{2,0},{3,1},{4,6},{5,7},{6,4},{7,5},{8,10},{9,11},{10,... | collective-permute-start | bytes 12296 | tf_op jit(solution)/shard_map/ppermute | solution.py:35
  14.2 7.0 %collective-permute-start.3 = (s32[8,256]{1,0:T(8,128)S(1)}, s32[8,256]{1,0:T(8,128)S(1)}, u32[]{:S(2)}, u32[]{:S(2)}) collective-permute-start(s32[8,256]{1,0:T(8,128)S(1)} %joined.6.near_ref), channel_id=1, source_target_pairs={{0,1},{1,0},{2,3},{3,2},{4,5},{5,4},{6,7},{7,6},{8,9},{9,8},{10,11... | collective-permute-start | bytes 24584 | tf_op jit(solution)/shard_map/ppermute | solution.py:35
  23.9 8.8 %collective-permute-start.4 = (bf16[32,2048]{1,0:T(8,128)(2,1)S(1)}, bf16[32,2048]{1,0:T(8,128)(2,1)S(1)}, u32[]{:S(2)}, u32[]{:S(2)}) collective-permute-start(bf16[32,2048]{1,0:T(8,128)(2,1)S(1)} %get-tuple-element.22.token_ref.refs_0_), channel_id=1, source_target_pairs={{0,4},{1,5},{2,6},{3,7},{4,0},{5,1},{6,2},{7,3},{8,12},{9,13},{10,... | collective-permute-start | bytes 393224 | tf_op jit(solution)/shard_map/ppermute | solution.py:35
  26.4 18.7 %collective-permute-start.13 = (bf16[2,32,2048]{2,1,0:T(8,128)(2,1)S(1)}, bf16[2,32,2048]{2,1,0:T(8,128)(2,1)S(1)}, u32[]{:S(2)}, u32[]{:S(2)}) collective-permute-start(bf16[2,32,2048]{2,1,0:T(8,128)(2,1)S(1)} %get-tuple-element.27), channel_id=1, source_target_pairs={{0,4},{1,5},{2,6},{3,7},{4,0},{5,1},{6,2},{7,3},{8,12},{9,13},{10,... | collective-permute-start | bytes 786440 | tf_op jit(solution)/shard_map/ppermute | solution.py:35
  28.4 16.7 %collective-permute-start.15 = (bf16[2,32,2048]{2,1,0:T(8,128)(2,1)S(1)}, bf16[2,32,2048]{2,1,0:T(8,128)(2,1)S(1)}, u32[]{:S(2)}, u32[]{:S(2)}) collective-permute-start(bf16[2,32,2048]{2,1,0:T(8,128)(2,1)S(1)} %get-tuple-element.28), channel_id=1, source_target_pairs={{0,2},{1,3},{2,0},{3,1},{4,6},{5,7},{6,4},{7,5},{8,10},{9,11},{10,... | collective-permute-start | bytes 786440 | tf_op jit(solution)/shard_map/ppermute | solution.py:35
  29.9 8.0 %collective-permute-start.5 = (bf16[32,2048]{1,0:T(8,128)(2,1)S(1)}, bf16[32,2048]{1,0:T(8,128)(2,1)S(1)}, u32[]{:S(2)}, u32[]{:S(2)}) collective-permute-start(bf16[32,2048]{1,0:T(8,128)(2,1)S(1)} %get-tuple-element.22.token_ref.refs_0_), channel_id=1, source_target_pairs={{0,8},{1,9},{2,10},{3,11},{4,12},{5,13},{6,14},{7,15},{8,0},{9,1},... | collective-permute-start | bytes 393224 | tf_op jit(solution)/shard_map/ppermute | solution.py:35
  32.5 10.7 %collective-permute-start.6 = (bf16[32,2048]{1,0:T(8,128)(2,1)S(1)}, bf16[32,2048]{1,0:T(8,128)(2,1)S(1)}, u32[]{:S(2)}, u32[]{:S(2)}) collective-permute-start(bf16[32,2048]{1,0:T(8,128)(2,1)S(1)} %get-tuple-element.22.token_ref.refs_0_), channel_id=1, source_target_pairs={{0,12},{1,13},{2,14},{3,15},{4,8},{5,9},{6,10},{7,11},{8,4},{9,5},... | collective-permute-start | bytes 393224 | tf_op jit(solution)/shard_map/ppermute | solution.py:35
  32.7 12.1 %collective-permute-start.9 = (bf16[32,2048]{1,0:T(8,128)(2,1)S(1)}, bf16[32,2048]{1,0:T(8,128)(2,1)S(1)}, u32[]{:S(2)}, u32[]{:S(2)}) collective-permute-start(bf16[32,2048]{1,0:T(8,128)(2,1)S(1)} %get-tuple-element.22.token_ref.refs_0_), channel_id=1, source_target_pairs={{0,2},{1,3},{2,0},{3,1},{4,6},{5,7},{6,4},{7,5},{8,10},{9,11},{10,... | collective-permute-start | bytes 393224 | tf_op jit(solution)/shard_map/ppermute | solution.py:35
  43.2 6.0 %collective-permute-start.11 = (bf16[3,32,2048]{2,1,0:T(8,128)(2,1)S(1)}, bf16[3,32,2048]{2,1,0:T(8,128)(2,1)S(1)}, u32[]{:S(2)}, u32[]{:S(2)}) collective-permute-start(bf16[3,32,2048]{2,1,0:T(8,128)(2,1)S(1)} %stacked.4.refs_1_), channel_id=1, source_target_pairs={{0,1},{1,0},{2,3},{3,2},{4,5},{5,4},{6,7},{7,6},{8,9},{9,8},{10,11... | collective-permute-start | bytes 1179656 | tf_op jit(solution)/shard_map/ppermute | solution.py:35
  43.3 12.0 %collective-permute-start.8 = (bf16[3,32,2048]{2,1,0:T(8,128)(2,1)S(1)}, bf16[3,32,2048]{2,1,0:T(8,128)(2,1)S(1)}, u32[]{:S(2)}, u32[]{:S(2)}) collective-permute-start(bf16[3,32,2048]{2,1,0:T(8,128)(2,1)S(1)} %stacked.4.refs_1_), channel_id=1, source_target_pairs={{0,2},{1,3},{2,0},{3,1},{4,6},{5,7},{6,4},{7,5},{8,10},{9,11},{10,... | collective-permute-start | bytes 1179656 | tf_op jit(solution)/shard_map/ppermute | solution.py:35
  44.8 3.1 %collective-permute-start.10 = (bf16[2,32,2048]{2,1,0:T(8,128)(2,1)S(1)}, bf16[2,32,2048]{2,1,0:T(8,128)(2,1)S(1)}, u32[]{:S(2)}, u32[]{:S(2)}) collective-permute-start(bf16[2,32,2048]{2,1,0:T(8,128)(2,1)S(1)} %stacked.5.refs_0_), channel_id=1, source_target_pairs={{0,1},{1,0},{2,3},{3,2},{4,5},{5,4},{6,7},{7,6},{8,9},{9,8},{10,11... | collective-permute-start | bytes 786440 | tf_op jit(solution)/shard_map/ppermute | solution.py:35
  45.2 14.6 %collective-permute-start.14 = (bf16[32,2048]{1,0:T(8,128)(2,1)S(1)}, bf16[32,2048]{1,0:T(8,128)(2,1)S(1)}, u32[]{:S(2)}, u32[]{:S(2)}) collective-permute-start(bf16[32,2048]{1,0:T(8,128)(2,1)S(1)} %get-tuple-element.45), channel_id=1, source_target_pairs={{0,2},{1,3},{2,0},{3,1},{4,6},{5,7},{6,4},{7,5},{8,10},{9,11},{10,... | collective-permute-start | bytes 393224 | tf_op jit(solution)/shard_map/ppermute | solution.py:35
  45.8 14.1 %collective-permute-start.16 = (bf16[32,2048]{1,0:T(8,128)(2,1)S(1)}, bf16[32,2048]{1,0:T(8,128)(2,1)S(1)}, u32[]{:S(2)}, u32[]{:S(2)}) collective-permute-start(bf16[32,2048]{1,0:T(8,128)(2,1)S(1)} %get-tuple-element.42), channel_id=1, source_target_pairs={{0,12},{1,13},{2,14},{3,15},{4,8},{5,9},{6,10},{7,11},{8,4},{9,5},... | collective-permute-start | bytes 393224 | tf_op jit(solution)/shard_map/ppermute | solution.py:35
  48.0 13.1 %collective-permute-start.17 = (bf16[32,2048]{1,0:T(8,128)(2,1)S(1)}, bf16[32,2048]{1,0:T(8,128)(2,1)S(1)}, u32[]{:S(2)}, u32[]{:S(2)}) collective-permute-start(bf16[32,2048]{1,0:T(8,128)(2,1)S(1)} %get-tuple-element.41), channel_id=1, source_target_pairs={{0,8},{1,9},{2,10},{3,11},{4,12},{5,13},{6,14},{7,15},{8,0},{9,1},... | collective-permute-start | bytes 393224 | tf_op jit(solution)/shard_map/ppermute | solution.py:35
  65.6 8.2 %collective-permute-start.18 = (bf16[32,2048]{1,0:T(8,128)(2,1)S(1)}, bf16[32,2048]{1,0:T(8,128)(2,1)S(1)}, u32[]{:S(2)}, u32[]{:S(2)}) collective-permute-start(bf16[32,2048]{1,0:T(8,128)(2,1)S(1)} %get-tuple-element.30.high_ref.refs_0_), channel_id=1, source_target_pairs={{0,4},{1,5},{2,6},{3,7},{4,0},{5,1},{6,2},{7,3},{8,12},{9,13},{10,... | collective-permute-start | bytes 393224 | tf_op jit(solution)/shard_map/ppermute | solution.py:35
  68.5 17.0 %collective-permute-start.27 = (bf16[2,32,2048]{2,1,0:T(8,128)(2,1)S(1)}, bf16[2,32,2048]{2,1,0:T(8,128)(2,1)S(1)}, u32[]{:S(2)}, u32[]{:S(2)}) collective-permute-start(bf16[2,32,2048]{2,1,0:T(8,128)(2,1)S(1)} %get-tuple-element.35), channel_id=1, source_target_pairs={{0,4},{1,5},{2,6},{3,7},{4,0},{5,1},{6,2},{7,3},{8,12},{9,13},{10,... | collective-permute-start | bytes 786440 | tf_op jit(solution)/shard_map/ppermute | solution.py:35
  69.1 16.4 %collective-permute-start.29 = (bf16[2,32,2048]{2,1,0:T(8,128)(2,1)S(1)}, bf16[2,32,2048]{2,1,0:T(8,128)(2,1)S(1)}, u32[]{:S(2)}, u32[]{:S(2)}) collective-permute-start(bf16[2,32,2048]{2,1,0:T(8,128)(2,1)S(1)} %get-tuple-element.36), channel_id=1, source_target_pairs={{0,2},{1,3},{2,0},{3,1},{4,6},{5,7},{6,4},{7,5},{8,10},{9,11},{10,... | collective-permute-start | bytes 786440 | tf_op jit(solution)/shard_map/ppermute | solution.py:35
  69.6 8.9 %collective-permute-start.19 = (bf16[32,2048]{1,0:T(8,128)(2,1)S(1)}, bf16[32,2048]{1,0:T(8,128)(2,1)S(1)}, u32[]{:S(2)}, u32[]{:S(2)}) collective-permute-start(bf16[32,2048]{1,0:T(8,128)(2,1)S(1)} %get-tuple-element.30.high_ref.refs_0_), channel_id=1, source_target_pairs={{0,8},{1,9},{2,10},{3,11},{4,12},{5,13},{6,14},{7,15},{8,0},{9,1},... | collective-permute-start | bytes 393224 | tf_op jit(solution)/shard_map/ppermute | solution.py:35
  72.1 11.5 %collective-permute-start.20 = (bf16[32,2048]{1,0:T(8,128)(2,1)S(1)}, bf16[32,2048]{1,0:T(8,128)(2,1)S(1)}, u32[]{:S(2)}, u32[]{:S(2)}) collective-permute-start(bf16[32,2048]{1,0:T(8,128)(2,1)S(1)} %get-tuple-element.30.high_ref.refs_0_), channel_id=1, source_target_pairs={{0,12},{1,13},{2,14},{3,15},{4,8},{5,9},{6,10},{7,11},{8,4},{9,5},... | collective-permute-start | bytes 393224 | tf_op jit(solution)/shard_map/ppermute | solution.py:35
  73.7 11.4 %collective-permute-start.23 = (bf16[32,2048]{1,0:T(8,128)(2,1)S(1)}, bf16[32,2048]{1,0:T(8,128)(2,1)S(1)}, u32[]{:S(2)}, u32[]{:S(2)}) collective-permute-start(bf16[32,2048]{1,0:T(8,128)(2,1)S(1)} %get-tuple-element.30.high_ref.refs_0_), channel_id=1, source_target_pairs={{0,2},{1,3},{2,0},{3,1},{4,6},{5,7},{6,4},{7,5},{8,10},{9,11},{10,... | collective-permute-start | bytes 393224 | tf_op jit(solution)/shard_map/ppermute | solution.py:35
  83.6 5.2 %collective-permute-start.25 = (bf16[3,32,2048]{2,1,0:T(8,128)(2,1)S(1)}, bf16[3,32,2048]{2,1,0:T(8,128)(2,1)S(1)}, u32[]{:S(2)}, u32[]{:S(2)}) collective-permute-start(bf16[3,32,2048]{2,1,0:T(8,128)(2,1)S(1)} %stacked.6.refs_1_), channel_id=1, source_target_pairs={{0,1},{1,0},{2,3},{3,2},{4,5},{5,4},{6,7},{7,6},{8,9},{9,8},{10,11... | collective-permute-start | bytes 1179656 | tf_op jit(solution)/shard_map/ppermute | solution.py:35
  83.7 12.0 %collective-permute-start.22 = (bf16[3,32,2048]{2,1,0:T(8,128)(2,1)S(1)}, bf16[3,32,2048]{2,1,0:T(8,128)(2,1)S(1)}, u32[]{:S(2)}, u32[]{:S(2)}) collective-permute-start(bf16[3,32,2048]{2,1,0:T(8,128)(2,1)S(1)} %stacked.6.refs_1_), channel_id=1, source_target_pairs={{0,2},{1,3},{2,0},{3,1},{4,6},{5,7},{6,4},{7,5},{8,10},{9,11},{10,... | collective-permute-start | bytes 1179656 | tf_op jit(solution)/shard_map/ppermute | solution.py:35
  85.2 3.1 %collective-permute-start.24 = (bf16[2,32,2048]{2,1,0:T(8,128)(2,1)S(1)}, bf16[2,32,2048]{2,1,0:T(8,128)(2,1)S(1)}, u32[]{:S(2)}, u32[]{:S(2)}) collective-permute-start(bf16[2,32,2048]{2,1,0:T(8,128)(2,1)S(1)} %stacked.7.refs_0_), channel_id=1, source_target_pairs={{0,1},{1,0},{2,3},{3,2},{4,5},{5,4},{6,7},{7,6},{8,9},{9,8},{10,11... | collective-permute-start | bytes 786440 | tf_op jit(solution)/shard_map/ppermute | solution.py:35
  85.6 14.9 %collective-permute-start.28 = (bf16[32,2048]{1,0:T(8,128)(2,1)S(1)}, bf16[32,2048]{1,0:T(8,128)(2,1)S(1)}, u32[]{:S(2)}, u32[]{:S(2)}) collective-permute-start(bf16[32,2048]{1,0:T(8,128)(2,1)S(1)} %get-tuple-element.43), channel_id=1, source_target_pairs={{0,2},{1,3},{2,0},{3,1},{4,6},{5,7},{6,4},{7,5},{8,10},{9,11},{10,... | collective-permute-start | bytes 393224 | tf_op jit(solution)/shard_map/ppermute | solution.py:35
  86.2 14.2 %collective-permute-start.30 = (bf16[32,2048]{1,0:T(8,128)(2,1)S(1)}, bf16[32,2048]{1,0:T(8,128)(2,1)S(1)}, u32[]{:S(2)}, u32[]{:S(2)}) collective-permute-start(bf16[32,2048]{1,0:T(8,128)(2,1)S(1)} %get-tuple-element.40), channel_id=1, source_target_pairs={{0,12},{1,13},{2,14},{3,15},{4,8},{5,9},{6,10},{7,11},{8,4},{9,5},... | collective-permute-start | bytes 393224 | tf_op jit(solution)/shard_map/ppermute | solution.py:35
  88.3 12.7 %collective-permute-start.31 = (bf16[32,2048]{1,0:T(8,128)(2,1)S(1)}, bf16[32,2048]{1,0:T(8,128)(2,1)S(1)}, u32[]{:S(2)}, u32[]{:S(2)}) collective-permute-start(bf16[32,2048]{1,0:T(8,128)(2,1)S(1)} %get-tuple-element.39), channel_id=1, source_target_pairs={{0,8},{1,9},{2,10},{3,11},{4,12},{5,13},{6,14},{7,15},{8,0},{9,1},... | collective-permute-start | bytes 393224 | tf_op jit(solution)/shard_map/ppermute | solution.py:35
  103.2 3.8 %collective-permute-start.33 = (f32[48,128]{1,0:T(8,128)S(1)}, f32[48,128]{1,0:T(8,128)S(1)}, u32[]{:S(2)}, u32[]{:S(2)}) collective-permute-start(f32[48,128]{1,0:T(8,128)S(1)} %add.45), channel_id=1, source_target_pairs={{0,2},{1,3},{2,0},{3,1},{4,6},{5,7},{6,4},{7,5},{8,10},{9,11},{10,... | collective-permute-start | bytes 73736 | tf_op jit(solution)/shard_map/ppermute | solution.py:35
  107.0 4.4 %collective-permute-start.34 = (f32[48,128]{1,0:T(8,128)S(1)}, f32[48,128]{1,0:T(8,128)S(1)}, u32[]{:S(2)}, u32[]{:S(2)}) collective-permute-start(f32[48,128]{1,0:T(8,128)S(1)} %add.46), channel_id=1, source_target_pairs={{0,4},{1,5},{2,6},{3,7},{4,0},{5,1},{6,2},{7,3},{8,12},{9,13},{10,... | collective-permute-start | bytes 73736 | tf_op jit(solution)/shard_map/ppermute | solution.py:35
  107.5 4.7 %collective-permute-start.35 = (f32[48,128]{1,0:T(8,128)S(1)}, f32[48,128]{1,0:T(8,128)S(1)}, u32[]{:S(2)}, u32[]{:S(2)}) collective-permute-start(f32[48,128]{1,0:T(8,128)S(1)} %add.46), channel_id=1, source_target_pairs={{0,8},{1,9},{2,10},{3,11},{4,12},{5,13},{6,14},{7,15},{8,0},{9,1},... | collective-permute-start | bytes 73736 | tf_op jit(solution)/shard_map/ppermute | solution.py:35
  110.2 5.6 %collective-permute-start.36 = (f32[48,128]{1,0:T(8,128)S(1)}, f32[48,128]{1,0:T(8,128)S(1)}, u32[]{:S(2)}, u32[]{:S(2)}) collective-permute-start(f32[48,128]{1,0:T(8,128)S(1)} %add.46), channel_id=1, source_target_pairs={{0,12},{1,13},{2,14},{3,15},{4,8},{5,9},{6,10},{7,11},{8,4},{9,5},... | collective-permute-start | bytes 73736 | tf_op jit(solution)/shard_map/ppermute | solution.py:35
  (8 other events, 22.4 us)
